TPU v7x, 512 devices: a whole 4x8x8 slice. The times are simulated.
512 devices in a mesh: sample: 8 (over z), space: 64 (over x, y, core).
Axes of the slice: x: 4, y: 8, z: 8, core: 2. Of those that a mesh axis runs over, the one named last changes fastest.
Arguments:
- inflow_seeds: int32 [8, 2], P('sample'), may hold values from 0 to 47
- rotor_cells: int32 [64, 3], replicated, may hold values from 0 to 191, as said below
- fluctuation: float32 [3, 192, 48, 128], P(None, 'space'), may hold values from -6 to 6
- profile: float32 [48], replicated, may hold values from 0.5 to 1.5
- correction: float32 [192, 48, 128], P('space'), may hold values from -0.7 to 0.7
- observed: float32 [192, 48, 128], P('space'), may hold values from -6 to 6
Outputs:
- velocity: float32 [8, 3, 192, 48, 128], P('sample', None, 'space')
- gradient: float32 [192, 48, 128], P('space')
Inputs may be any that keep to these rules, and one draw needn't show every extreme that they name: `inflow_seeds`: column 0 is the spanwise offset and column 1 the vertical offset of a sample's inflow. `rotor_cells`: column 0 is a turbine's streamwise cell, column 1 the first of its 8 spanwise cells (at most 120), column 2 the lowest of its 8 vertical cells (1 to 23). Discs may intersect.
All inputs are finite; a program needn't handle non-finite values.
Results may differ from a plain program's by a relative error of at most 0.0001.
Values sent between devices are 32-bit elements; how exact they have to be, the bound alone decides.
No kernel may reach another device: no remote copies, remote signals or barrier semaphores. Data moves between devices by JAX's collectives and lax.ppermute only.
A program may use at most 64 MiB of HBM per device.

v0:
```python
import math

import jax
import jax.numpy as jnp
from jax import lax
from jax.sharding import PartitionSpec as P

NX = 192
NY = 128
NZ = 48
ROTOR = 8


TIME_STEP = 0.2
BASE_VISCOSITY = 0.15
THRUST = 1.0
PRECISE = lax.Precision.HIGHEST


def extended_2(block, sides, width):
    for axis, dim in sides:
        count = lax.axis_size(axis)
        forward = [(i, i + 1) for i in range(count - 1)]
        forward.append((count - 1, 0))
        backward = [(target, source) for source, target in forward]
        low = lax.ppermute(
            lax.slice_in_dim(block, block.shape[dim] - width, None, axis=dim), axis, forward
        )
        high = lax.ppermute(lax.slice_in_dim(block, 0, width, axis=dim), axis, backward)
        block = jnp.concatenate([low, block, high], axis=dim)
    return block


def along_height(field):
    return 0.5 * (jnp.roll(field, -1, axis=-2) - jnp.roll(field, 1, axis=-2))


def along_span(field):
    return 0.5 * (jnp.roll(field, -1, axis=-1) - jnp.roll(field, 1, axis=-1))


def rim_slope(extended):
    return 0.5 * (extended[..., 2:, :, :] - extended[..., :-2, :, :])


def rim_laplace(extended):
    centre = extended[..., 1:-1, :, :]
    summed = extended[..., 2:, :, :] + extended[..., :-2, :, :]
    summed = summed + jnp.roll(centre, -1, axis=-2) + jnp.roll(centre, 1, axis=-2)
    summed = summed + jnp.roll(centre, -1, axis=-1) + jnp.roll(centre, 1, axis=-1)
    return summed - 6.0 * centre


def symbol(wave_x, wave_z, wave_y):
    sine_x = jnp.sin(2.0 * math.pi / NX * wave_x.astype(jnp.float32))
    sine_z = jnp.sin(2.0 * math.pi / NZ * wave_z.astype(jnp.float32))
    sine_y = jnp.sin(2.0 * math.pi / NY * wave_y.astype(jnp.float32))
    summed = sine_x * sine_x + sine_z * sine_z + sine_y * sine_y
    null_mode = (wave_x % (NX // 2) == 0) & (wave_z % (NZ // 2) == 0) & (wave_y % (NY // 2) == 0)
    return jnp.where(null_mode, 0.0, -1.0 / jnp.where(null_mode, 1.0, summed))


def dft_table(length):
    cells = jnp.arange(length, dtype=jnp.int32)
    phase = 2.0 * math.pi / length * (cells[:, None] * cells[None, :] % length).astype(jnp.float32)
    cosine = jnp.cos(phase)
    sine_part = jnp.sin(phase)
    return jnp.stack([jnp.stack([cosine, -sine_part]), jnp.stack([sine_part, cosine])])


def vertical_tables():
    cells = jnp.arange(NZ, dtype=jnp.int32)
    wave_z = jnp.arange(NZ // 2 + 1, dtype=jnp.int32)
    phase = 2.0 * math.pi / NZ * (cells[:, None] * wave_z[None, :] % NZ).astype(jnp.float32)
    cosine = jnp.cos(phase)
    sine_part = jnp.sin(phase)
    forward = jnp.stack([cosine, -sine_part])
    weight = jnp.where((wave_z == 0) | (wave_z == NZ // 2), 1.0, 2.0) / (NX * NY * NZ)
    inverse = jnp.stack([cosine.T * weight[:, None], -sine_part.T * weight[:, None]])
    return (forward, inverse)


def rotor_field(rotor_cells, stream_cells):
    rotor_stream = rotor_cells[:, 0:1]
    rotor_span = rotor_cells[:, 1:2]
    rotor_base = rotor_cells[:, 2:3]
    heights = jnp.arange(NZ, dtype=jnp.int32)[None, :]
    spans = jnp.arange(NY, dtype=jnp.int32)[None, :]
    in_stream = (stream_cells[None, :] == rotor_stream).astype(jnp.float32)
    in_height = ((heights >= rotor_base) & (heights < rotor_base + ROTOR)).astype(jnp.float32)
    in_span = ((spans >= rotor_span) & (spans < rotor_span + ROTOR)).astype(jnp.float32)
    sheet = (in_stream[:, :, None] * in_height[:, None, :]).reshape(in_stream.shape[0], -1)
    counted = jnp.dot(sheet.T, in_span, precision=PRECISE)
    return counted.reshape(stream_cells.shape[0], NZ, NY)


def pressure_solve(source, tables):
    forward_z, inverse_z, table_y, table_x = tables
    spectrum = jnp.einsum("sxzy,azk->saxky", source, forward_z, precision=PRECISE)
    spectrum = jnp.einsum("saxky,abyq->sbxkq", spectrum, table_y, precision=PRECISE)
    part_count = lax.axis_size("space")
    position = lax.axis_index("space")
    wave_x = jnp.arange(NX, dtype=jnp.int32)[:, None, None]
    span_width = spectrum.shape[4] // part_count
    columns = lax.all_to_all(spectrum, "space", split_axis=4, concat_axis=2, tiled=True)
    columns = jnp.einsum("saxkq,abxw->sbwkq", columns, table_x, precision=PRECISE)
    wave_z = jnp.arange(NZ // 2 + 1, dtype=jnp.int32)[None, :, None]
    wave_y = (position * span_width + jnp.arange(span_width, dtype=jnp.int32))[None, None, :]
    columns = columns * symbol(wave_x, wave_z, wave_y)
    columns = jnp.einsum("sbwkq,cbxw->scxkq", columns, table_x, precision=PRECISE)
    spectrum = lax.all_to_all(columns, "space", split_axis=2, concat_axis=4, tiled=True)
    spectrum = jnp.einsum("sbxkq,cbyq->scxky", spectrum, table_y, precision=PRECISE)
    return jnp.einsum("saxky,akz->sxzy", spectrum, inverse_z, precision=PRECISE)


def project(trial, tables):
    extended = extended_2(trial[:, 0], (("space", 1),), 1)
    source = rim_slope(extended) + along_span(trial[:, 1]) + along_height(trial[:, 2])
    pressure = pressure_solve(source, tables)
    beside_all = extended_2(pressure, (("space", 1),), 1)
    push = jnp.stack([rim_slope(beside_all), along_span(pressure), along_height(pressure)], axis=1)
    return trial - push


def flow_terms(state, viscosity, rotor_count, column):
    extended = extended_2(state, (("space", 2),), 1)
    curvature = rim_laplace(extended)
    forcing = -column * rim_slope(extended) + viscosity * curvature - THRUST * rotor_count * state
    return (forcing, curvature)


def adjoint_terms(cotangent, viscosity, rotor_count, column):
    stacked = jnp.concatenate([cotangent, viscosity * cotangent], axis=1)
    extended = extended_2(stacked, (("space", 2),), 1)
    return (
        column * rim_slope(extended[:, :3])
        + rim_laplace(extended[:, 3:])
        - THRUST * rotor_count * cotangent
    )


def first_share(adjoint_two, laplace_start, viscosity, rotor_count, column, tables):
    pulled = adjoint_terms(adjoint_two, viscosity, rotor_count, column)
    adjoint_one = project(0.5 * adjoint_two + 0.5 * TIME_STEP * pulled, tables)
    return TIME_STEP * viscosity * jnp.sum(adjoint_one * laplace_start, axis=(0, 1))


def shards(inflow_seeds, rotor_cells, fluctuation, profile, correction, observed):
    slab = correction.shape[0]
    position = lax.axis_index("space")
    viscosity = BASE_VISCOSITY * jnp.exp(correction)
    rotor_count = rotor_field(rotor_cells, position * slab + jnp.arange(slab, dtype=jnp.int32))
    column = profile[:, None]
    forward_z, inverse_z = vertical_tables()
    tables = (forward_z, inverse_z, dft_table(NY), dft_table(NX))
    shifted = jnp.roll(fluctuation, inflow_seeds[0, 0], axis=3)
    shifted = jnp.roll(shifted, inflow_seeds[0, 1], axis=2)
    starts = [jnp.concatenate([shifted[:1] + column, shifted[1:]], axis=0)]
    initial = jnp.stack(starts)
    forcing, laplace_start = flow_terms(initial, viscosity, rotor_count, column)
    middle = project(initial + TIME_STEP * forcing, tables)
    forcing, laplace_mid = flow_terms(middle, viscosity, rotor_count, column)
    velocity = project(0.5 * initial + 0.5 * (middle + TIME_STEP * forcing), tables)
    misfit = velocity[:, 0] - observed
    blank = jnp.zeros_like(misfit)
    adjoint_two = project(jnp.stack([misfit, blank, blank], axis=1), tables)
    share_two = TIME_STEP * viscosity * (0.5 * jnp.sum(adjoint_two * laplace_mid, axis=(0, 1)))
    share_one = first_share(adjoint_two, laplace_start, viscosity, rotor_count, column, tables)
    gradient = lax.psum(share_two + share_one, "sample")
    return (velocity, gradient)


def solution(mesh):
    return jax.shard_map(
        shards,
        mesh=mesh,
        in_specs=(
            P("sample", None),
            P(),
            P(None, "space", None, None),
            P(),
            P("space", None, None),
            P("space", None, None),
        ),
        out_specs=(P("sample", None, "space", None, None), P("space", None, None)),
        check_vma=False,
    )
```

profile of v0, /device:TPU:2, one launch (start us, length us, event | category | flops | bytes accessed | tf_op | source)
XLA Modules:
  0.0 390.7 jit_solution(11517804080122447719)
XLA Ops:
  15.7 5.8 %collective-permute-start = (f32[1,3,1,48,128]{4,3,2,1,0:T(8,128)S(1)}, f32[1,3,1,48,128]{4,3,2,1,0:T(8,128)}, u32[]{:S(2)}, u32[]{:S(2)}) collective-permute-start(f32[1,3,1,48,128]{4,3,2,1,0:T(8,128)S(1)} %get-tuple-element.48), channel_id=1, source_target_pairs={{1,0},{2,1},{3,2},{4,3},{5,4},{6,5},{7,6},{8,7},{9,8},{10,9},{11,1... | collective-permute-start | bytes 221192 | tf_op jit(solution)/shard_map/ppermute | solution.py:29
  27.2 3.7 collective-permute-start.2
  32.8 5.3 %collective-permute-done.3 = f32[1,1,48,128]{3,2,1,0:T(8,128)S(1)} collective-permute-done((f32[1,1,48,128]{3,2,1,0:T(8,128)S(1)}, f32[1,1,48,128]{3,2,1,0:T(8,128)S(1)}, u32[]{:S(2)}, u32[]{:S(2)}) %collective-permute-start.3) | collective-permute-done | bytes 24608 | tf_op jit(solution)/shard_map/ppermute | solution.py:26
  40.1 13.7 %all-to-all-start = ((f32[64,1,300]{2,1,0:T(1,128)}), f32[64,1,300]{2,1,0:T(1,128)S(1)}, u32[]{:S(2)}, u32[]{:S(2)}) async-start(f32[64,1,300]{2,1,0:T(1,128)} %reshape.1742), calls=%async_computation | async-start | bytes 196608 | tf_op jit(solution)/shard_map/all_to_all | solution.py:105
  53.9 9.2 %all-to-all-done = f32[64,1,300]{2,1,0:T(1,128)S(1)} async-done(((f32[64,1,300]{2,1,0:T(1,128)}), f32[64,1,300]{2,1,0:T(1,128)S(1)}, u32[]{:S(2)}, u32[]{:S(2)}) %all-to-all-start) | async-done | bytes 76832 | tf_op jit(solution)/shard_map/all_to_all | solution.py:105
  68.2 5.5 %all-to-all-start.1 = ((f32[64,1,300]{2,1,0:T(1,128)}), f32[64,1,300]{2,1,0:T(1,128)S(1)}, u32[]{:S(2)}, u32[]{:S(2)}) async-start(f32[64,1,300]{2,1,0:T(1,128)} %reshape.1744), calls=%async_computation.1 | async-start | bytes 196608 | tf_op jit(solution)/shard_map/all_to_all | solution.py:111
  73.9 9.1 %all-to-all-done.1 = f32[64,1,300]{2,1,0:T(1,128)S(1)} async-done(((f32[64,1,300]{2,1,0:T(1,128)}), f32[64,1,300]{2,1,0:T(1,128)S(1)}, u32[]{:S(2)}, u32[]{:S(2)}) %all-to-all-start.1) | async-done | bytes 76832 | tf_op jit(solution)/shard_map/all_to_all | solution.py:111
  91.2 4.9 %collective-permute-done.5 = f32[1,1,48,128]{3,2,1,0:T(8,128)S(1)} collective-permute-done((f32[1,1,48,128]{3,2,1,0:T(8,128)S(1)}, f32[1,1,48,128]{3,2,1,0:T(8,128)S(1)}, u32[]{:S(2)}, u32[]{:S(2)}) %collective-permute-start.5) | collective-permute-done | bytes 24608 | tf_op jit(solution)/shard_map/ppermute | solution.py:26
  98.4 5.8 %collective-permute-start.6 = (f32[1,3,1,48,128]{4,3,2,1,0:T(8,128)S(1)}, f32[1,3,1,48,128]{4,3,2,1,0:T(8,128)S(1)}, u32[]{:S(2)}, u32[]{:S(2)}) collective-permute-start(f32[1,3,1,48,128]{4,3,2,1,0:T(8,128)S(1)} %get-tuple-element.35), channel_id=1, source_target_pairs={{1,0},{2,1},{3,2},{4,3},{5,4},{6,5},{7,6},{8,7},{9,8},{10,9},{11,1... | collective-permute-start | bytes 221192 | tf_op jit(solution)/shard_map/ppermute | solution.py:29
  106.6 5.8 %collective-permute-start.8 = (f32[1,1,48,128]{3,2,1,0:T(8,128)S(1)}, f32[1,1,48,128]{3,2,1,0:T(8,128)S(1)}, u32[]{:S(2)}, u32[]{:S(2)}) collective-permute-start(f32[1,1,48,128]{3,2,1,0:T(8,128)S(1)} %get-tuple-element.103), channel_id=1, source_target_pairs={{1,0},{2,1},{3,2},{4,3},{5,4},{6,5},{7,6},{8,7},{9,8},{10,9},{11,1... | collective-permute-start | bytes 73736 | tf_op jit(solution)/shard_map/ppermute | solution.py:29
  114.4 5.3 %collective-permute-done.9 = f32[1,1,48,128]{3,2,1,0:T(8,128)S(1)} collective-permute-done((f32[1,1,48,128]{3,2,1,0:T(8,128)S(1)}, f32[1,1,48,128]{3,2,1,0:T(8,128)S(1)}, u32[]{:S(2)}, u32[]{:S(2)}) %collective-permute-start.9) | collective-permute-done | bytes 24608 | tf_op jit(solution)/shard_map/ppermute | solution.py:26
  121.1 18.5 %all_to_all.120 = f32[64,1,300]{2,1,0:T(1,128)S(1)} all-to-all(f32[64,1,300]{2,1,0:T(1,128)S(1)} %reshape.1746), channel_id=1, replica_groups=mesh['sample'=8,'space'=64] {'space'}, dimensions={0} | all-to-all | bytes 153600 | tf_op jit(solution)/shard_map/all_to_all | solution.py:105
  143.6 14.3 %all_to_all.121 = f32[64,1,300]{2,1,0:T(1,128)S(1)} all-to-all(f32[64,1,300]{2,1,0:T(1,128)S(1)} %reshape.1748), channel_id=1, replica_groups=mesh['sample'=8,'space'=64] {'space'}, dimensions={0} | all-to-all | bytes 153600 | tf_op jit(solution)/shard_map/all_to_all | solution.py:111
  165.9 5.2 %collective-permute-done.11 = f32[1,1,48,128]{3,2,1,0:T(8,128)S(1)} collective-permute-done((f32[1,1,48,128]{3,2,1,0:T(8,128)S(1)}, f32[1,1,48,128]{3,2,1,0:T(8,128)S(1)}, u32[]{:S(2)}, u32[]{:S(2)}) %collective-permute-start.11) | collective-permute-done | bytes 24608 | tf_op jit(solution)/shard_map/ppermute | solution.py:26
  176.4 4.8 %collective-permute-done.13 = f32[1,1,48,128]{3,2,1,0:T(8,128)S(1)} collective-permute-done((f32[1,1,48,128]{3,2,1,0:T(8,128)S(1)}, f32[1,1,48,128]{3,2,1,0:T(8,128)S(1)}, u32[]{:S(2)}, u32[]{:S(2)}) %collective-permute-start.13) | collective-permute-done | bytes 24608 | tf_op jit(solution)/shard_map/ppermute | solution.py:26
  182.6 25.9 %all_to_all.122 = f32[64,1,300]{2,1,0:T(1,128)S(1)} all-to-all(f32[64,1,300]{2,1,0:T(1,128)S(1)} %reshape.1750), channel_id=1, replica_groups=mesh['sample'=8,'space'=64] {'space'}, dimensions={0} | all-to-all | bytes 153600 | tf_op jit(solution)/shard_map/all_to_all | solution.py:105
  212.4 14.4 %all_to_all.123 = f32[64,1,300]{2,1,0:T(1,128)S(1)} all-to-all(f32[64,1,300]{2,1,0:T(1,128)S(1)} %reshape.1752), channel_id=1, replica_groups=mesh['sample'=8,'space'=64] {'space'}, dimensions={0} | all-to-all | bytes 153600 | tf_op jit(solution)/shard_map/all_to_all | solution.py:111
  234.8 5.2 %collective-permute-done.15 = f32[1,1,48,128]{3,2,1,0:T(8,128)S(1)} collective-permute-done((f32[1,1,48,128]{3,2,1,0:T(8,128)S(1)}, f32[1,1,48,128]{3,2,1,0:T(8,128)S(1)}, u32[]{:S(2)}, u32[]{:S(2)}) %collective-permute-start.15) | collective-permute-done | bytes 24608 | tf_op jit(solution)/shard_map/ppermute | solution.py:26
  245.0 5.9 %collective-permute-done.17 = f32[1,6,1,48,128]{4,3,2,1,0:T(8,128)S(1)} collective-permute-done((f32[1,6,1,48,128]{4,3,2,1,0:T(8,128)S(1)}, f32[1,6,1,48,128]{4,3,2,1,0:T(8,128)S(1)}, u32[]{:S(2)}, u32[]{:S(2)}) %collective-permute-start.17) | collective-permute-done | bytes 147488 | tf_op jit(solution)/shard_map/ppermute | solution.py:26
  255.8 4.8 %collective-permute-done.19 = f32[1,1,48,128]{3,2,1,0:T(8,128)S(1)} collective-permute-done((f32[1,1,48,128]{3,2,1,0:T(8,128)S(1)}, f32[1,1,48,128]{3,2,1,0:T(8,128)S(1)}, u32[]{:S(2)}, u32[]{:S(2)}) %collective-permute-start.19) | collective-permute-done | bytes 24608 | tf_op jit(solution)/shard_map/ppermute | solution.py:26
  262.0 17.3 %all_to_all.124 = f32[64,1,300]{2,1,0:T(1,128)S(1)} all-to-all(f32[64,1,300]{2,1,0:T(1,128)S(1)} %reshape.1754), channel_id=1, replica_groups=mesh['sample'=8,'space'=64] {'space'}, dimensions={0} | all-to-all | bytes 153600 | tf_op jit(solution)/shard_map/all_to_all | solution.py:105
  283.3 14.3 %all_to_all.125 = f32[64,1,300]{2,1,0:T(1,128)S(1)} all-to-all(f32[64,1,300]{2,1,0:T(1,128)S(1)} %reshape.1756), channel_id=1, replica_groups=mesh['sample'=8,'space'=64] {'space'}, dimensions={0} | all-to-all | bytes 153600 | tf_op jit(solution)/shard_map/all_to_all | solution.py:111
  305.6 5.2 %collective-permute-done.21 = f32[1,1,48,128]{3,2,1,0:T(8,128)S(1)} collective-permute-done((f32[1,1,48,128]{3,2,1,0:T(8,128)S(1)}, f32[1,1,48,128]{3,2,1,0:T(8,128)S(1)}, u32[]{:S(2)}, u32[]{:S(2)}) %collective-permute-start.21) | collective-permute-done | bytes 24608 | tf_op jit(solution)/shard_map/ppermute | solution.py:26
  312.4 69.7 %all-reduce.5.cloned.1.call-done = f32[3,48,128]{2,1,0:T(8,128)} async-done(((f32[3,48,128]{2,1,0:T(8,128)}), f32[3,48,128]{2,1,0:T(8,128)}) %all-reduce.5.cloned.1.call-update) | async-done | bytes 73744 | tf_op jit(solution)/shard_map/psum | solution.py:169
  (235 shorter events, 93.2 us)
Async XLA Ops:
  13.8 11.9 %collective-permute-start.1 = (f32[1,3,1,48,128]{4,3,2,1,0:T(8,128)S(1)}, f32[1,3,1,48,128]{4,3,2,1,0:T(8,128)}, u32[]{:S(2)}, u32[]{:S(2)}) collective-permute-start(f32[1,3,1,48,128]{4,3,2,1,0:T(8,128)S(1)} %get-tuple-element.47), channel_id=1, source_target_pairs={{0,1},{1,2},{2,3},{3,4},{4,5},{5,6},{6,7},{7,8},{8,9},{9,10},{10,1... | collective-permute-start | bytes 221192 | tf_op jit(solution)/shard_map/ppermute | solution.py:26
  15.7 10.0 %collective-permute-start = (f32[1,3,1,48,128]{4,3,2,1,0:T(8,128)S(1)}, f32[1,3,1,48,128]{4,3,2,1,0:T(8,128)}, u32[]{:S(2)}, u32[]{:S(2)}) collective-permute-start(f32[1,3,1,48,128]{4,3,2,1,0:T(8,128)S(1)} %get-tuple-element.48), channel_id=1, source_target_pairs={{1,0},{2,1},{3,2},{4,3},{5,4},{6,5},{7,6},{8,7},{9,8},{10,9},{11,1... | collective-permute-start | bytes 221192 | tf_op jit(solution)/shard_map/ppermute | solution.py:29
  27.2 5.6 %collective-permute-start.2 = (f32[1,1,48,128]{3,2,1,0:T(8,128)S(1)}, f32[1,1,48,128]{3,2,1,0:T(8,128)S(1)}, u32[]{:S(2)}, u32[]{:S(2)}) collective-permute-start(f32[1,1,48,128]{3,2,1,0:T(8,128)S(1)} %get-tuple-element.123), channel_id=1, source_target_pairs={{1,0},{2,1},{3,2},{4,3},{5,4},{6,5},{7,6},{8,7},{9,8},{10,9},{11,1... | collective-permute-start | bytes 73736 | tf_op jit(solution)/shard_map/ppermute | solution.py:29
  30.8 7.3 %collective-permute-start.3 = (f32[1,1,48,128]{3,2,1,0:T(8,128)S(1)}, f32[1,1,48,128]{3,2,1,0:T(8,128)S(1)}, u32[]{:S(2)}, u32[]{:S(2)}) collective-permute-start(f32[1,1,48,128]{3,2,1,0:T(8,128)S(1)} %get-tuple-element.124), channel_id=1, source_target_pairs={{0,1},{1,2},{2,3},{3,4},{4,5},{5,6},{6,7},{7,8},{8,9},{9,10},{10,1... | collective-permute-start | bytes 73736 | tf_op jit(solution)/shard_map/ppermute | solution.py:26
  40.1 22.9 %all-to-all-start = ((f32[64,1,300]{2,1,0:T(1,128)}), f32[64,1,300]{2,1,0:T(1,128)S(1)}, u32[]{:S(2)}, u32[]{:S(2)}) async-start(f32[64,1,300]{2,1,0:T(1,128)} %reshape.1742), calls=%async_computation | async-start | bytes 196608 | tf_op jit(solution)/shard_map/all_to_all | solution.py:105
  68.2 14.8 %all-to-all-start.1 = ((f32[64,1,300]{2,1,0:T(1,128)}), f32[64,1,300]{2,1,0:T(1,128)S(1)}, u32[]{:S(2)}, u32[]{:S(2)}) async-start(f32[64,1,300]{2,1,0:T(1,128)} %reshape.1744), calls=%async_computation.1 | async-start | bytes 196608 | tf_op jit(solution)/shard_map/all_to_all | solution.py:111
  73.7 308.4 %all-reduce.5.cloned.1.call-start = ((), (), s32[]{:S(2)}) async-start(), calls=%async_computation.8 | async-start | bytes 147456 | tf_op jit(solution)/shard_map/psum | solution.py:169
  85.8 5.4 %collective-permute-start.4 = (f32[1,1,48,128]{3,2,1,0:T(8,128)S(1)}, f32[1,1,48,128]{3,2,1,0:T(8,128)S(1)}, u32[]{:S(2)}, u32[]{:S(2)}) collective-permute-start(f32[1,1,48,128]{3,2,1,0:T(8,128)S(1)} %get-tuple-element.105), channel_id=1, source_target_pairs={{1,0},{2,1},{3,2},{4,3},{5,4},{6,5},{7,6},{8,7},{9,8},{10,9},{11,1... | collective-permute-start | bytes 73736 | tf_op jit(solution)/shard_map/ppermute | solution.py:29
  88.9 7.3 %collective-permute-start.5 = (f32[1,1,48,128]{3,2,1,0:T(8,128)S(1)}, f32[1,1,48,128]{3,2,1,0:T(8,128)S(1)}, u32[]{:S(2)}, u32[]{:S(2)}) collective-permute-start(f32[1,1,48,128]{3,2,1,0:T(8,128)S(1)} %get-tuple-element.106), channel_id=1, source_target_pairs={{0,1},{1,2},{2,3},{3,4},{4,5},{5,6},{6,7},{7,8},{8,9},{9,10},{10,1... | collective-permute-start | bytes 73736 | tf_op jit(solution)/shard_map/ppermute | solution.py:26
  96.5 7.8 %collective-permute-start.7 = (f32[1,3,1,48,128]{4,3,2,1,0:T(8,128)S(1)}, f32[1,3,1,48,128]{4,3,2,1,0:T(8,128)S(1)}, u32[]{:S(2)}, u32[]{:S(2)}) collective-permute-start(f32[1,3,1,48,128]{4,3,2,1,0:T(8,128)S(1)} %get-tuple-element.34), channel_id=1, source_target_pairs={{0,1},{1,2},{2,3},{3,4},{4,5},{5,6},{6,7},{7,8},{8,9},{9,10},{10,1... | collective-permute-start | bytes 221192 | tf_op jit(solution)/shard_map/ppermute | solution.py:26
  98.4 7.7 %collective-permute-start.6 = (f32[1,3,1,48,128]{4,3,2,1,0:T(8,128)S(1)}, f32[1,3,1,48,128]{4,3,2,1,0:T(8,128)S(1)}, u32[]{:S(2)}, u32[]{:S(2)}) collective-permute-start(f32[1,3,1,48,128]{4,3,2,1,0:T(8,128)S(1)} %get-tuple-element.35), channel_id=1, source_target_pairs={{1,0},{2,1},{3,2},{4,3},{5,4},{6,5},{7,6},{8,7},{9,8},{10,9},{11,1... | collective-permute-start | bytes 221192 | tf_op jit(solution)/shard_map/ppermute | solution.py:29
  106.6 7.8 %collective-permute-start.8 = (f32[1,1,48,128]{3,2,1,0:T(8,128)S(1)}, f32[1,1,48,128]{3,2,1,0:T(8,128)S(1)}, u32[]{:S(2)}, u32[]{:S(2)}) collective-permute-start(f32[1,1,48,128]{3,2,1,0:T(8,128)S(1)} %get-tuple-element.103), channel_id=1, source_target_pairs={{1,0},{2,1},{3,2},{4,3},{5,4},{6,5},{7,6},{8,7},{9,8},{10,9},{11,1... | collective-permute-start | bytes 73736 | tf_op jit(solution)/shard_map/ppermute | solution.py:29
  112.5 7.3 %collective-permute-start.9 = (f32[1,1,48,128]{3,2,1,0:T(8,128)S(1)}, f32[1,1,48,128]{3,2,1,0:T(8,128)S(1)}, u32[]{:S(2)}, u32[]{:S(2)}) collective-permute-start(f32[1,1,48,128]{3,2,1,0:T(8,128)S(1)} %get-tuple-element.104), channel_id=1, source_target_pairs={{0,1},{1,2},{2,3},{3,4},{4,5},{5,6},{6,7},{7,8},{8,9},{9,10},{10,1... | collective-permute-start | bytes 73736 | tf_op jit(solution)/shard_map/ppermute | solution.py:26
  160.7 5.2 %collective-permute-start.10 = (f32[1,1,48,128]{3,2,1,0:T(8,128)S(1)}, f32[1,1,48,128]{3,2,1,0:T(8,128)S(1)}, u32[]{:S(2)}, u32[]{:S(2)}) collective-permute-start(f32[1,1,48,128]{3,2,1,0:T(8,128)S(1)} %get-tuple-element.85), channel_id=1, source_target_pairs={{1,0},{2,1},{3,2},{4,3},{5,4},{6,5},{7,6},{8,7},{9,8},{10,9},{11,1... | collective-permute-start | bytes 73736 | tf_op jit(solution)/shard_map/ppermute | solution.py:29
  163.8 7.3 %collective-permute-start.11 = (f32[1,1,48,128]{3,2,1,0:T(8,128)S(1)}, f32[1,1,48,128]{3,2,1,0:T(8,128)S(1)}, u32[]{:S(2)}, u32[]{:S(2)}) collective-permute-start(f32[1,1,48,128]{3,2,1,0:T(8,128)S(1)} %get-tuple-element.86), channel_id=1, source_target_pairs={{0,1},{1,2},{2,3},{3,4},{4,5},{5,6},{6,7},{7,8},{8,9},{9,10},{10,1... | collective-permute-start | bytes 73736 | tf_op jit(solution)/shard_map/ppermute | solution.py:26
  172.0 4.4 %collective-permute-start.12 = (f32[1,1,48,128]{3,2,1,0:T(8,128)S(1)}, f32[1,1,48,128]{3,2,1,0:T(8,128)S(1)}, u32[]{:S(2)}, u32[]{:S(2)}) collective-permute-start(f32[1,1,48,128]{3,2,1,0:T(8,128)S(1)} %get-tuple-element.83), channel_id=1, source_target_pairs={{1,0},{2,1},{3,2},{4,3},{5,4},{6,5},{7,6},{8,7},{9,8},{10,9},{11,1... | collective-permute-start | bytes 73736 | tf_op jit(solution)/shard_map/ppermute | solution.py:29
  173.9 7.3 %collective-permute-start.13 = (f32[1,1,48,128]{3,2,1,0:T(8,128)S(1)}, f32[1,1,48,128]{3,2,1,0:T(8,128)S(1)}, u32[]{:S(2)}, u32[]{:S(2)}) collective-permute-start(f32[1,1,48,128]{3,2,1,0:T(8,128)S(1)} %get-tuple-element.84), channel_id=1, source_target_pairs={{0,1},{1,2},{2,3},{3,4},{4,5},{5,6},{6,7},{7,8},{8,9},{9,10},{10,1... | collective-permute-start | bytes 73736 | tf_op jit(solution)/shard_map/ppermute | solution.py:26
  229.7 5.2 %collective-permute-start.14 = (f32[1,1,48,128]{3,2,1,0:T(8,128)S(1)}, f32[1,1,48,128]{3,2,1,0:T(8,128)S(1)}, u32[]{:S(2)}, u32[]{:S(2)}) collective-permute-start(f32[1,1,48,128]{3,2,1,0:T(8,128)S(1)} %get-tuple-element.73), channel_id=1, source_target_pairs={{1,0},{2,1},{3,2},{4,3},{5,4},{6,5},{7,6},{8,7},{9,8},{10,9},{11,1... | collective-permute-start | bytes 73736 | tf_op jit(solution)/shard_map/ppermute | solution.py:29
  232.8 7.3 %collective-permute-start.15 = (f32[1,1,48,128]{3,2,1,0:T(8,128)S(1)}, f32[1,1,48,128]{3,2,1,0:T(8,128)S(1)}, u32[]{:S(2)}, u32[]{:S(2)}) collective-permute-start(f32[1,1,48,128]{3,2,1,0:T(8,128)S(1)} %get-tuple-element.74), channel_id=1, source_target_pairs={{0,1},{1,2},{2,3},{3,4},{4,5},{5,6},{6,7},{7,8},{8,9},{9,10},{10,1... | collective-permute-start | bytes 73736 | tf_op jit(solution)/shard_map/ppermute | solution.py:26
  240.4 4.6 %collective-permute-start.16 = (f32[1,6,1,48,128]{4,3,2,1,0:T(8,128)S(1)}, f32[1,6,1,48,128]{4,3,2,1,0:T(8,128)S(1)}, u32[]{:S(2)}, u32[]{:S(2)}) collective-permute-start(f32[1,6,1,48,128]{4,3,2,1,0:T(8,128)S(1)} %get-tuple-element.8), channel_id=1, source_target_pairs={{1,0},{2,1},{3,2},{4,3},{5,4},{6,5},{7,6},{8,7},{9,8},{10,9},{11,1... | collective-permute-start | bytes 442376 | tf_op jit(solution)/shard_map/ppermute | solution.py:29
  242.4 8.6 %collective-permute-start.17 = (f32[1,6,1,48,128]{4,3,2,1,0:T(8,128)S(1)}, f32[1,6,1,48,128]{4,3,2,1,0:T(8,128)S(1)}, u32[]{:S(2)}, u32[]{:S(2)}) collective-permute-start(f32[1,6,1,48,128]{4,3,2,1,0:T(8,128)S(1)} %get-tuple-element.9), channel_id=1, source_target_pairs={{0,1},{1,2},{2,3},{3,4},{4,5},{5,6},{6,7},{7,8},{8,9},{9,10},{10,1... | collective-permute-start | bytes 442376 | tf_op jit(solution)/shard_map/ppermute | solution.py:26
  253.4 7.3 %collective-permute-start.19 = (f32[1,1,48,128]{3,2,1,0:T(8,128)S(1)}, f32[1,1,48,128]{3,2,1,0:T(8,128)S(1)}, u32[]{:S(2)}, u32[]{:S(2)}) collective-permute-start(f32[1,1,48,128]{3,2,1,0:T(8,128)S(1)} %get-tuple-element.72), channel_id=1, source_target_pairs={{0,1},{1,2},{2,3},{3,4},{4,5},{5,6},{6,7},{7,8},{8,9},{9,10},{10,1... | collective-permute-start | bytes 73736 | tf_op jit(solution)/shard_map/ppermute | solution.py:26
  300.4 5.2 %collective-permute-start.20 = (f32[1,1,48,128]{3,2,1,0:T(8,128)S(1)}, f32[1,1,48,128]{3,2,1,0:T(8,128)S(1)}, u32[]{:S(2)}, u32[]{:S(2)}) collective-permute-start(f32[1,1,48,128]{3,2,1,0:T(8,128)S(1)} %get-tuple-element.53), channel_id=1, source_target_pairs={{1,0},{2,1},{3,2},{4,3},{5,4},{6,5},{7,6},{8,7},{9,8},{10,9},{11,1... | collective-permute-start | bytes 73736 | tf_op jit(solution)/shard_map/ppermute | solution.py:29
  303.5 7.3 %collective-permute-start.21 = (f32[1,1,48,128]{3,2,1,0:T(8,128)S(1)}, f32[1,1,48,128]{3,2,1,0:T(8,128)S(1)}, u32[]{:S(2)}, u32[]{:S(2)}) collective-permute-start(f32[1,1,48,128]{3,2,1,0:T(8,128)S(1)} %get-tuple-element.54), channel_id=1, source_target_pairs={{0,1},{1,2},{2,3},{3,4},{4,5},{5,6},{6,7},{7,8},{8,9},{9,10},{10,1... | collective-permute-start | bytes 73736 | tf_op jit(solution)/shard_map/ppermute | solution.py:26
  (9 other events, 28.3 us)
Sparse Core Ops, SparseCore 0:
  312.5 69.5 all-reduce.4
where the time goes:
time: 396 us; the launch traced here: 391 us
  waiting for transfers between devices  137 us (35%)
  blocking collectives  105 us (27%)
  starting transfers between devices  81.2 us (21%)
  local copies, waits for them, and re-layouts  21.1 us (5%)
  between operations  18.1 us (5%)
  other arithmetic  14.6 us (4%)
  matrix products  14.3 us (4%)
    psum x1, waiting for transfers between devices, shards(): gradient = lax.psum(share_two + share_one, 'sample')  69.7 us
    all_to_all x3, blocking collectives, pressure_solve(): lax.all_to_all(spectrum, 'space', split_axis=4, concat_axis=2, tiled=True)  61.6 us
    ppermute x11, waiting for transfers between devices, extended_2(): lax.ppermute(lax.slice_in_dim(block, block.shape[dim] - width, None, axis...  46.6 us
    all_to_all x3, blocking collectives, pressure_solve(): lax.all_to_all(columns, 'space', split_axis=2, concat_axis=4, tiled=True)  43.1 us
    ppermute x11, starting transfers between devices, extended_2(): lax.ppermute(lax.slice_in_dim(block, 0, width, axis=dim), axis, backward)  39.1 us
    ppermute x11, starting transfers between devices, extended_2(): lax.ppermute(lax.slice_in_dim(block, block.shape[dim] - width, None, axis...  22.8 us
    all_to_all x1, starting transfers between devices, pressure_solve(): lax.all_to_all(spectrum, 'space', split_axis=4, concat_axis=2, tiled=True)  13.7 us
    unnamed x33, local copies, waits for them, and re-layouts  13 us
  transfers between devices with their start and end apart: 25, of which 15 were waited for; matrix products, arithmetic and copies ran while one was open for 1% of the time, Pallas kernels for 0%

commit v1 on v0

v1 whole, which is shorter than its diff:
```python
import functools
import math

import jax
import jax.numpy as jnp
import ml_dtypes
import numpy as np
from jax import lax
from jax.experimental import pallas as pl
from jax.experimental.pallas import tpu as pltpu
from jax.sharding import PartitionSpec as P

NX = 192
NY = 128
NZ = 48
ROTOR = 8
SPACE = 64
SLAB = NX // SPACE

TIME_STEP = 0.2
BASE_VISCOSITY = 0.15
THRUST = 1.0
F32 = jnp.float32
BF16 = jnp.bfloat16


def real_basis(length):
    half = length // 2
    cells = np.arange(length)[:, None]
    waves = np.arange(half)[None, :]
    phase = 2.0 * np.pi / length * ((cells * waves) % length)
    even = np.cos(phase) * math.sqrt(2.0 / length)
    even[:, 0] = math.sqrt(1.0 / length)
    odd = np.sin(phase) * math.sqrt(2.0 / length)
    odd[:, 0] = (1.0 - 2.0 * (np.arange(length) % 2)) * math.sqrt(1.0 / length)
    return np.concatenate([even, odd], axis=1)


def sine_of(length):
    half = length // 2
    waves = np.arange(length) % half
    return np.sin(2.0 * np.pi / length * waves)


def two_part(matrix):
    matrix = np.asarray(matrix, np.float32)
    high = matrix.astype(ml_dtypes.bfloat16)
    low = (matrix - high.astype(np.float32)).astype(ml_dtypes.bfloat16)
    return np.stack([high, low])


BASIS_X = real_basis(NX)
BASIS_Y = real_basis(NY)
BASIS_Z = real_basis(NZ)


def stream_rows(first, count):
    device = np.arange(SPACE)[None, :]
    slot = np.arange(first, first + count)[:, None]
    return ((SLAB * device + slot) % NX).reshape(-1)


TO_Y = two_part(BASIS_Y)
FROM_Y = two_part(BASIS_Y.T)
TO_Z = two_part(BASIS_Z.T)
FROM_Z = two_part(BASIS_Z)
TO_X3 = two_part(BASIS_X[stream_rows(0, 3)].T)
TO_X5 = two_part(BASIS_X[stream_rows(-1, 5)].T)
FROM_X7 = two_part(BASIS_X[stream_rows(-2, 7)])
FROM_X5 = two_part(BASIS_X[stream_rows(-1, 5)])
SINE_X = np.broadcast_to(sine_of(NX)[:, None], (NX, NY)).astype(np.float32)


def split(value):
    high = value.astype(BF16)
    return high, (value - high.astype(F32)).astype(BF16)


def dot(a, b):
    return jnp.dot(a, b, preferred_element_type=F32)


def left_product(matrix, value):
    high, low = split(value)
    return dot(matrix[0], high) + dot(matrix[0], low) + dot(matrix[1], high)


def right_product(value, matrix):
    high, low = split(value)
    return dot(high, matrix[0]) + dot(low, matrix[0]) + dot(high, matrix[1])


def up_z(f):
    return pltpu.roll(f, NZ - 1, 0)


def down_z(f):
    return pltpu.roll(f, 1, 0)


def up_y(f):
    return pltpu.roll(f, NY - 1, 1)


def down_y(f):
    return pltpu.roll(f, 1, 1)


def along_height(f):
    return 0.5 * (up_z(f) - down_z(f))


def along_span(f):
    return 0.5 * (up_y(f) - down_y(f))


def along_stream(planes, j):
    return 0.5 * (planes[j + 1] - planes[j - 1])


def laplace(planes, j):
    f = planes[j]
    summed = planes[j + 1] + planes[j - 1] + up_z(f) + down_z(f) + up_y(f) + down_y(f)
    return summed - 6.0 * f


def to_modes(planes, to_z, to_y, out_ref):
    count = len(planes)
    side = left_product(to_z, jnp.concatenate(planes, axis=1))
    rows = jnp.concatenate([side[:, NY * i : NY * (i + 1)] for i in range(count)], axis=0)
    rows = right_product(rows, to_y)
    for i in range(count):
        out_ref[pl.ds(i, NZ, stride=count), :] = rows[NZ * i : NZ * (i + 1)]
    out_ref[NZ * count :, :] = jnp.zeros(((SPACE - NZ) * count, NY), F32)


def from_modes(in_ref, count, from_z, from_y):
    rows = jnp.concatenate([in_ref[pl.ds(i, NZ, stride=count), :] for i in range(count)], axis=0)
    rows = right_product(rows, from_y)
    side = jnp.concatenate([rows[NZ * i : NZ * (i + 1)] for i in range(count)], axis=1)
    side = left_product(from_z, side)
    return [side[:, NY * i : NY * (i + 1)] for i in range(count)]


def gather_slots(in_ref, first, count, total):
    parts = [in_ref[pl.ds(i, SPACE, stride=total), :] for i in range(first, first + count)]
    return jnp.concatenate(parts, axis=0)


def scatter_slots(out_ref, rows, first, count, total):
    for i in range(count):
        out_ref[pl.ds(first + i, SPACE, stride=total), :] = rows[SPACE * i : SPACE * (i + 1)]


def swap_waves(modes, sine):
    half = NX // 2
    return jnp.concatenate([sine[:half] * modes[half:], -sine[half:] * modes[:half]], axis=0)


def start_kernel(
    seeds, own, low, high, correction, rotor, column, to_z, to_y,
    buffer, first_trial, initial_out, laplace_out, viscosity_out,
):
    span_shift = seeds[0, 0]
    height_shift = seeds[0, 1]
    profile = column[...]
    outer = {-1: low[6], 3: high[6]}
    viscosity = {}
    for j in range(-1, 4):
        raw = correction[j] if 0 <= j < 3 else outer[j]
        viscosity[j] = BASE_VISCOSITY * jnp.exp(raw)
        viscosity_out[j + 1] = viscosity[j]
    trial = []
    for c in range(3):
        state = {}
        for j in range(-2, 5):
            if j < 0:
                raw = low[2 * c + j + 2]
            elif j < 3:
                raw = own[c, j]
            else:
                raw = high[2 * c + j - 3]
            raw = pltpu.roll(pltpu.roll(raw, span_shift, 1), height_shift, 0)
            state[j] = raw + profile if c == 0 else raw
        moved = {}
        for j in range(-1, 4):
            curvature = laplace(state, j)
            forcing = (
                viscosity[j] * curvature
                - profile * along_stream(state, j)
                - THRUST * rotor[j + 1] * state[j]
            )
            moved[j] = state[j] + TIME_STEP * forcing
            first_trial[5 * c + j + 1] = moved[j]
            if 0 <= j < 3:
                initial_out[3 * c + j] = state[j]
                laplace_out[3 * c + j] = curvature
        trial.append(moved)
    sources = [
        along_stream(trial[0], j) + along_span(trial[1][j]) + along_height(trial[2][j])
        for j in range(3)
    ]
    to_modes(sources, to_z, to_y, buffer)


def solve_one_kernel(modes_in, green, to_x, from_x, out):
    spectrum = left_product(to_x, gather_slots(modes_in, 0, 3, 3)) * green[...]
    scatter_slots(out, left_product(from_x, spectrum), 0, 7, 7)


def middle_kernel(
    modes_in, first_trial, initial, viscosity, rotor, observed, low, high, column,
    from_z, from_y, to_z, to_y,
    buffer, second_trial, laplace_out,
):
    profile = column[...]
    found = from_modes(modes_in, 7, from_z, from_y)
    pressure = {j - 2: found[j] for j in range(7)}
    seen = {j: observed[j] for j in range(3)}
    seen[-1] = low[7]
    seen[3] = high[7]
    trial = []
    for c in range(3):
        middle = {}
        for j in range(-1, 4):
            if c == 0:
                push = along_stream(pressure, j)
            elif c == 1:
                push = along_span(pressure[j])
            else:
                push = along_height(pressure[j])
            middle[j] = first_trial[5 * c + j + 1] - push
        moved = []
        for j in range(3):
            curvature = laplace(middle, j)
            laplace_out[3 * c + j] = curvature
            forcing = (
                viscosity[j + 1] * curvature
                - profile * along_stream(middle, j)
                - THRUST * rotor[j + 1] * middle[j]
            )
            moved.append(0.5 * initial[3 * c + j] + 0.5 * (middle[j] + TIME_STEP * forcing))
            if c > 0:
                second_trial[3 * (c - 1) + j] = moved[j]
        trial.append(moved)
    sheets = [trial[0][j] - seen[j] for j in range(3)]
    for j in range(3):
        sheets.append(
            along_span(trial[1][j]) + along_height(trial[2][j]) + along_stream(seen, j)
        )
    to_modes(sheets, to_z, to_y, buffer)


def solve_two_kernel(modes_in, green, sine_in, to_x, from_x, out):
    sine = sine_in[...]
    inverse = green[...]
    both = jnp.concatenate(
        [gather_slots(modes_in, 0, 3, 6), gather_slots(modes_in, 3, 3, 6)], axis=1
    )
    both = left_product(to_x, both)
    lead = both[:, :NY]
    second = inverse * (swap_waves(lead, sine) + both[:, NY:])
    misfit = lead - swap_waves(second, sine)
    third = inverse * swap_waves(misfit, sine)
    stream = misfit - swap_waves(third, sine)
    wide = left_product(from_x, jnp.concatenate([stream, third], axis=1))
    scatter_slots(out, wide[:, :NY], 0, 5, 13)
    scatter_slots(out, wide[:, NY:], 5, 5, 13)
    scatter_slots(out, left_product(from_x[:, SPACE : 4 * SPACE, :], second), 10, 3, 13)


def adjoint_kernel(
    modes_in, second_trial, laplace_mid, viscosity, rotor, observed, column,
    from_z, from_y, to_z, to_y,
    buffer, fourth_trial, velocity, share_out,
):
    profile = column[...]
    found = from_modes(modes_in, 13, from_z, from_y)
    stream = {j - 1: found[j] for j in range(5)}
    third = {j - 1: found[5 + j] for j in range(5)}
    second = found[10:]
    for j in range(3):
        velocity[0, 0, j] = stream[j] + observed[j] + along_stream(third, j)
        velocity[0, 1, j] = second_trial[j] - along_span(second[j])
        velocity[0, 2, j] = second_trial[3 + j] - along_height(second[j])
    share = [None] * 3
    trial = []
    for c in range(3):
        if c == 0:
            adjoint = stream
        elif c == 1:
            adjoint = {j: -along_span(third[j]) for j in range(-1, 4)}
        else:
            adjoint = {j: -along_height(third[j]) for j in range(-1, 4)}
        spread = {j: viscosity[j + 1] * adjoint[j] for j in range(-1, 4)}
        moved = []
        for j in range(3):
            pulled = (
                profile * along_stream(adjoint, j)
                + laplace(spread, j)
                - THRUST * rotor[j + 1] * adjoint[j]
            )
            moved.append(0.5 * adjoint[j] + 0.5 * TIME_STEP * pulled)
            fourth_trial[3 * c + j] = moved[j]
            term = adjoint[j] * laplace_mid[3 * c + j]
            share[j] = term if c == 0 else share[j] + term
        trial.append(moved)
    for j in range(3):
        share_out[j] = 0.5 * share[j]
    cross = [along_span(trial[1][j]) + along_height(trial[2][j]) for j in range(3)]
    lead = [0.5 * trial[0][j] for j in range(3)]
    sheets = [
        lead[0],
        cross[0] + lead[1],
        cross[1] + lead[2] - lead[0],
        cross[2] - lead[1],
        -lead[2],
    ]
    to_modes(sheets, to_z, to_y, buffer)


def solve_four_kernel(modes_in, green, to_x, from_x, out):
    spectrum = left_product(to_x, gather_slots(modes_in, 0, 5, 5)) * green[...]
    scatter_slots(out, left_product(from_x, spectrum), 0, 5, 5)


def gradient_kernel(
    modes_in, fourth_trial, laplace_start, viscosity, share, from_z, from_y, out
):
    found = from_modes(modes_in, 5, from_z, from_y)
    pressure = {j - 1: found[j] for j in range(5)}
    for j in range(3):
        push = [along_stream(pressure, j), along_span(pressure[j]), along_height(pressure[j])]
        total = share[j]
        for c in range(3):
            total = total + (fourth_trial[3 * c + j] - push[c]) * laplace_start[3 * c + j]
        total = TIME_STEP * viscosity[j + 1] * total
        for copy in range(out.shape[0]):
            out[copy, NZ * j : NZ * (j + 1), :] = total


def local_call(kernel, name, outs, *args):
    specs = [pl.BlockSpec(memory_space=pltpu.VMEM) for _ in args]
    if args[0].dtype == jnp.int32:
        specs[0] = pl.BlockSpec(memory_space=pltpu.SMEM)
    shapes = [jax.ShapeDtypeStruct(shape, F32) for shape in outs]
    spaces = [pl.BlockSpec(memory_space=pltpu.VMEM) for _ in outs]
    single = len(outs) == 1
    return pl.pallas_call(
        kernel,
        out_shape=shapes[0] if single else shapes,
        in_specs=specs,
        out_specs=spaces[0] if single else spaces,
        name=name,
        compiler_params=pltpu.CompilerParams(vmem_limit_bytes=24 * 1024 * 1024),
    )(*args)


def exchange(rows, axis="space"):
    count = lax.axis_size(axis)
    wide = rows.reshape(count, 1, rows.size // count)
    return lax.all_to_all(wide, axis, 0, 0, tiled=True).reshape(rows.shape)


def rotor_field(rotor_cells, stream_cells):
    rotor_stream = rotor_cells[:, 0:1]
    rotor_span = rotor_cells[:, 1:2]
    rotor_base = rotor_cells[:, 2:3]
    heights = jnp.arange(NZ, dtype=jnp.int32)[None, :]
    spans = jnp.arange(NY, dtype=jnp.int32)[None, :]
    in_stream = (stream_cells[None, :] == rotor_stream).astype(F32)
    in_height = ((heights >= rotor_base) & (heights < rotor_base + ROTOR)).astype(F32)
    in_span = ((spans >= rotor_span) & (spans < rotor_span + ROTOR)).astype(F32)
    sheet = (in_stream[:, :, None] * in_height[:, None, :]).reshape(in_stream.shape[0], -1)
    counted = jnp.dot(sheet.T, in_span, preferred_element_type=F32)
    return counted.reshape(stream_cells.shape[0], NZ, NY)


def green_table(position):
    square_x = jnp.asarray((sine_of(NX) ** 2).astype(np.float32))[:, None]
    square_y = jnp.asarray((sine_of(NY) ** 2).astype(np.float32))[None, :]
    square_z = jnp.asarray((sine_of(NZ) ** 2).astype(np.float32))
    height = jnp.minimum(position, NZ - 1)
    summed = square_x + lax.dynamic_index_in_dim(square_z, height, keepdims=False) + square_y
    null_x = jnp.asarray(np.arange(NX) % (NX // 2) == 0)[:, None]
    null_y = jnp.asarray(np.arange(NY) % (NY // 2) == 0)[None, :]
    null_mode = null_x & null_y & (height % (NZ // 2) == 0)
    table = jnp.where(null_mode, 0.0, -1.0 / jnp.where(null_mode, 1.0, summed))
    return jnp.where(position < NZ, table, 0.0)


def shards(inflow_seeds, rotor_cells, fluctuation, profile, correction, observed):
    position = lax.axis_index("space")
    samples = lax.axis_size("sample")
    forward = [(i, (i + 1) % SPACE) for i in range(SPACE)]
    backward = [(target, source) for source, target in forward]
    plane = (NZ, NY)
    last = jnp.concatenate(
        [fluctuation[:, 1:].reshape(6, NZ, NY), correction[2:], observed[2:]], axis=0
    )
    first = jnp.concatenate(
        [fluctuation[:, :2].reshape(6, NZ, NY), correction[:1], observed[:1]], axis=0
    )
    low = lax.ppermute(last, "space", forward)
    high = lax.ppermute(first, "space", backward)
    cells = (position * SLAB + jnp.arange(-1, SLAB + 1, dtype=jnp.int32)) % NX
    rotor = rotor_field(rotor_cells, cells)
    column = jnp.broadcast_to(profile[:, None], plane)
    green = green_table(position)
    to_y, from_y = jnp.asarray(TO_Y), jnp.asarray(FROM_Y)
    to_z, from_z = jnp.asarray(TO_Z), jnp.asarray(FROM_Z)

    buffer, first_trial, initial, laplace_start, viscosity = local_call(
        start_kernel, "start",
        [(SPACE * 3, NY), (15, *plane), (9, *plane), (9, *plane), (5, *plane)],
        inflow_seeds, fluctuation, low, high, correction, rotor, column, to_z, to_y,
    )
    buffer = exchange(buffer)
    buffer = local_call(
        solve_one_kernel, "solve_one", [(SPACE * 7, NY)],
        buffer, green, jnp.asarray(TO_X3), jnp.asarray(FROM_X7),
    )
    buffer = exchange(buffer)
    buffer, second_trial, laplace_mid = local_call(
        middle_kernel, "middle",
        [(SPACE * 6, NY), (6, *plane), (9, *plane)],
        buffer, first_trial, initial, viscosity, rotor, observed, low, high, column,
        from_z, from_y, to_z, to_y,
    )
    buffer = exchange(buffer)
    buffer = local_call(
        solve_two_kernel, "solve_two", [(SPACE * 13, NY)],
        buffer, green, jnp.asarray(SINE_X), jnp.asarray(TO_X3), jnp.asarray(FROM_X5),
    )
    buffer = exchange(buffer)
    buffer, fourth_trial, velocity, share = local_call(
        adjoint_kernel, "adjoint",
        [(SPACE * 5, NY), (9, *plane), (1, 3, 3, *plane), (3, *plane)],
        buffer, second_trial, laplace_mid, viscosity, rotor, observed, column,
        from_z, from_y, to_z, to_y,
    )
    buffer = exchange(buffer)
    buffer = local_call(
        solve_four_kernel, "solve_four", [(SPACE * 5, NY)],
        buffer, green, jnp.asarray(TO_X5), jnp.asarray(FROM_X5),
    )
    buffer = exchange(buffer)
    terms = local_call(
        gradient_kernel, "gradient", [(samples, SLAB * NZ, NY)],
        buffer, fourth_trial, laplace_start, viscosity, share, from_z, from_y,
    )
    terms = lax.all_to_all(terms, "sample", 0, 0, tiled=True)
    gradient = jnp.sum(terms, axis=0).reshape(SLAB, *plane)
    return (velocity, gradient)


def solution(mesh):
    return jax.shard_map(
        shards,
        mesh=mesh,
        in_specs=(
            P("sample", None),
            P(),
            P(None, "space", None, None),
            P(),
            P("space", None, None),
            P("space", None, None),
        ),
        out_specs=(P("sample", None, "space", None, None), P("space", None, None)),
        check_vma=False,
    )
```

time: 396 us -> 157 us (0.40)
  the two profiles are of different devices: /device:TPU:2 before, /device:TPU:1 now
where the time goes in v1:
time: 157 us
  blocking collectives  110 us (70%)
  starting transfers between devices  23.6 us (15%)
  waiting for transfers between devices  10 us (6%)
  Pallas kernels  7.68 us (5%)
  local copies, waits for them, and re-layouts  2.75 us (2%)
  other arithmetic  1.57 us (1%)
    all_to_all x5, blocking collectives, exchange(): return lax.all_to_all(wide, axis, 0, 0, tiled=True).reshape(rows.shape)  85.7 us
    all_to_all x1, blocking collectives, shards(): terms = lax.all_to_all(terms, 'sample', 0, 0, tiled=True)  24.2 us
    all_to_all x1, starting transfers between devices, exchange(): return lax.all_to_all(wide, axis, 0, 0, tiled=True).reshape(rows.shape)  12.8 us
    all_to_all x1, waiting for transfers between devices, exchange(): return lax.all_to_all(wide, axis, 0, 0, tiled=True).reshape(rows.shape)  10 us
    pallas_call x7, Pallas kernels, local_call(): pl.pallas_call(kernel, out_shape=shapes[0] if single else shapes, in_spec...  7.68 us
    ppermute x1, starting transfers between devices, shards(): high = lax.ppermute(first, 'space', backward)  6.24 us
    ppermute x1, starting transfers between devices, shards(): low = lax.ppermute(last, 'space', forward)  4.59 us
  transfers between devices with their start and end apart: 3, of which 1 were waited for; matrix products, arithmetic and copies ran while one was open for 1% of the time, Pallas kernels for 0%

profile of v1, /device:TPU:1, one launch (start us, length us, event | category | flops | bytes accessed | tf_op | source)
XLA Modules:
  0.0 156.8 jit_solution(16177830295018258758)
XLA Ops:
  0.6 1.0 fusion.12
  1.8 4.6 %collective-permute-start = (f32[8,48,128]{2,1,0:T(8,128)S(1)}, f32[8,48,128]{2,1,0:T(8,128)S(1)}, u32[]{:S(2)}, u32[]{:S(2)}) collective-permute-start(f32[8,48,128]{2,1,0:T(8,128)S(1)} %pad_maximum_fusion), channel_id=1, source_target_pairs={{0,1},{1,2},{2,3},{3,4},{4,5},{5,6},{6,7},{7,8},{8,9},{9,10},{10,1... | collective-permute-start | bytes 589832 | tf_op jit(solution)/shard_map/ppermute | solution.py:404
  6.4 6.2 %collective-permute-start.1 = (f32[8,48,128]{2,1,0:T(8,128)S(1)}, f32[8,48,128]{2,1,0:T(8,128)S(1)}, u32[]{:S(2)}, u32[]{:S(2)}) collective-permute-start(f32[8,48,128]{2,1,0:T(8,128)S(1)} %pad_maximum_fusion.1), channel_id=1, source_target_pairs={{1,0},{2,1},{3,2},{4,3},{5,4},{6,5},{7,6},{8,7},{9,8},{10,9},{11,1... | collective-permute-start | bytes 589832 | tf_op jit(solution)/shard_map/ppermute | solution.py:405
  12.8 0.6 dynamic_slice.4
  13.5 0.2 fusion.rotor
  13.7 0.4 copy-done.14
  14.1 0.6 broadcast_add_fusion
  14.9 0.5 copy-done.12
  15.4 1.9 %start.1 = (f32[192,128]{1,0:T(8,128)}, f32[15,48,128]{2,1,0:T(8,128)S(1)}, f32[9,48,128]{2,1,0:T(8,128)S(1)}, f32[9,48,128]{2,1,0:T(8,128)S(1)}, f32[5,48,128]{2,1,0:T(8,128)S(1)}) custom-call(s32[1,2]{1,0:T(1,128)S(1)} %copy-done.12, f32[3,3,48,128]{3,2,1,0:T(8,128)S(1)} %copy-done.1, f32[8,48,128]{2,1,0:T(8,128)S(1)} %collective-permute-done.low, ...), custom_call_target="tpu_custom_call" | custom-call | tf_op jit(solution)/shard_map/start/pallas_call | solution.py:349
  17.3 12.8 %all-to-all-start = ((f32[64,1,384]{2,1,0:T(1,128)}), f32[64,1,384]{2,1,0:T(1,128)S(1)}, u32[]{:S(2)}, u32[]{:S(2)}) async-start(f32[64,1,384]{2,1,0:T(1,128)} %bitcast.11), calls=%async_computation | async-start | bytes 196608 | tf_op jit(solution)/shard_map/all_to_all | solution.py:362
  30.3 10.0 %all-to-all-done = f32[64,1,384]{2,1,0:T(1,128)S(1)} async-done(((f32[64,1,384]{2,1,0:T(1,128)}), f32[64,1,384]{2,1,0:T(1,128)S(1)}, u32[]{:S(2)}, u32[]{:S(2)}) %all-to-all-start) | async-done | bytes 98336 | tf_op jit(solution)/shard_map/all_to_all | solution.py:362
  40.3 0.7 solve_one.1
  41.0 15.4 %all_to_all.35 = f32[64,1,896]{2,1,0:T(1,128)S(1)} all-to-all(f32[64,1,896]{2,1,0:T(1,128)S(1)} %bitcast.38), channel_id=1, replica_groups=mesh['sample'=8,'space'=64] {'space'}, dimensions={0} | all-to-all | bytes 458752 | tf_op jit(solution)/shard_map/all_to_all | solution.py:362
  56.5 1.3 middle.1
  57.8 17.1 %all_to_all.36 = f32[64,1,768]{2,1,0:T(1,128)S(1)} all-to-all(f32[64,1,768]{2,1,0:T(1,128)S(1)} %bitcast.45), channel_id=1, replica_groups=mesh['sample'=8,'space'=64] {'space'}, dimensions={0} | all-to-all | bytes 393216 | tf_op jit(solution)/shard_map/all_to_all | solution.py:362
  74.9 0.7 solve_two.1
  75.6 20.8 %all_to_all.37 = f32[64,1,1664]{2,1,0:T(1,128)S(1)} all-to-all(f32[64,1,1664]{2,1,0:T(1,128)S(1)} %bitcast.37), channel_id=1, replica_groups=mesh['sample'=8,'space'=64] {'space'}, dimensions={0} | all-to-all | bytes 851968 | tf_op jit(solution)/shard_map/all_to_all | solution.py:362
  96.4 1.9 %adjoint.1 = (f32[320,128]{1,0:T(8,128)S(1)}, f32[9,48,128]{2,1,0:T(8,128)S(1)}, f32[1,3,3,48,128]{4,3,2,1,0:T(8,128)}, f32[3,48,128]{2,1,0:T(8,128)S(1)}) custom-call(f32[832,128]{1,0:T(8,128)S(1)} %bitcast.36, f32[6,48,128]{2,1,0:T(8,128)S(1)} %get-tuple-element.19.second_trial, f32[9,48,128]{2,1,0:T(8,128)S(1)} %get-tuple-element.20.laplace_mid, ...), custom_call_target="tpu_custom_call" | custom-call | tf_op jit(solution)/shard_map/adjoint/pallas_call | solution.py:349
  98.4 16.7 %all_to_all.38 = f32[64,1,640]{2,1,0:T(1,128)S(1)} all-to-all(f32[64,1,640]{2,1,0:T(1,128)S(1)} %bitcast.46), channel_id=1, replica_groups=mesh['sample'=8,'space'=64] {'space'}, dimensions={0} | all-to-all | bytes 327680 | tf_op jit(solution)/shard_map/all_to_all | solution.py:362
  115.1 0.5 solve_four.1
  115.6 15.7 %all_to_all.39 = f32[64,1,640]{2,1,0:T(1,128)S(1)} all-to-all(f32[64,1,640]{2,1,0:T(1,128)S(1)} %bitcast.43), channel_id=1, replica_groups=mesh['sample'=8,'space'=64] {'space'}, dimensions={0} | all-to-all | bytes 327680 | tf_op jit(solution)/shard_map/all_to_all | solution.py:362
  131.3 0.6 gradient.1
  131.9 24.2 %all_to_all.40 = f32[8,144,128]{2,1,0:T(8,128)S(1)} all-to-all(f32[8,144,128]{2,1,0:T(8,128)S(1)} %gradient.1), channel_id=1, replica_groups=mesh['sample'=8,'space'=64] {'sample'}, dimensions={0} | all-to-all | bytes 1179648 | tf_op jit(solution)/shard_map/all_to_all | solution.py:452
  156.2 0.7 reduce_sum.9
  (49 shorter events, 0.4 us)
Async XLA Ops:
  0.6 1.1 copy-start.5
  0.6 1.1 copy-start.10
  1.8 13.0 %collective-permute-start = (f32[8,48,128]{2,1,0:T(8,128)S(1)}, f32[8,48,128]{2,1,0:T(8,128)S(1)}, u32[]{:S(2)}, u32[]{:S(2)}) collective-permute-start(f32[8,48,128]{2,1,0:T(8,128)S(1)} %pad_maximum_fusion), channel_id=1, source_target_pairs={{0,1},{1,2},{2,3},{3,4},{4,5},{5,6},{6,7},{7,8},{8,9},{9,10},{10,1... | collective-permute-start | bytes 589832 | tf_op jit(solution)/shard_map/ppermute | solution.py:404
  6.4 6.4 %copy-start.13 = (s32[64,3]{0,1:T(4,128)S(1)}, s32[64,3]{0,1:T(4,128)}, u32[]{:S(2)}) copy-start(s32[64,3]{0,1:T(4,128)} %param.21) | copy-start | bytes 2308
  6.4 6.4 %copy-start.19 = (f32[48]{0:T(128)S(1)}, f32[48]{0:T(128)}, u32[]{:S(2)}) copy-start(f32[48]{0:T(128)} %constant.76.clone) | copy-start | bytes 580
  6.4 8.5 %copy-start.4 = (bf16[2,128,128]{2,1,0:T(8,128)(2,1)S(1)}, bf16[2,128,128]{2,1,0:T(8,128)(2,1)}, u32[]{:S(2)}) copy-start(bf16[2,128,128]{2,1,0:T(8,128)(2,1)} %constant.79.clone.to_y) | copy-start | bytes 196612
  6.4 8.5 %copy-start.1 = (f32[3,3,48,128]{3,2,1,0:T(8,128)S(1)}, f32[3,3,48,128]{3,2,1,0:T(8,128)}, u32[]{:S(2)}) copy-start(f32[3,3,48,128]{3,2,1,0:T(8,128)} %own.1) | copy-start | bytes 663556
  6.4 8.4 %collective-permute-start.1 = (f32[8,48,128]{2,1,0:T(8,128)S(1)}, f32[8,48,128]{2,1,0:T(8,128)S(1)}, u32[]{:S(2)}, u32[]{:S(2)}) collective-permute-start(f32[8,48,128]{2,1,0:T(8,128)S(1)} %pad_maximum_fusion.1), channel_id=1, source_target_pairs={{1,0},{2,1},{3,2},{4,3},{5,4},{6,5},{7,6},{8,7},{9,8},{10,9},{11,1... | collective-permute-start | bytes 589832 | tf_op jit(solution)/shard_map/ppermute | solution.py:405
  13.4 0.7 copy-start.14
  13.4 1.4 copy-start.18
  13.7 1.2 copy-start.9
  14.8 0.7 copy-start.12
  15.4 24.9 %copy-start.6 = (bf16[2,448,192]{2,1,0:T(8,128)(2,1)S(1)}, bf16[2,448,192]{2,1,0:T(8,128)(2,1)}, u32[]{:S(2)}) copy-start(bf16[2,448,192]{2,1,0:T(8,128)(2,1)} %constant.84.clone.from_x) | copy-start | bytes 1032196
  17.3 23.0 %copy-start.2 = (bf16[2,192,192]{2,1,0:T(8,128)(2,1)S(1)}, bf16[2,192,192]{2,1,0:T(8,128)(2,1)}, u32[]{:S(2)}) copy-start(bf16[2,192,192]{2,1,0:T(8,128)(2,1)} %constant.83.clone.to_x) | copy-start | bytes 442372
  17.3 12.8 %copy-start.15 = (pred[128]{0:T(512)(128)(4,1)S(1)}, pred[128]{0:T(512)(128)(4,1)}, u32[]{:S(2)}) copy-start(pred[128]{0:T(512)(128)(4,1)} %constant.78.clone) | copy-start | bytes 388
  17.3 12.8 %copy-start.16 = (pred[192]{0:T(512)(128)(4,1)S(1)}, pred[192]{0:T(512)(128)(4,1)}, u32[]{:S(2)}) copy-start(pred[192]{0:T(512)(128)(4,1)} %constant.77.clone) | copy-start | bytes 580
  17.3 12.8 %copy-start.17 = (f32[128]{0:T(128)S(1)}, f32[128]{0:T(128)}, u32[]{:S(2)}) copy-start(f32[128]{0:T(128)} %constant.75.clone) | copy-start | bytes 1540
  17.3 23.0 %all-to-all-start = ((f32[64,1,384]{2,1,0:T(1,128)}), f32[64,1,384]{2,1,0:T(1,128)S(1)}, u32[]{:S(2)}, u32[]{:S(2)}) async-start(f32[64,1,384]{2,1,0:T(1,128)} %bitcast.11), calls=%async_computation | async-start | bytes 196608 | tf_op jit(solution)/shard_map/all_to_all | solution.py:362
  41.0 15.4 %copy-start.3 = (bf16[2,128,128]{2,1,0:T(8,128)(2,1)S(1)}, bf16[2,128,128]{2,1,0:T(8,128)(2,1)}, u32[]{:S(2)}) copy-start(bf16[2,128,128]{2,1,0:T(8,128)(2,1)} %constant.80.clone.from_y) | copy-start | bytes 196612
  41.0 15.4 %copy-start.8 = (bf16[2,48,48]{2,1,0:T(8,128)(2,1)S(1)}, bf16[2,48,48]{2,1,0:T(8,128)(2,1)}, u32[]{:S(2)}) copy-start(bf16[2,48,48]{2,1,0:T(8,128)(2,1)} %constant.82.clone.from_z) | copy-start | bytes 27652
  56.5 18.4 %copy-start.11 = (f32[192,128]{1,0:T(8,128)S(1)}, f32[192,128]{1,0:T(8,128)}, u32[]{:S(2)}) copy-start(f32[192,128]{1,0:T(8,128)} %constant.85.clone.sine_in) | copy-start | bytes 294916
  57.8 17.1 %copy-start = (bf16[2,320,192]{2,1,0:T(8,128)(2,1)S(1)}, bf16[2,320,192]{2,1,0:T(8,128)(2,1)}, u32[]{:S(2)}) copy-start(bf16[2,320,192]{2,1,0:T(8,128)(2,1)} %constant.86.clone.from_x) | copy-start | bytes 737284
  98.3 16.7 %copy-start.7 = (bf16[2,192,320]{2,1,0:T(8,128)(2,1)S(1)}, bf16[2,192,320]{2,1,0:T(8,128)(2,1)}, u32[]{:S(2)}) copy-start(bf16[2,192,320]{2,1,0:T(8,128)(2,1)} %constant.87.clone.to_x) | copy-start | bytes 737284

commit v2 on v1

--- a/solution.py
+++ b/solution.py
@@ -42,11 +42,13 @@
     return np.sin(2.0 * np.pi / length * waves)
 
 
-def two_part(matrix):
-    matrix = np.asarray(matrix, np.float32)
-    high = matrix.astype(ml_dtypes.bfloat16)
-    low = (matrix - high.astype(np.float32)).astype(ml_dtypes.bfloat16)
-    return np.stack([high, low])
+def in_parts(matrix, count):
+    parts = []
+    rest = np.asarray(matrix, np.float64)
+    for _ in range(count):
+        parts.append(rest.astype(ml_dtypes.bfloat16))
+        rest = rest - parts[-1].astype(np.float64)
+    return np.stack(parts)
 
 
 BASIS_X = real_basis(NX)
@@ -60,20 +62,21 @@
     return ((SLAB * device + slot) % NX).reshape(-1)
 
 
-TO_Y = two_part(BASIS_Y)
-FROM_Y = two_part(BASIS_Y.T)
-TO_Z = two_part(BASIS_Z.T)
-FROM_Z = two_part(BASIS_Z)
-TO_X3 = two_part(BASIS_X[stream_rows(0, 3)].T)
-TO_X5 = two_part(BASIS_X[stream_rows(-1, 5)].T)
-FROM_X7 = two_part(BASIS_X[stream_rows(-2, 7)])
-FROM_X5 = two_part(BASIS_X[stream_rows(-1, 5)])
+TO_Y = in_parts(BASIS_Y, 2)
+TO_Z = in_parts(BASIS_Z.T, 2)
+TO_X = in_parts(BASIS_X[stream_rows(0, 3)].T, 2)
+FROM_Y = in_parts(BASIS_Y.T, 3)
+FROM_Z = in_parts(BASIS_Z, 3)
+FROM_X = in_parts(BASIS_X[stream_rows(0, 4)], 3)
 SINE_X = np.broadcast_to(sine_of(NX)[:, None], (NX, NY)).astype(np.float32)
 
 
-def split(value):
-    high = value.astype(BF16)
-    return high, (value - high.astype(F32)).astype(BF16)
+def split(value, count):
+    parts = []
+    for _ in range(count - 1):
+        parts.append(value.astype(BF16))
+        value = value - parts[-1].astype(F32)
+    return parts + [value.astype(BF16)]
 
 
 def dot(a, b):
@@ -81,13 +84,17 @@
 
 
 def left_product(matrix, value):
-    high, low = split(value)
-    return dot(matrix[0], high) + dot(matrix[0], low) + dot(matrix[1], high)
+    count = matrix.shape[0]
+    parts = split(value, count)
+    pairs = [(i, order - i) for order in reversed(range(count)) for i in range(order + 1)]
+    return sum(dot(matrix[i], parts[k]) for i, k in pairs)
 
 
 def right_product(value, matrix):
-    high, low = split(value)
-    return dot(high, matrix[0]) + dot(low, matrix[0]) + dot(high, matrix[1])
+    count = matrix.shape[0]
+    parts = split(value, count)
+    pairs = [(i, order - i) for order in reversed(range(count)) for i in range(order + 1)]
+    return sum(dot(parts[k], matrix[i]) for i, k in pairs)
 
 
 def up_z(f):
@@ -122,6 +129,15 @@
     f = planes[j]
     summed = planes[j + 1] + planes[j - 1] + up_z(f) + down_z(f) + up_y(f) + down_y(f)
     return summed - 6.0 * f
+
+
+def cross_laplace(f):
+    return along_span(along_span(f)) + along_height(along_height(f))
+
+
+def with_plane_below(planes, source):
+    below = 2.0 * planes[1] - planes[3] + 4.0 * (source - cross_laplace(planes[1]))
+    return {-1: below, 0: planes[0], 1: planes[1], 2: planes[2], 3: planes[3]}
 
 
 def to_modes(planes, to_z, to_y, out_ref):
@@ -158,18 +174,22 @@
 
 
 def start_kernel(
-    seeds, own, low, high, correction, rotor, column, to_z, to_y,
-    buffer, first_trial, initial_out, laplace_out, viscosity_out,
+    seeds, own, low, high, correction, rotor, column, green, to_z, to_y,
+    buffer, first_trial, source_out, initial_out, laplace_out, viscosity_out,
 ):
     span_shift = seeds[0, 0]
     height_shift = seeds[0, 1]
     profile = column[...]
-    outer = {-1: low[6], 3: high[6]}
     viscosity = {}
-    for j in range(-1, 4):
-        raw = correction[j] if 0 <= j < 3 else outer[j]
+    for j in range(-2, 5):
+        if j < 0:
+            raw = low[8 + j]
+        elif j < 3:
+            raw = correction[j]
+        else:
+            raw = high[3 + j]
         viscosity[j] = BASE_VISCOSITY * jnp.exp(raw)
-        viscosity_out[j + 1] = viscosity[j]
+        viscosity_out[j + 2] = viscosity[j]
     trial = []
     for c in range(3):
         state = {}
@@ -200,58 +220,52 @@
         along_stream(trial[0], j) + along_span(trial[1][j]) + along_height(trial[2][j])
         for j in range(3)
     ]
+    source_out[...] = sources[1]
     to_modes(sources, to_z, to_y, buffer)
 
 
-def solve_one_kernel(modes_in, green, to_x, from_x, out):
+def solve_kernel(modes_in, green, to_x, from_x, out):
     spectrum = left_product(to_x, gather_slots(modes_in, 0, 3, 3)) * green[...]
-    scatter_slots(out, left_product(from_x, spectrum), 0, 7, 7)
+    scatter_slots(out, left_product(from_x, spectrum), 0, 4, 4)
 
 
 def middle_kernel(
-    modes_in, first_trial, initial, viscosity, rotor, observed, low, high, column,
+    modes_in, first_trial, source, initial, viscosity, rotor, observed, low, high, column,
     from_z, from_y, to_z, to_y,
-    buffer, second_trial, laplace_out,
+    buffer, second_trial, source_out, laplace_out,
 ):
     profile = column[...]
-    found = from_modes(modes_in, 7, from_z, from_y)
-    pressure = {j - 2: found[j] for j in range(7)}
+    pressure = with_plane_below(from_modes(modes_in, 4, from_z, from_y), source[...])
     seen = {j: observed[j] for j in range(3)}
-    seen[-1] = low[7]
-    seen[3] = high[7]
+    seen[-1] = low[8]
+    seen[3] = high[8]
+    span = {j: first_trial[6 + j] - along_span(pressure[j]) for j in range(-1, 4)}
+    height = {j: first_trial[11 + j] - along_height(pressure[j]) for j in range(-1, 4)}
+    stream = {j: first_trial[1 + j] - along_stream(pressure, j) for j in range(3)}
+    stream[-1] = stream[1] + 2.0 * (along_span(span[0]) + along_height(height[0]))
+    stream[3] = stream[1] - 2.0 * (along_span(span[2]) + along_height(height[2]))
     trial = []
-    for c in range(3):
-        middle = {}
-        for j in range(-1, 4):
-            if c == 0:
-                push = along_stream(pressure, j)
-            elif c == 1:
-                push = along_span(pressure[j])
-            else:
-                push = along_height(pressure[j])
-            middle[j] = first_trial[5 * c + j + 1] - push
-        moved = []
+    for c, middle in enumerate((stream, span, height)):
+        moved = {}
         for j in range(3):
             curvature = laplace(middle, j)
             laplace_out[3 * c + j] = curvature
             forcing = (
-                viscosity[j + 1] * curvature
+                viscosity[j + 2] * curvature
                 - profile * along_stream(middle, j)
                 - THRUST * rotor[j + 1] * middle[j]
             )
-            moved.append(0.5 * initial[3 * c + j] + 0.5 * (middle[j] + TIME_STEP * forcing))
-            if c > 0:
-                second_trial[3 * (c - 1) + j] = moved[j]
+            moved[j] = 0.5 * initial[3 * c + j] + 0.5 * (middle[j] + TIME_STEP * forcing)
+            second_trial[3 * c + j] = moved[j]
         trial.append(moved)
+    cross = [along_span(trial[1][j]) + along_height(trial[2][j]) for j in range(3)]
+    source_out[...] = along_stream(trial[0], 1) + cross[1]
     sheets = [trial[0][j] - seen[j] for j in range(3)]
-    for j in range(3):
-        sheets.append(
-            along_span(trial[1][j]) + along_height(trial[2][j]) + along_stream(seen, j)
-        )
+    sheets += [cross[j] + along_stream(seen, j) for j in range(3)]
     to_modes(sheets, to_z, to_y, buffer)
 
 
-def solve_two_kernel(modes_in, green, sine_in, to_x, from_x, out):
+def solve_both_kernel(modes_in, green, sine_in, to_x, from_x, out):
     sine = sine_in[...]
     inverse = green[...]
     both = jnp.concatenate(
@@ -260,89 +274,82 @@
     both = left_product(to_x, both)
     lead = both[:, :NY]
     second = inverse * (swap_waves(lead, sine) + both[:, NY:])
-    misfit = lead - swap_waves(second, sine)
-    third = inverse * swap_waves(misfit, sine)
-    stream = misfit - swap_waves(third, sine)
-    wide = left_product(from_x, jnp.concatenate([stream, third], axis=1))
-    scatter_slots(out, wide[:, :NY], 0, 5, 13)
-    scatter_slots(out, wide[:, NY:], 5, 5, 13)
-    scatter_slots(out, left_product(from_x[:, SPACE : 4 * SPACE, :], second), 10, 3, 13)
+    third = inverse * swap_waves(lead - swap_waves(second, sine), sine)
+    wide = left_product(from_x, jnp.concatenate([second, third], axis=1))
+    scatter_slots(out, wide[:, :NY], 0, 4, 8)
+    scatter_slots(out, wide[:, NY:], 4, 4, 8)
 
 
 def adjoint_kernel(
-    modes_in, second_trial, laplace_mid, viscosity, rotor, observed, column,
+    modes_in, second_trial, source, laplace_mid, viscosity, rotor, observed, column,
     from_z, from_y, to_z, to_y,
-    buffer, fourth_trial, velocity, share_out,
+    buffer, fourth_trial, source_out, velocity, share_out,
 ):
     profile = column[...]
-    found = from_modes(modes_in, 13, from_z, from_y)
-    stream = {j - 1: found[j] for j in range(5)}
-    third = {j - 1: found[5 + j] for j in range(5)}
-    second = found[10:]
+    found = from_modes(modes_in, 8, from_z, from_y)
+    second = with_plane_below(found[:4], source[...])
+    misfit = []
     for j in range(3):
-        velocity[0, 0, j] = stream[j] + observed[j] + along_stream(third, j)
-        velocity[0, 1, j] = second_trial[j] - along_span(second[j])
-        velocity[0, 2, j] = second_trial[3 + j] - along_height(second[j])
+        stream = second_trial[j] - along_stream(second, j)
+        velocity[0, 0, j] = stream
+        velocity[0, 1, j] = second_trial[3 + j] - along_span(second[j])
+        velocity[0, 2, j] = second_trial[6 + j] - along_height(second[j])
+        misfit.append(stream - observed[j])
+    third = with_plane_below(found[4:], 0.5 * (misfit[2] - misfit[0]))
+    span = {j: -along_span(third[j]) for j in range(-1, 4)}
+    height = {j: -along_height(third[j]) for j in range(-1, 4)}
+    cross = {j: along_span(span[j]) + along_height(height[j]) for j in range(-1, 4)}
+    stream = {j: misfit[j] - along_stream(third, j) for j in range(3)}
+    stream[-1] = stream[1] + 2.0 * cross[0]
+    stream[3] = stream[1] - 2.0 * cross[2]
+    stream[-2] = stream[0] + 2.0 * cross[-1]
+    stream[4] = stream[2] - 2.0 * cross[3]
     share = [None] * 3
     trial = []
-    for c in range(3):
-        if c == 0:
-            adjoint = stream
-        elif c == 1:
-            adjoint = {j: -along_span(third[j]) for j in range(-1, 4)}
-        else:
-            adjoint = {j: -along_height(third[j]) for j in range(-1, 4)}
-        spread = {j: viscosity[j + 1] * adjoint[j] for j in range(-1, 4)}
-        moved = []
-        for j in range(3):
+    for c, adjoint in enumerate((stream, span, height)):
+        spread = {j: viscosity[j + 2] * adjoint[j] for j in adjoint}
+        moved = {}
+        for j in range(-1, 4) if c == 0 else range(3):
             pulled = (
                 profile * along_stream(adjoint, j)
                 + laplace(spread, j)
                 - THRUST * rotor[j + 1] * adjoint[j]
             )
-            moved.append(0.5 * adjoint[j] + 0.5 * TIME_STEP * pulled)
+            moved[j] = 0.5 * adjoint[j] + 0.5 * TIME_STEP * pulled
+        for j in range(3):
             fourth_trial[3 * c + j] = moved[j]
             term = adjoint[j] * laplace_mid[3 * c + j]
             share[j] = term if c == 0 else share[j] + term
         trial.append(moved)
     for j in range(3):
         share_out[j] = 0.5 * share[j]
-    cross = [along_span(trial[1][j]) + along_height(trial[2][j]) for j in range(3)]
-    lead = [0.5 * trial[0][j] for j in range(3)]
-    sheets = [
-        lead[0],
-        cross[0] + lead[1],
-        cross[1] + lead[2] - lead[0],
-        cross[2] - lead[1],
-        -lead[2],
+    sources = [
+        along_stream(trial[0], j) + along_span(trial[1][j]) + along_height(trial[2][j])
+        for j in range(3)
     ]
-    to_modes(sheets, to_z, to_y, buffer)
-
-
-def solve_four_kernel(modes_in, green, to_x, from_x, out):
-    spectrum = left_product(to_x, gather_slots(modes_in, 0, 5, 5)) * green[...]
-    scatter_slots(out, left_product(from_x, spectrum), 0, 5, 5)
+    source_out[...] = sources[1]
+    to_modes(sources, to_z, to_y, buffer)
 
 
 def gradient_kernel(
-    modes_in, fourth_trial, laplace_start, viscosity, share, from_z, from_y, out
+    modes_in, fourth_trial, source, laplace_start, viscosity, share, from_z, from_y, out
 ):
-    found = from_modes(modes_in, 5, from_z, from_y)
-    pressure = {j - 1: found[j] for j in range(5)}
+    pressure = with_plane_below(from_modes(modes_in, 4, from_z, from_y), source[...])
     for j in range(3):
         push = [along_stream(pressure, j), along_span(pressure[j]), along_height(pressure[j])]
         total = share[j]
         for c in range(3):
             total = total + (fourth_trial[3 * c + j] - push[c]) * laplace_start[3 * c + j]
-        total = TIME_STEP * viscosity[j + 1] * total
+        total = TIME_STEP * viscosity[j + 2] * total
         for copy in range(out.shape[0]):
             out[copy, NZ * j : NZ * (j + 1), :] = total
 
 
 def local_call(kernel, name, outs, *args):
     specs = [pl.BlockSpec(memory_space=pltpu.VMEM) for _ in args]
-    if args[0].dtype == jnp.int32:
+    if name == "start":
         specs[0] = pl.BlockSpec(memory_space=pltpu.SMEM)
+        specs[7] = pl.BlockSpec(memory_space=pl.ANY)
     shapes = [jax.ShapeDtypeStruct(shape, F32) for shape in outs]
     spaces = [pl.BlockSpec(memory_space=pltpu.VMEM) for _ in outs]
     single = len(outs) == 1
@@ -396,10 +403,10 @@
     backward = [(target, source) for source, target in forward]
     plane = (NZ, NY)
     last = jnp.concatenate(
-        [fluctuation[:, 1:].reshape(6, NZ, NY), correction[2:], observed[2:]], axis=0
+        [fluctuation[:, 1:].reshape(6, NZ, NY), correction[1:], observed[2:]], axis=0
     )
     first = jnp.concatenate(
-        [fluctuation[:, :2].reshape(6, NZ, NY), correction[:1], observed[:1]], axis=0
+        [fluctuation[:, :2].reshape(6, NZ, NY), correction[:2], observed[:1]], axis=0
     )
     low = lax.ppermute(last, "space", forward)
     high = lax.ppermute(first, "space", backward)
@@ -407,47 +414,46 @@
     rotor = rotor_field(rotor_cells, cells)
     column = jnp.broadcast_to(profile[:, None], plane)
     green = green_table(position)
+    to_x, from_x = jnp.asarray(TO_X), jnp.asarray(FROM_X)
     to_y, from_y = jnp.asarray(TO_Y), jnp.asarray(FROM_Y)
     to_z, from_z = jnp.asarray(TO_Z), jnp.asarray(FROM_Z)
 
-    buffer, first_trial, initial, laplace_start, viscosity = local_call(
+    buffer, first_trial, source, initial, laplace_start, viscosity = local_call(
         start_kernel, "start",
-        [(SPACE * 3, NY), (15, *plane), (9, *plane), (9, *plane), (5, *plane)],
-        inflow_seeds, fluctuation, low, high, correction, rotor, column, to_z, to_y,
+        [(SPACE * 3, NY), (15, *plane), plane, (9, *plane), (9, *plane), (7, *plane)],
+        inflow_seeds, fluctuation, low, high, correction, rotor, column, green, to_z, to_y,
     )
     buffer = exchange(buffer)
     buffer = local_call(
-        solve_one_kernel, "solve_one", [(SPACE * 7, NY)],
-        buffer, green, jnp.asarray(TO_X3), jnp.asarray(FROM_X7),
-    )
-    buffer = exchange(buffer)
-    buffer, second_trial, laplace_mid = local_call(
+        solve_kernel, "solve_one", [(SPACE * 4, NY)], buffer, green, to_x, from_x
+    )
+    buffer = exchange(buffer)
+    buffer, second_trial, source, laplace_mid = local_call(
         middle_kernel, "middle",
-        [(SPACE * 6, NY), (6, *plane), (9, *plane)],
-        buffer, first_trial, initial, viscosity, rotor, observed, low, high, column,
+        [(SPACE * 6, NY), (9, *plane), plane, (9, *plane)],
+        buffer, first_trial, source, initial, viscosity, rotor, observed, low, high, column,
         from_z, from_y, to_z, to_y,
     )
     buffer = exchange(buffer)
     buffer = local_call(
-        solve_two_kernel, "solve_two", [(SPACE * 13, NY)],
-        buffer, green, jnp.asarray(SINE_X), jnp.asarray(TO_X3), jnp.asarray(FROM_X5),
-    )
-    buffer = exchange(buffer)
-    buffer, fourth_trial, velocity, share = local_call(
+        solve_both_kernel, "solve_two", [(SPACE * 8, NY)],
+        buffer, green, jnp.asarray(SINE_X), to_x, from_x,
+    )
+    buffer = exchange(buffer)
+    buffer, fourth_trial, source, velocity, share = local_call(
         adjoint_kernel, "adjoint",
-        [(SPACE * 5, NY), (9, *plane), (1, 3, 3, *plane), (3, *plane)],
-        buffer, second_trial, laplace_mid, viscosity, rotor, observed, column,
+        [(SPACE * 3, NY), (9, *plane), plane, (1, 3, 3, *plane), (3, *plane)],
+        buffer, second_trial, source, laplace_mid, viscosity, rotor, observed, column,
         from_z, from_y, to_z, to_y,
     )
     buffer = exchange(buffer)
     buffer = local_call(
-        solve_four_kernel, "solve_four", [(SPACE * 5, NY)],
-        buffer, green, jnp.asarray(TO_X5), jnp.asarray(FROM_X5),
+        solve_kernel, "solve_four", [(SPACE * 4, NY)], buffer, green, to_x, from_x
     )
     buffer = exchange(buffer)
     terms = local_call(
         gradient_kernel, "gradient", [(samples, SLAB * NZ, NY)],
-        buffer, fourth_trial, laplace_start, viscosity, share, from_z, from_y,
+        buffer, fourth_trial, source, laplace_start, viscosity, share, from_z, from_y,
     )
     terms = lax.all_to_all(terms, "sample", 0, 0, tiled=True)
     gradient = jnp.sum(terms, axis=0).reshape(SLAB, *plane)

time: 157 us -> 151 us (0.962)
  blocking collectives: 110 us -> 124 us
  starting transfers between devices: 23.6 us -> 10.7 us
  waiting for transfers between devices: 10 us -> 0.01 us
  local copies, waits for them, and re-layouts: 2.75 us -> 4.76 us
    all_to_all x5 -> x6, blocking collectives: 85.7 us -> 99.2 us  [exchange(): return lax.all_to_all(wide, axis, 0, 0, tiled=True).reshape(rows.shape)]
    all_to_all x1 -> x0, starting transfers between devices: 12.8 us -> none  [exchange(): return lax.all_to_all(wide, axis, 0, 0, tiled=True).reshape(rows.shape)]
    all_to_all x1 -> x0, waiting for transfers between devices: 10 us -> none  [exchange(): return lax.all_to_all(wide, axis, 0, 0, tiled=True).reshape(rows.shape)]
    unnamed x40 -> x36, local copies, waits for them, and re-layouts: 1.04 us -> 3.28 us
  transfers between devices with their start and end apart: 3 -> 2, of which waited for: 1 -> 0; matrix products, arithmetic and copies ran while one was open for 1% -> 1% of each run, Pallas kernels for 0% -> 0%
where the time goes in v2:
time: 151 us; the launch traced here: 150 us
  blocking collectives  124 us (82%)
  starting transfers between devices  10.7 us (7%)
  Pallas kernels  7.42 us (5%)
  local copies, waits for them, and re-layouts  4.76 us (3%)
  other arithmetic  1.57 us (1%)
    all_to_all x6, blocking collectives, exchange(): return lax.all_to_all(wide, axis, 0, 0, tiled=True).reshape(rows.shape)  99.2 us
    all_to_all x1, blocking collectives, shards(): terms = lax.all_to_all(terms, 'sample', 0, 0, tiled=True)  25.2 us
    pallas_call x7, Pallas kernels, local_call(): pl.pallas_call(kernel, out_shape=shapes[0] if single else shapes, in_spec...  7.42 us
    ppermute x1, starting transfers between devices, shards(): high = lax.ppermute(first, 'space', backward)  6.11 us
    ppermute x1, starting transfers between devices, shards(): low = lax.ppermute(last, 'space', forward)  4.59 us
    unnamed x36, local copies, waits for them, and re-layouts  3.28 us
  transfers between devices with their start and end apart: 2, of which 0 were waited for; matrix products, arithmetic and copies ran while one was open for 1% of the time, Pallas kernels for 0%

profile of v2, /device:TPU:1, one launch (start us, length us, event | category | flops | bytes accessed | tf_op | source)
XLA Modules:
  0.0 150.0 jit_solution(12211510838972865996)
XLA Ops:
  0.6 0.8 fusion.14
  1.7 4.6 %collective-permute-start = (f32[9,48,128]{2,1,0:T(8,128)S(1)}, f32[9,48,128]{2,1,0:T(8,128)S(1)}, u32[]{:S(2)}, u32[]{:S(2)}) collective-permute-start(f32[9,48,128]{2,1,0:T(8,128)S(1)} %pad_maximum_fusion), channel_id=1, source_target_pairs={{0,1},{1,2},{2,3},{3,4},{4,5},{5,6},{6,7},{7,8},{8,9},{9,10},{10,1... | collective-permute-start | bytes 663560 | tf_op jit(solution)/shard_map/ppermute | solution.py:411
  6.3 6.1 %collective-permute-start.1 = (f32[9,48,128]{2,1,0:T(8,128)S(1)}, f32[9,48,128]{2,1,0:T(8,128)S(1)}, u32[]{:S(2)}, u32[]{:S(2)}) collective-permute-start(f32[9,48,128]{2,1,0:T(8,128)S(1)} %pad_maximum_fusion.1), channel_id=1, source_target_pairs={{1,0},{2,1},{3,2},{4,3},{5,4},{6,5},{7,6},{8,7},{9,8},{10,9},{11,1... | collective-permute-start | bytes 663560 | tf_op jit(solution)/shard_map/ppermute | solution.py:412
  12.5 0.7 copy-done.11
  13.1 0.7 copy-done.17
  13.8 0.6 dynamic_slice.4
  14.4 0.7 copy-done.12
  15.1 0.6 broadcast_add_fusion
  16.7 0.5 copy-done.16
  17.4 1.3 start.1
  18.7 20.8 %all_to_all.35 = f32[64,1,384]{2,1,0:T(1,128)S(1)} all-to-all(f32[64,1,384]{2,1,0:T(1,128)S(1)} %bitcast.47), channel_id=1, replica_groups=mesh['sample'=8,'space'=64] {'space'}, dimensions={0} | all-to-all | bytes 196608 | tf_op jit(solution)/shard_map/all_to_all | solution.py:369
  39.5 0.7 solve_one.1
  40.2 14.7 %all_to_all.36 = f32[64,1,512]{2,1,0:T(1,128)S(1)} all-to-all(f32[64,1,512]{2,1,0:T(1,128)S(1)} %bitcast.42), channel_id=1, replica_groups=mesh['sample'=8,'space'=64] {'space'}, dimensions={0} | all-to-all | bytes 262144 | tf_op jit(solution)/shard_map/all_to_all | solution.py:369
  54.9 1.3 middle.1
  56.2 15.8 %all_to_all.37 = f32[64,1,768]{2,1,0:T(1,128)S(1)} all-to-all(f32[64,1,768]{2,1,0:T(1,128)S(1)} %bitcast.45), channel_id=1, replica_groups=mesh['sample'=8,'space'=64] {'space'}, dimensions={0} | all-to-all | bytes 393216 | tf_op jit(solution)/shard_map/all_to_all | solution.py:369
  72.0 0.7 solve_two.1
  72.7 17.5 %all_to_all.38 = f32[64,1,1024]{2,1,0:T(1,128)S(1)} all-to-all(f32[64,1,1024]{2,1,0:T(1,128)S(1)} %bitcast.36), channel_id=1, replica_groups=mesh['sample'=8,'space'=64] {'space'}, dimensions={0} | all-to-all | bytes 524288 | tf_op jit(solution)/shard_map/all_to_all | solution.py:369
  90.2 2.0 %adjoint.1 = (f32[192,128]{1,0:T(8,128)S(1)}, f32[9,48,128]{2,1,0:T(8,128)S(1)}, f32[48,128]{1,0:T(8,128)S(1)}, f32[1,3,3,48,128]{4,3,2,1,0:T(8,128)}, f32[3,48,128]{2,1,0:T(8,128)S(1)}) custom-call(f32[512,128]{1,0:T(8,128)S(1)} %bitcast.37, f32[9,48,128]{2,1,0:T(8,128)S(1)} %get-tuple-element.23.second_trial, f32[48,128]{1,0:T(8,128)S(1)} %get-tuple-element.24.source, ...), custom_call_target="tpu_custom_call" | custom-call | tf_op jit(solution)/shard_map/adjoint/pallas_call | solution.py:356
  92.2 16.0 %all_to_all.39 = f32[64,1,384]{2,1,0:T(1,128)S(1)} all-to-all(f32[64,1,384]{2,1,0:T(1,128)S(1)} %bitcast.46), channel_id=1, replica_groups=mesh['sample'=8,'space'=64] {'space'}, dimensions={0} | all-to-all | bytes 196608 | tf_op jit(solution)/shard_map/all_to_all | solution.py:369
  108.2 0.7 solve_four.1
  108.9 14.5 %all_to_all.40 = f32[64,1,512]{2,1,0:T(1,128)S(1)} all-to-all(f32[64,1,512]{2,1,0:T(1,128)S(1)} %bitcast.41), channel_id=1, replica_groups=mesh['sample'=8,'space'=64] {'space'}, dimensions={0} | all-to-all | bytes 262144 | tf_op jit(solution)/shard_map/all_to_all | solution.py:369
  123.4 0.7 gradient.1
  124.1 25.2 %all_to_all.41 = f32[8,144,128]{2,1,0:T(8,128)S(1)} all-to-all(f32[8,144,128]{2,1,0:T(8,128)S(1)} %gradient.1), channel_id=1, replica_groups=mesh['sample'=8,'space'=64] {'sample'}, dimensions={0} | all-to-all | bytes 1179648 | tf_op jit(solution)/shard_map/all_to_all | solution.py:458
  149.3 0.7 reduce_sum.9
  (45 shorter events, 1.4 us)
Async XLA Ops:
  0.6 0.9 copy-start.6
  0.6 1.0 copy-start.2
  1.7 15.0 %collective-permute-start = (f32[9,48,128]{2,1,0:T(8,128)S(1)}, f32[9,48,128]{2,1,0:T(8,128)S(1)}, u32[]{:S(2)}, u32[]{:S(2)}) collective-permute-start(f32[9,48,128]{2,1,0:T(8,128)S(1)} %pad_maximum_fusion), channel_id=1, source_target_pairs={{0,1},{1,2},{2,3},{3,4},{4,5},{5,6},{6,7},{7,8},{8,9},{9,10},{10,1... | collective-permute-start | bytes 663560 | tf_op jit(solution)/shard_map/ppermute | solution.py:411
  6.3 10.4 %collective-permute-start.1 = (f32[9,48,128]{2,1,0:T(8,128)S(1)}, f32[9,48,128]{2,1,0:T(8,128)S(1)}, u32[]{:S(2)}, u32[]{:S(2)}) collective-permute-start(f32[9,48,128]{2,1,0:T(8,128)S(1)} %pad_maximum_fusion.1), channel_id=1, source_target_pairs={{1,0},{2,1},{3,2},{4,3},{5,4},{6,5},{7,6},{8,7},{9,8},{10,9},{11,1... | collective-permute-start | bytes 663560 | tf_op jit(solution)/shard_map/ppermute | solution.py:412
  12.5 0.7 copy-start.11
  13.1 0.7 copy-start.17
  14.4 0.7 copy-start.12
  15.8 0.7 copy-start.13
  15.8 0.7 copy-start.14
  15.8 0.7 copy-start.15
  16.5 0.7 copy-start.16
  16.5 0.9 copy-start.4
  16.6 0.7 copy-start.8
  16.6 0.7 copy-start.10
  17.4 22.1 %copy-start = (bf16[3,256,192]{2,1,0:T(8,128)(2,1)S(1)}, bf16[3,256,192]{2,1,0:T(8,128)(2,1)}, u32[]{:S(2)}) copy-start(bf16[3,256,192]{2,1,0:T(8,128)(2,1)} %constant.76.clone.from_x) | copy-start | bytes 884740
  18.7 20.8 %copy-start.1 = (bf16[2,192,192]{2,1,0:T(8,128)(2,1)S(1)}, bf16[2,192,192]{2,1,0:T(8,128)(2,1)}, u32[]{:S(2)}) copy-start(bf16[2,192,192]{2,1,0:T(8,128)(2,1)} %constant.75.clone.to_x) | copy-start | bytes 442372
  40.2 14.7 %copy-start.3 = (bf16[3,128,128]{2,1,0:T(8,128)(2,1)S(1)}, bf16[3,128,128]{2,1,0:T(8,128)(2,1)}, u32[]{:S(2)}) copy-start(bf16[3,128,128]{2,1,0:T(8,128)(2,1)} %constant.78.clone.from_y) | copy-start | bytes 294916
  40.2 14.7 %copy-start.5 = (f32[3,48,128]{2,1,0:T(8,128)S(1)}, f32[3,48,128]{2,1,0:T(8,128)}, u32[]{:S(2)}) copy-start(f32[3,48,128]{2,1,0:T(8,128)} %observed.3) | copy-start | bytes 221188
  40.2 14.7 %copy-start.7 = (bf16[3,48,48]{2,1,0:T(8,128)(2,1)S(1)}, bf16[3,48,48]{2,1,0:T(8,128)(2,1)}, u32[]{:S(2)}) copy-start(bf16[3,48,48]{2,1,0:T(8,128)(2,1)} %constant.80.clone.from_z) | copy-start | bytes 41476
  56.2 15.8 %copy-start.9 = (f32[192,128]{1,0:T(8,128)S(1)}, f32[192,128]{1,0:T(8,128)}, u32[]{:S(2)}) copy-start(f32[192,128]{1,0:T(8,128)} %constant.81.clone.sine_in) | copy-start | bytes 294916

commit v3 on v2

--- a/solution.py
+++ b/solution.py
@@ -69,6 +69,9 @@
 FROM_Z = in_parts(BASIS_Z, 3)
 FROM_X = in_parts(BASIS_X[stream_rows(0, 4)], 3)
 SINE_X = np.broadcast_to(sine_of(NX)[:, None], (NX, NY)).astype(np.float32)
+SQUARES = (sine_of(NX)[:, None] ** 2 + sine_of(NY)[None, :] ** 2).astype(np.float32)
+SQUARES_Z = np.zeros((1, SPACE), np.float32)
+SQUARES_Z[0, :NZ] = sine_of(NZ) ** 2
 
 
 def split(value, count):
@@ -173,13 +176,46 @@
     return jnp.concatenate([sine[:half] * modes[half:], -sine[half:] * modes[:half]], axis=0)
 
 
+def count_rotors(cells):
+    stream = cells[0:1, :]
+    span = cells[1:2, :]
+    base = cells[2:3, :]
+    turbines = cells.shape[1]
+    spans = lax.broadcasted_iota(jnp.int32, (NY, turbines), 0)
+    in_span = ((spans >= span) & (spans < span + ROTOR)).astype(F32).astype(BF16)
+    heights = lax.broadcasted_iota(jnp.int32, (NZ, turbines), 0)
+    in_height = (heights >= base) & (heights < base + ROTOR)
+    first = lax.axis_index("space") * SLAB
+    sheets = []
+    for j in range(-1, 4):
+        here = stream == lax.rem(first + (j + NX), NX)
+        sheets.append((in_height & here).astype(F32).astype(BF16))
+    counted = lax.dot_general(
+        jnp.concatenate(sheets, axis=0), in_span, (((1,), (1,)), ((), ())),
+        preferred_element_type=F32,
+    )
+    return [counted[NZ * i : NZ * (i + 1)] for i in range(5)]
+
+
+def spread_profile(row):
+    cells = lax.broadcasted_iota(jnp.int32, (NZ, NZ), 0)
+    others = lax.broadcasted_iota(jnp.int32, (NZ, NZ), 1)
+    column = jnp.sum(jnp.where(cells == others, row, 0.0), axis=1, keepdims=True)
+    return jnp.broadcast_to(column, (NZ, NY))
+
+
 def start_kernel(
-    seeds, own, low, high, correction, rotor, column, green, to_z, to_y,
-    buffer, first_trial, source_out, initial_out, laplace_out, viscosity_out,
+    seeds, own, low, high, correction, cells, heights, to_z, to_y,
+    buffer, first_trial, source_out, initial_out, laplace_out, viscosity_out, rotor_out,
+    column_out,
 ):
     span_shift = seeds[0, 0]
     height_shift = seeds[0, 1]
-    profile = column[...]
+    profile = spread_profile(heights[...])
+    column_out[...] = profile
+    rotor = count_rotors(cells)
+    for j in range(5):
+        rotor_out[j] = rotor[j]
     viscosity = {}
     for j in range(-2, 5):
         if j < 0:
@@ -212,8 +248,11 @@
             )
             moved[j] = state[j] + TIME_STEP * forcing
             first_trial[5 * c + j + 1] = moved[j]
+            if c == 0:
+                initial_out[j + 1] = state[j]
+            elif 0 <= j < 3:
+                initial_out[3 * c + 2 + j] = state[j]
             if 0 <= j < 3:
-                initial_out[3 * c + j] = state[j]
                 laplace_out[3 * c + j] = curvature
         trial.append(moved)
     sources = [
@@ -224,44 +263,66 @@
     to_modes(sources, to_z, to_y, buffer)
 
 
+def green_table(squares, squares_z):
+    place = lax.broadcasted_iota(jnp.int32, (1, SPACE), 1)
+    mine = jnp.where(place == lax.axis_index("space"), squares_z[...], 0.0)
+    summed = squares[...] + jnp.sum(mine, axis=1, keepdims=True)
+    null_mode = summed == 0.0
+    return jnp.where(null_mode, 0.0, -1.0 / jnp.where(null_mode, 1.0, summed))
+
+
+def solve_rows(modes_in, green, to_x, from_x, out):
+    spectrum = left_product(to_x, gather_slots(modes_in, 0, 3, 3)) * green
+    scatter_slots(out, left_product(from_x, spectrum), 0, 4, 4)
+
+
+def solve_first_kernel(modes_in, squares, squares_z, to_x, from_x, out, green_out):
+    green = green_table(squares, squares_z)
+    green_out[...] = green
+    solve_rows(modes_in, green, to_x, from_x, out)
+
+
 def solve_kernel(modes_in, green, to_x, from_x, out):
-    spectrum = left_product(to_x, gather_slots(modes_in, 0, 3, 3)) * green[...]
-    scatter_slots(out, left_product(from_x, spectrum), 0, 4, 4)
+    solve_rows(modes_in, green[...], to_x, from_x, out)
 
 
 def middle_kernel(
-    modes_in, first_trial, source, initial, viscosity, rotor, observed, low, high, column,
+    modes_in, first_trial, source, initial, viscosity, rotor, observed, column,
     from_z, from_y, to_z, to_y,
     buffer, second_trial, source_out, laplace_out,
 ):
     profile = column[...]
     pressure = with_plane_below(from_modes(modes_in, 4, from_z, from_y), source[...])
-    seen = {j: observed[j] for j in range(3)}
-    seen[-1] = low[8]
-    seen[3] = high[8]
     span = {j: first_trial[6 + j] - along_span(pressure[j]) for j in range(-1, 4)}
     height = {j: first_trial[11 + j] - along_height(pressure[j]) for j in range(-1, 4)}
     stream = {j: first_trial[1 + j] - along_stream(pressure, j) for j in range(3)}
-    stream[-1] = stream[1] + 2.0 * (along_span(span[0]) + along_height(height[0]))
-    stream[3] = stream[1] - 2.0 * (along_span(span[2]) + along_height(height[2]))
+    cross = {j: along_span(span[j]) + along_height(height[j]) for j in range(-1, 4)}
+    stream[-1] = stream[1] + 2.0 * cross[0]
+    stream[3] = stream[1] - 2.0 * cross[2]
+    stream[-2] = stream[0] + 2.0 * cross[-1]
+    stream[4] = stream[2] - 2.0 * cross[3]
     trial = []
     for c, middle in enumerate((stream, span, height)):
         moved = {}
-        for j in range(3):
+        for j in range(-1, 4) if c == 0 else range(3):
+            start = initial[j + 1] if c == 0 else initial[3 * c + 2 + j]
             curvature = laplace(middle, j)
-            laplace_out[3 * c + j] = curvature
             forcing = (
                 viscosity[j + 2] * curvature
                 - profile * along_stream(middle, j)
                 - THRUST * rotor[j + 1] * middle[j]
             )
-            moved[j] = 0.5 * initial[3 * c + j] + 0.5 * (middle[j] + TIME_STEP * forcing)
-            second_trial[3 * c + j] = moved[j]
+            moved[j] = 0.5 * start + 0.5 * (middle[j] + TIME_STEP * forcing)
+            if 0 <= j < 3:
+                laplace_out[3 * c + j] = curvature
+                second_trial[3 * c + j] = moved[j]
         trial.append(moved)
-    cross = [along_span(trial[1][j]) + along_height(trial[2][j]) for j in range(3)]
-    source_out[...] = along_stream(trial[0], 1) + cross[1]
-    sheets = [trial[0][j] - seen[j] for j in range(3)]
-    sheets += [cross[j] + along_stream(seen, j) for j in range(3)]
+    sources = [
+        along_stream(trial[0], j) + along_span(trial[1][j]) + along_height(trial[2][j])
+        for j in range(3)
+    ]
+    source_out[...] = sources[1]
+    sheets = [trial[0][j] - observed[j] for j in range(3)] + sources
     to_modes(sheets, to_z, to_y, buffer)
 
 
@@ -273,7 +334,7 @@
     )
     both = left_product(to_x, both)
     lead = both[:, :NY]
-    second = inverse * (swap_waves(lead, sine) + both[:, NY:])
+    second = inverse * both[:, NY:]
     third = inverse * swap_waves(lead - swap_waves(second, sine), sine)
     wide = left_product(from_x, jnp.concatenate([second, third], axis=1))
     scatter_slots(out, wide[:, :NY], 0, 4, 8)
@@ -349,7 +410,6 @@
     specs = [pl.BlockSpec(memory_space=pltpu.VMEM) for _ in args]
     if name == "start":
         specs[0] = pl.BlockSpec(memory_space=pltpu.SMEM)
-        specs[7] = pl.BlockSpec(memory_space=pl.ANY)
     shapes = [jax.ShapeDtypeStruct(shape, F32) for shape in outs]
     spaces = [pl.BlockSpec(memory_space=pltpu.VMEM) for _ in outs]
     single = len(outs) == 1
@@ -369,69 +429,38 @@
     return lax.all_to_all(wide, axis, 0, 0, tiled=True).reshape(rows.shape)
 
 
-def rotor_field(rotor_cells, stream_cells):
-    rotor_stream = rotor_cells[:, 0:1]
-    rotor_span = rotor_cells[:, 1:2]
-    rotor_base = rotor_cells[:, 2:3]
-    heights = jnp.arange(NZ, dtype=jnp.int32)[None, :]
-    spans = jnp.arange(NY, dtype=jnp.int32)[None, :]
-    in_stream = (stream_cells[None, :] == rotor_stream).astype(F32)
-    in_height = ((heights >= rotor_base) & (heights < rotor_base + ROTOR)).astype(F32)
-    in_span = ((spans >= rotor_span) & (spans < rotor_span + ROTOR)).astype(F32)
-    sheet = (in_stream[:, :, None] * in_height[:, None, :]).reshape(in_stream.shape[0], -1)
-    counted = jnp.dot(sheet.T, in_span, preferred_element_type=F32)
-    return counted.reshape(stream_cells.shape[0], NZ, NY)
-
-
-def green_table(position):
-    square_x = jnp.asarray((sine_of(NX) ** 2).astype(np.float32))[:, None]
-    square_y = jnp.asarray((sine_of(NY) ** 2).astype(np.float32))[None, :]
-    square_z = jnp.asarray((sine_of(NZ) ** 2).astype(np.float32))
-    height = jnp.minimum(position, NZ - 1)
-    summed = square_x + lax.dynamic_index_in_dim(square_z, height, keepdims=False) + square_y
-    null_x = jnp.asarray(np.arange(NX) % (NX // 2) == 0)[:, None]
-    null_y = jnp.asarray(np.arange(NY) % (NY // 2) == 0)[None, :]
-    null_mode = null_x & null_y & (height % (NZ // 2) == 0)
-    table = jnp.where(null_mode, 0.0, -1.0 / jnp.where(null_mode, 1.0, summed))
-    return jnp.where(position < NZ, table, 0.0)
-
-
 def shards(inflow_seeds, rotor_cells, fluctuation, profile, correction, observed):
-    position = lax.axis_index("space")
     samples = lax.axis_size("sample")
     forward = [(i, (i + 1) % SPACE) for i in range(SPACE)]
     backward = [(target, source) for source, target in forward]
     plane = (NZ, NY)
-    last = jnp.concatenate(
-        [fluctuation[:, 1:].reshape(6, NZ, NY), correction[1:], observed[2:]], axis=0
-    )
-    first = jnp.concatenate(
-        [fluctuation[:, :2].reshape(6, NZ, NY), correction[:2], observed[:1]], axis=0
-    )
+    last = jnp.concatenate([fluctuation[:, 1:].reshape(6, NZ, NY), correction[1:]], axis=0)
+    first = jnp.concatenate([fluctuation[:, :2].reshape(6, NZ, NY), correction[:2]], axis=0)
     low = lax.ppermute(last, "space", forward)
     high = lax.ppermute(first, "space", backward)
-    cells = (position * SLAB + jnp.arange(-1, SLAB + 1, dtype=jnp.int32)) % NX
-    rotor = rotor_field(rotor_cells, cells)
-    column = jnp.broadcast_to(profile[:, None], plane)
-    green = green_table(position)
     to_x, from_x = jnp.asarray(TO_X), jnp.asarray(FROM_X)
     to_y, from_y = jnp.asarray(TO_Y), jnp.asarray(FROM_Y)
     to_z, from_z = jnp.asarray(TO_Z), jnp.asarray(FROM_Z)
 
-    buffer, first_trial, source, initial, laplace_start, viscosity = local_call(
+    buffer, first_trial, source, initial, laplace_start, viscosity, rotor, column = local_call(
         start_kernel, "start",
-        [(SPACE * 3, NY), (15, *plane), plane, (9, *plane), (9, *plane), (7, *plane)],
-        inflow_seeds, fluctuation, low, high, correction, rotor, column, green, to_z, to_y,
+        [
+            (SPACE * 3, NY), (15, *plane), plane, (11, *plane), (9, *plane), (7, *plane),
+            (5, *plane), plane,
+        ],
+        inflow_seeds, fluctuation, low, high, correction, rotor_cells.T, profile[None, :],
+        to_z, to_y,
     )
     buffer = exchange(buffer)
-    buffer = local_call(
-        solve_kernel, "solve_one", [(SPACE * 4, NY)], buffer, green, to_x, from_x
+    buffer, green = local_call(
+        solve_first_kernel, "solve_one", [(SPACE * 4, NY), (NX, NY)],
+        buffer, jnp.asarray(SQUARES), jnp.asarray(SQUARES_Z), to_x, from_x,
     )
     buffer = exchange(buffer)
     buffer, second_trial, source, laplace_mid = local_call(
         middle_kernel, "middle",
         [(SPACE * 6, NY), (9, *plane), plane, (9, *plane)],
-        buffer, first_trial, source, initial, viscosity, rotor, observed, low, high, column,
+        buffer, first_trial, source, initial, viscosity, rotor, observed, column,
         from_z, from_y, to_z, to_y,
     )
     buffer = exchange(buffer)

time: 151 us -> 152 us (level)
  blocking collectives: 124 us -> 127 us
    all_to_all x6, blocking collectives: 99.2 us -> 103 us  [exchange(): return lax.all_to_all(wide, axis, 0, 0, tiled=True).reshape(rows.shape)]
    unnamed x36 -> x30, local copies, waits for them, and re-layouts: 3.28 us -> 1.35 us
  transfers between devices with their start and end apart: 2 -> 2, of which waited for: 0 -> 1; matrix products, arithmetic and copies ran while one was open for 1% -> 0% of each run, Pallas kernels for 0% -> 0%
where the time goes in v3:
time: 152 us; the launch traced here: 151 us
  blocking collectives  127 us (84%)
  starting transfers between devices  11 us (7%)
  Pallas kernels  7.58 us (5%)
  local copies, waits for them, and re-layouts  3.24 us (2%)
    all_to_all x6, blocking collectives, exchange(): return lax.all_to_all(wide, axis, 0, 0, tiled=True).reshape(rows.shape)  103 us
    all_to_all x1, blocking collectives, shards(): terms = lax.all_to_all(terms, 'sample', 0, 0, tiled=True)  24.2 us
    pallas_call x7, Pallas kernels, local_call(): pl.pallas_call(kernel, out_shape=shapes[0] if single else shapes, in_spec...  7.58 us
    ppermute x1, starting transfers between devices, shards(): high = lax.ppermute(first, 'space', backward)  6.24 us
    ppermute x1, starting transfers between devices, shards(): low = lax.ppermute(last, 'space', forward)  4.73 us
  transfers between devices with their start and end apart: 2, of which 1 were waited for; matrix products, arithmetic and copies ran while one was open for 0% of the time, Pallas kernels for 0%

profile of v3, /device:TPU:1, one launch (start us, length us, event | category | flops | bytes accessed | tf_op | source)
XLA Modules:
  0.0 151.3 jit_solution(11273607208370723165)
XLA Ops:
  0.6 0.9 fusion.1
  1.5 1.0 fusion
  2.6 4.7 %collective-permute-start = (f32[8,48,128]{2,1,0:T(8,128)S(1)}, f32[8,48,128]{2,1,0:T(8,128)S(1)}, u32[]{:S(2)}, u32[]{:S(2)}) collective-permute-start(f32[8,48,128]{2,1,0:T(8,128)S(1)} %pad_maximum_fusion), channel_id=1, source_target_pairs={{0,1},{1,2},{2,3},{3,4},{4,5},{5,6},{6,7},{7,8},{8,9},{9,10},{10,1... | collective-permute-start | bytes 589832 | tf_op jit(solution)/shard_map/ppermute | solution.py:439
  7.3 0.0 copy-start.4
  7.4 6.2 %collective-permute-start.1 = (f32[8,48,128]{2,1,0:T(8,128)S(1)}, f32[8,48,128]{2,1,0:T(8,128)S(1)}, u32[]{:S(2)}, u32[]{:S(2)}) collective-permute-start(f32[8,48,128]{2,1,0:T(8,128)S(1)} %pad_maximum_fusion.1), channel_id=1, source_target_pairs={{1,0},{2,1},{3,2},{4,3},{5,4},{6,5},{7,6},{8,7},{9,8},{10,9},{11,1... | collective-permute-start | bytes 589832 | tf_op jit(solution)/shard_map/ppermute | solution.py:440
  13.6 1.0 collective-permute-done.1.high
  14.7 0.6 copy-done.12
  15.3 0.0 copy-done.13
  15.3 1.4 start.1
  16.7 24.3 %all_to_all.35 = f32[64,1,384]{2,1,0:T(1,128)S(1)} all-to-all(f32[64,1,384]{2,1,0:T(1,128)S(1)} %bitcast.28), channel_id=1, replica_groups=mesh['sample'=8,'space'=64] {'space'}, dimensions={0} | all-to-all | bytes 196608 | tf_op jit(solution)/shard_map/all_to_all | solution.py:429
  41.1 0.6 copy-done.14
  41.8 0.7 solve_one.1
  42.5 14.7 %all_to_all.36 = f32[64,1,512]{2,1,0:T(1,128)S(1)} all-to-all(f32[64,1,512]{2,1,0:T(1,128)S(1)} %bitcast.26), channel_id=1, replica_groups=mesh['sample'=8,'space'=64] {'space'}, dimensions={0} | all-to-all | bytes 262144 | tf_op jit(solution)/shard_map/all_to_all | solution.py:429
  57.1 1.3 middle.1
  58.5 15.7 %all_to_all.37 = f32[64,1,768]{2,1,0:T(1,128)S(1)} all-to-all(f32[64,1,768]{2,1,0:T(1,128)S(1)} %bitcast.25), channel_id=1, replica_groups=mesh['sample'=8,'space'=64] {'space'}, dimensions={0} | all-to-all | bytes 393216 | tf_op jit(solution)/shard_map/all_to_all | solution.py:429
  74.3 0.7 solve_two.1
  75.0 17.5 %all_to_all.38 = f32[64,1,1024]{2,1,0:T(1,128)S(1)} all-to-all(f32[64,1,1024]{2,1,0:T(1,128)S(1)} %bitcast.17), channel_id=1, replica_groups=mesh['sample'=8,'space'=64] {'space'}, dimensions={0} | all-to-all | bytes 524288 | tf_op jit(solution)/shard_map/all_to_all | solution.py:429
  92.5 2.0 %adjoint.1 = (f32[192,128]{1,0:T(8,128)S(1)}, f32[9,48,128]{2,1,0:T(8,128)S(1)}, f32[48,128]{1,0:T(8,128)S(1)}, f32[1,3,3,48,128]{4,3,2,1,0:T(8,128)}, f32[3,48,128]{2,1,0:T(8,128)S(1)}) custom-call(f32[512,128]{1,0:T(8,128)S(1)} %bitcast.18, f32[9,48,128]{2,1,0:T(8,128)S(1)} %get-tuple-element.31.second_trial, f32[48,128]{1,0:T(8,128)S(1)} %get-tuple-element.32.source, ...), custom_call_target="tpu_custom_call" | custom-call | tf_op jit(solution)/shard_map/adjoint/pallas_call | solution.py:416
  94.5 16.0 %all_to_all.39 = f32[64,1,384]{2,1,0:T(1,128)S(1)} all-to-all(f32[64,1,384]{2,1,0:T(1,128)S(1)} %bitcast.27), channel_id=1, replica_groups=mesh['sample'=8,'space'=64] {'space'}, dimensions={0} | all-to-all | bytes 196608 | tf_op jit(solution)/shard_map/all_to_all | solution.py:429
  110.5 0.7 solve_four.1
  111.2 14.5 %all_to_all.40 = f32[64,1,512]{2,1,0:T(1,128)S(1)} all-to-all(f32[64,1,512]{2,1,0:T(1,128)S(1)} %bitcast.21), channel_id=1, replica_groups=mesh['sample'=8,'space'=64] {'space'}, dimensions={0} | all-to-all | bytes 262144 | tf_op jit(solution)/shard_map/all_to_all | solution.py:429
  125.7 0.7 gradient.1
  126.4 24.2 %all_to_all.41 = f32[8,144,128]{2,1,0:T(8,128)S(1)} all-to-all(f32[8,144,128]{2,1,0:T(8,128)S(1)} %gradient.1), channel_id=1, replica_groups=mesh['sample'=8,'space'=64] {'sample'}, dimensions={0} | all-to-all | bytes 1179648 | tf_op jit(solution)/shard_map/all_to_all | solution.py:487
  150.7 0.7 reduce_sum.9
  (29 shorter events, 0.1 us)
Async XLA Ops:
  2.5 12.1 %copy-start.2 = (f32[3,3,48,128]{3,2,1,0:T(8,128)S(1)}, f32[3,3,48,128]{3,2,1,0:T(8,128)}, u32[]{:S(2)}) copy-start(f32[3,3,48,128]{3,2,1,0:T(8,128)} %own.1) | copy-start | bytes 663556
  2.6 11.1 %collective-permute-start = (f32[8,48,128]{2,1,0:T(8,128)S(1)}, f32[8,48,128]{2,1,0:T(8,128)S(1)}, u32[]{:S(2)}, u32[]{:S(2)}) collective-permute-start(f32[8,48,128]{2,1,0:T(8,128)S(1)} %pad_maximum_fusion), channel_id=1, source_target_pairs={{0,1},{1,2},{2,3},{3,4},{4,5},{5,6},{6,7},{7,8},{8,9},{9,10},{10,1... | collective-permute-start | bytes 589832 | tf_op jit(solution)/shard_map/ppermute | solution.py:439
  7.3 7.4 %copy-start.4 = (bf16[2,128,128]{2,1,0:T(8,128)(2,1)S(1)}, bf16[2,128,128]{2,1,0:T(8,128)(2,1)}, u32[]{:S(2)}) copy-start(bf16[2,128,128]{2,1,0:T(8,128)(2,1)} %constant.22.clone.to_y) | copy-start | bytes 196612
  7.3 7.4 %copy-start.5 = (f32[3,48,128]{2,1,0:T(8,128)S(1)}, f32[3,48,128]{2,1,0:T(8,128)}, u32[]{:S(2)}) copy-start(f32[3,48,128]{2,1,0:T(8,128)} %correction.1) | copy-start | bytes 221188
  7.3 7.4 %copy-start.8 = (bf16[2,48,48]{2,1,0:T(8,128)(2,1)S(1)}, bf16[2,48,48]{2,1,0:T(8,128)(2,1)}, u32[]{:S(2)}) copy-start(bf16[2,48,48]{2,1,0:T(8,128)(2,1)} %constant.24.clone.to_z) | copy-start | bytes 27652
  7.4 7.3 %copy-start.11 = (s32[64,3]{0,1:T(4,128)S(1)}, s32[64,3]{0,1:T(4,128)}, u32[]{:S(2)}) copy-start(s32[64,3]{0,1:T(4,128)} %param.16) | copy-start | bytes 2308
  7.4 7.3 %collective-permute-start.1 = (f32[8,48,128]{2,1,0:T(8,128)S(1)}, f32[8,48,128]{2,1,0:T(8,128)S(1)}, u32[]{:S(2)}, u32[]{:S(2)}) collective-permute-start(f32[8,48,128]{2,1,0:T(8,128)S(1)} %pad_maximum_fusion.1), channel_id=1, source_target_pairs={{1,0},{2,1},{3,2},{4,3},{5,4},{6,5},{7,6},{8,7},{9,8},{10,9},{11,1... | collective-permute-start | bytes 589832 | tf_op jit(solution)/shard_map/ppermute | solution.py:440
  14.7 0.7 copy-start.12
  14.7 0.7 copy-start.13
  15.3 25.8 %copy-start = (bf16[3,256,192]{2,1,0:T(8,128)(2,1)S(1)}, bf16[3,256,192]{2,1,0:T(8,128)(2,1)}, u32[]{:S(2)}) copy-start(bf16[3,256,192]{2,1,0:T(8,128)(2,1)} %constant.21.clone.from_x) | copy-start | bytes 884740
  15.3 25.8 %copy-start.10 = (f32[192,128]{1,0:T(8,128)S(1)}, f32[192,128]{1,0:T(8,128)}, u32[]{:S(2)}) copy-start(f32[192,128]{1,0:T(8,128)} %constant.26.clone.squares) | copy-start | bytes 294916
  16.7 24.4 %copy-start.1 = (bf16[2,192,192]{2,1,0:T(8,128)(2,1)S(1)}, bf16[2,192,192]{2,1,0:T(8,128)(2,1)}, u32[]{:S(2)}) copy-start(bf16[2,192,192]{2,1,0:T(8,128)(2,1)} %constant.20.clone.to_x) | copy-start | bytes 442372
  41.1 0.7 copy-start.14
  42.4 14.7 %copy-start.3 = (bf16[3,128,128]{2,1,0:T(8,128)(2,1)S(1)}, bf16[3,128,128]{2,1,0:T(8,128)(2,1)}, u32[]{:S(2)}) copy-start(bf16[3,128,128]{2,1,0:T(8,128)(2,1)} %constant.23.clone.from_y) | copy-start | bytes 294916
  42.5 14.7 %copy-start.6 = (bf16[3,48,48]{2,1,0:T(8,128)(2,1)S(1)}, bf16[3,48,48]{2,1,0:T(8,128)(2,1)}, u32[]{:S(2)}) copy-start(bf16[3,48,48]{2,1,0:T(8,128)(2,1)} %constant.25.clone.from_z) | copy-start | bytes 41476
  42.5 14.7 %copy-start.7 = (f32[3,48,128]{2,1,0:T(8,128)S(1)}, f32[3,48,128]{2,1,0:T(8,128)}, u32[]{:S(2)}) copy-start(f32[3,48,128]{2,1,0:T(8,128)} %observed.3) | copy-start | bytes 221188
  58.5 15.8 %copy-start.9 = (f32[192,128]{1,0:T(8,128)S(1)}, f32[192,128]{1,0:T(8,128)}, u32[]{:S(2)}) copy-start(f32[192,128]{1,0:T(8,128)} %constant.28.clone.sine_in) | copy-start | bytes 294916

commit v4 on v3

--- a/solution.py
+++ b/solution.py
@@ -69,9 +69,9 @@
 FROM_Z = in_parts(BASIS_Z, 3)
 FROM_X = in_parts(BASIS_X[stream_rows(0, 4)], 3)
 SINE_X = np.broadcast_to(sine_of(NX)[:, None], (NX, NY)).astype(np.float32)
-SQUARES = (sine_of(NX)[:, None] ** 2 + sine_of(NY)[None, :] ** 2).astype(np.float32)
-SQUARES_Z = np.zeros((1, SPACE), np.float32)
-SQUARES_Z[0, :NZ] = sine_of(NZ) ** 2
+SQUARES = np.zeros((NX + 8, NY), np.float32)
+SQUARES[:NX] = sine_of(NX)[:, None] ** 2 + sine_of(NY)[None, :] ** 2
+SQUARES[NX, :NZ] = sine_of(NZ) ** 2
 
 
 def split(value, count):
@@ -204,40 +204,84 @@
     return jnp.broadcast_to(column, (NZ, NY))
 
 
-def start_kernel(
-    seeds, own, low, high, correction, cells, heights, to_z, to_y,
-    buffer, first_trial, source_out, initial_out, laplace_out, viscosity_out, rotor_out,
-    column_out,
+def pack_kernel(own, correction, inner, outer, arrived):
+    even = lax.rem(lax.axis_index("space"), 2) == 0
+
+    def fill(first, last):
+        copies = []
+        for i, (target, start) in enumerate(((last, 1), (first, 0))):
+            planes = pl.ds(start, 2)
+            copies.append(
+                pltpu.make_async_copy(own.at[:, planes], target.at[0:3], arrived.at[2 * i])
+            )
+            copies.append(
+                pltpu.make_async_copy(
+                    correction.at[planes], target.at[3], arrived.at[2 * i + 1]
+                )
+            )
+        for copy in copies:
+            copy.start()
+        for copy in copies:
+            copy.wait()
+
+    @pl.when(even)
+    def _():
+        fill(outer, inner)
+
+    @pl.when(jnp.logical_not(even))
+    def _():
+        fill(inner, outer)
+
+
+def rolled(plane, seeds):
+    return pltpu.roll(pltpu.roll(plane, seeds[0, 0], 1), seeds[0, 1], 0)
+
+
+def prepare_kernel(
+    seeds, own, correction, cells, heights, state_out, viscosity_out, rotor_out, column_out
 ):
-    span_shift = seeds[0, 0]
-    height_shift = seeds[0, 1]
     profile = spread_profile(heights[...])
     column_out[...] = profile
     rotor = count_rotors(cells)
     for j in range(5):
         rotor_out[j] = rotor[j]
+    for j in range(3):
+        viscosity_out[j] = BASE_VISCOSITY * jnp.exp(correction[j])
+        for c in range(3):
+            plane = rolled(own[c, j], seeds)
+            state_out[3 * c + j] = plane + profile if c == 0 else plane
+
+
+def start_kernel(
+    seeds, inner, outer, own_state, own_viscosity, rotor, column, to_z, to_y,
+    buffer, first_trial, source_out, beside_out, laplace_out, viscosity_out,
+):
+    even = lax.rem(lax.axis_index("space"), 2) == 0
+    profile = column[...]
+
+    def halo(j, c):
+        i = j + 2 if j < 0 else j - 3
+        low = outer if j < 0 else inner
+        high = inner if j < 0 else outer
+        return jnp.where(even, low[c, i], high[c, i])
+
     viscosity = {}
     for j in range(-2, 5):
-        if j < 0:
-            raw = low[8 + j]
-        elif j < 3:
-            raw = correction[j]
+        if 0 <= j < 3:
+            viscosity[j] = own_viscosity[j]
         else:
-            raw = high[3 + j]
-        viscosity[j] = BASE_VISCOSITY * jnp.exp(raw)
+            viscosity[j] = BASE_VISCOSITY * jnp.exp(halo(j, 3))
         viscosity_out[j + 2] = viscosity[j]
     trial = []
     for c in range(3):
         state = {}
         for j in range(-2, 5):
-            if j < 0:
-                raw = low[2 * c + j + 2]
-            elif j < 3:
-                raw = own[c, j]
+            if 0 <= j < 3:
+                state[j] = own_state[3 * c + j]
             else:
-                raw = high[2 * c + j - 3]
-            raw = pltpu.roll(pltpu.roll(raw, span_shift, 1), height_shift, 0)
-            state[j] = raw + profile if c == 0 else raw
+                state[j] = rolled(halo(j, c), seeds)
+                if c == 0:
+                    state[j] = state[j] + profile
         moved = {}
         for j in range(-1, 4):
             curvature = laplace(state, j)
@@ -248,13 +292,12 @@
             )
             moved[j] = state[j] + TIME_STEP * forcing
             first_trial[5 * c + j + 1] = moved[j]
-            if c == 0:
-                initial_out[j + 1] = state[j]
-            elif 0 <= j < 3:
-                initial_out[3 * c + 2 + j] = state[j]
             if 0 <= j < 3:
                 laplace_out[3 * c + j] = curvature
         trial.append(moved)
+        if c == 0:
+            beside_out[0] = state[-1]
+            beside_out[1] = state[3]
     sources = [
         along_stream(trial[0], j) + along_span(trial[1][j]) + along_height(trial[2][j])
         for j in range(3)
@@ -263,10 +306,10 @@
     to_modes(sources, to_z, to_y, buffer)
 
 
-def green_table(squares, squares_z):
-    place = lax.broadcasted_iota(jnp.int32, (1, SPACE), 1)
-    mine = jnp.where(place == lax.axis_index("space"), squares_z[...], 0.0)
-    summed = squares[...] + jnp.sum(mine, axis=1, keepdims=True)
+def green_table(squares):
+    place = lax.broadcasted_iota(jnp.int32, (1, NY), 1)
+    mine = jnp.where(place == lax.axis_index("space"), squares[NX : NX + 1, :], 0.0)
+    summed = squares[:NX, :] + jnp.sum(mine, axis=1, keepdims=True)
     null_mode = summed == 0.0
     return jnp.where(null_mode, 0.0, -1.0 / jnp.where(null_mode, 1.0, summed))
 
@@ -276,8 +319,8 @@
     scatter_slots(out, left_product(from_x, spectrum), 0, 4, 4)
 
 
-def solve_first_kernel(modes_in, squares, squares_z, to_x, from_x, out, green_out):
-    green = green_table(squares, squares_z)
+def solve_first_kernel(modes_in, squares, to_x, from_x, out, green_out):
+    green = green_table(squares)
     green_out[...] = green
     solve_rows(modes_in, green, to_x, from_x, out)
 
@@ -287,7 +330,7 @@
 
 
 def middle_kernel(
-    modes_in, first_trial, source, initial, viscosity, rotor, observed, column,
+    modes_in, first_trial, source, state, beside, viscosity, rotor, observed, column,
     from_z, from_y, to_z, to_y,
     buffer, second_trial, source_out, laplace_out,
 ):
@@ -305,7 +348,7 @@
     for c, middle in enumerate((stream, span, height)):
         moved = {}
         for j in range(-1, 4) if c == 0 else range(3):
-            start = initial[j + 1] if c == 0 else initial[3 * c + 2 + j]
+            start = state[3 * c + j] if 0 <= j < 3 else beside[0 if j < 0 else 1]
             curvature = laplace(middle, j)
             forcing = (
                 viscosity[j + 2] * curvature
@@ -406,19 +449,18 @@
             out[copy, NZ * j : NZ * (j + 1), :] = total
 
 
-def local_call(kernel, name, outs, *args):
-    specs = [pl.BlockSpec(memory_space=pltpu.VMEM) for _ in args]
-    if name == "start":
-        specs[0] = pl.BlockSpec(memory_space=pltpu.SMEM)
+def local_call(kernel, outs, *args, spaces={}, scratch=()):
+    specs = [pl.BlockSpec(memory_space=spaces.get(i, pltpu.VMEM)) for i in range(len(args))]
     shapes = [jax.ShapeDtypeStruct(shape, F32) for shape in outs]
-    spaces = [pl.BlockSpec(memory_space=pltpu.VMEM) for _ in outs]
+    out_specs = [pl.BlockSpec(memory_space=pltpu.VMEM) for _ in outs]
     single = len(outs) == 1
     return pl.pallas_call(
         kernel,
         out_shape=shapes[0] if single else shapes,
         in_specs=specs,
-        out_specs=spaces[0] if single else spaces,
-        name=name,
+        out_specs=out_specs[0] if single else out_specs,
+        scratch_shapes=scratch,
+        name=kernel.__name__,
         compiler_params=pltpu.CompilerParams(vmem_limit_bytes=24 * 1024 * 1024),
     )(*args)
 
@@ -431,57 +473,63 @@
 
 def shards(inflow_seeds, rotor_cells, fluctuation, profile, correction, observed):
     samples = lax.axis_size("sample")
-    forward = [(i, (i + 1) % SPACE) for i in range(SPACE)]
-    backward = [(target, source) for source, target in forward]
+    within = [(i, i + 1 - 2 * (i % 2)) for i in range(SPACE)]
+    between = [(i, (i - 1 + 2 * (i % 2)) % SPACE) for i in range(SPACE)]
     plane = (NZ, NY)
-    last = jnp.concatenate([fluctuation[:, 1:].reshape(6, NZ, NY), correction[1:]], axis=0)
-    first = jnp.concatenate([fluctuation[:, :2].reshape(6, NZ, NY), correction[:2]], axis=0)
-    low = lax.ppermute(last, "space", forward)
-    high = lax.ppermute(first, "space", backward)
+    inner, outer = local_call(
+        pack_kernel, [(4, 2, *plane), (4, 2, *plane)],
+        pltpu.with_memory_space_constraint(fluctuation, pltpu.HBM),
+        pltpu.with_memory_space_constraint(correction, pltpu.HBM),
+        spaces={0: pltpu.HBM, 1: pltpu.HBM}, scratch=[pltpu.SemaphoreType.DMA((4,))],
+    )
+    inner = lax.ppermute(inner, "space", within)
+    outer = lax.ppermute(outer, "space", between)
     to_x, from_x = jnp.asarray(TO_X), jnp.asarray(FROM_X)
     to_y, from_y = jnp.asarray(TO_Y), jnp.asarray(FROM_Y)
     to_z, from_z = jnp.asarray(TO_Z), jnp.asarray(FROM_Z)
 
-    buffer, first_trial, source, initial, laplace_start, viscosity, rotor, column = local_call(
-        start_kernel, "start",
-        [
-            (SPACE * 3, NY), (15, *plane), plane, (11, *plane), (9, *plane), (7, *plane),
-            (5, *plane), plane,
-        ],
-        inflow_seeds, fluctuation, low, high, correction, rotor_cells.T, profile[None, :],
-        to_z, to_y,
+    state, viscosity, rotor, column = local_call(
+        prepare_kernel, [(9, *plane), (3, *plane), (5, *plane), plane],
+        inflow_seeds, fluctuation, correction, rotor_cells.T, profile[None, :],
+        spaces={0: pltpu.SMEM},
+    )
+    buffer, first_trial, source, beside, laplace_start, viscosity = local_call(
+        start_kernel,
+        [(SPACE * 3, NY), (15, *plane), plane, (2, *plane), (9, *plane), (7, *plane)],
+        inflow_seeds, inner, outer, state, viscosity, rotor, column, to_z, to_y,
+        spaces={0: pltpu.SMEM},
     )
     buffer = exchange(buffer)
     buffer, green = local_call(
-        solve_first_kernel, "solve_one", [(SPACE * 4, NY), (NX, NY)],
-        buffer, jnp.asarray(SQUARES), jnp.asarray(SQUARES_Z), to_x, from_x,
+        solve_first_kernel, [(SPACE * 4, NY), (NX, NY)],
+        buffer, jnp.asarray(SQUARES), to_x, from_x,
     )
     buffer = exchange(buffer)
     buffer, second_trial, source, laplace_mid = local_call(
-        middle_kernel, "middle",
+        middle_kernel,
         [(SPACE * 6, NY), (9, *plane), plane, (9, *plane)],
-        buffer, first_trial, source, initial, viscosity, rotor, observed, column,
+        buffer, first_trial, source, state, beside, viscosity, rotor, observed, column,
         from_z, from_y, to_z, to_y,
     )
     buffer = exchange(buffer)
     buffer = local_call(
-        solve_both_kernel, "solve_two", [(SPACE * 8, NY)],
+        solve_both_kernel, [(SPACE * 8, NY)],
         buffer, green, jnp.asarray(SINE_X), to_x, from_x,
     )
     buffer = exchange(buffer)
     buffer, fourth_trial, source, velocity, share = local_call(
-        adjoint_kernel, "adjoint",
+        adjoint_kernel,
         [(SPACE * 3, NY), (9, *plane), plane, (1, 3, 3, *plane), (3, *plane)],
         buffer, second_trial, source, laplace_mid, viscosity, rotor, observed, column,
         from_z, from_y, to_z, to_y,
     )
     buffer = exchange(buffer)
     buffer = local_call(
-        solve_kernel, "solve_four", [(SPACE * 4, NY)], buffer, green, to_x, from_x
+        solve_kernel, [(SPACE * 4, NY)], buffer, green, to_x, from_x
     )
     buffer = exchange(buffer)
     terms = local_call(
-        gradient_kernel, "gradient", [(samples, SLAB * NZ, NY)],
+        gradient_kernel, [(samples, SLAB * NZ, NY)],
         buffer, fourth_trial, source, laplace_start, viscosity, share, from_z, from_y,
     )
     terms = lax.all_to_all(terms, "sample", 0, 0, tiled=True)

time: 152 us -> 149 us (0.980)
  blocking collectives: 127 us -> 123 us
  waiting for transfers between devices: 1.04 us -> 3.64 us
  local copies, waits for them, and re-layouts: 3.24 us -> 0.69 us
  Pallas kernels: 7.58 us -> 9.25 us
    all_to_all x6, blocking collectives: 103 us -> 95.4 us  [exchange(): return lax.all_to_all(wide, axis, 0, 0, tiled=True).reshape(rows.shape)]
    all_to_all x1, blocking collectives: 24.2 us -> 27.3 us  [shards(): terms = lax.all_to_all(terms, 'sample', 0, 0, tiled=True)]
    ppermute x2, waiting for transfers between devices: 1.04 us -> 3.64 us  [the longest x1 3.64 us: shards(): outer = lax.ppermute(outer, 'space', between)]
    slice x2 -> x0, local copies, waits for them, and re-layouts: 1.89 us -> none  [the longest x1 1.01 us: shards(): fluctuation[:, :2].reshape(6, NZ, NY)]
    pallas_call x7 -> x9, Pallas kernels: 7.58 us -> 9.25 us  [local_call(): pl.pallas_call(kernel, out_shape=shapes[0] if single else shapes, in_spec...]
where the time goes in v4:
time: 149 us; the launch traced here: 148 us
  blocking collectives  123 us (83%)
  starting transfers between devices  10.7 us (7%)
  Pallas kernels  9.25 us (6%)
  waiting for transfers between devices  3.64 us (2%)
    all_to_all x6, blocking collectives, exchange(): return lax.all_to_all(wide, axis, 0, 0, tiled=True).reshape(rows.shape)  95.4 us
    all_to_all x1, blocking collectives, shards(): terms = lax.all_to_all(terms, 'sample', 0, 0, tiled=True)  27.3 us
    pallas_call x9, Pallas kernels, local_call(): pl.pallas_call(kernel, out_shape=shapes[0] if single else shapes, in_spec...  9.25 us
    ppermute x1, starting transfers between devices, shards(): inner = lax.ppermute(inner, 'space', within)  8.77 us
    ppermute x1, waiting for transfers between devices, shards(): outer = lax.ppermute(outer, 'space', between)  3.64 us
  transfers between devices with their start and end apart: 2, of which 1 were waited for; matrix products, arithmetic and copies ran while one was open for 0% of the time, Pallas kernels for 0%

profile of v4, /device:TPU:1, one launch (start us, length us, event | category | flops | bytes accessed | tf_op | source)
XLA Modules:
  0.0 148.5 jit_solution(2246379090305665151)
XLA Ops:
  0.6 1.1 pack_kernel.1
  1.8 8.8 %collective-permute-start = (f32[4,2,48,128]{3,2,1,0:T(8,128)S(1)}, f32[4,2,48,128]{3,2,1,0:T(8,128)S(1)}, u32[]{:S(2)}, u32[]{:S(2)}) collective-permute-start(f32[4,2,48,128]{3,2,1,0:T(8,128)S(1)} %get-tuple-element.25), channel_id=1, source_target_pairs={{0,1},{1,0},{2,3},{3,2},{4,5},{5,4},{6,7},{7,6},{8,9},{9,8},{10,11... | collective-permute-start | bytes 589832 | tf_op jit(solution)/shard_map/ppermute | solution.py:485
  10.6 1.9 %collective-permute-start.1 = (f32[4,2,48,128]{3,2,1,0:T(8,128)S(1)}, f32[4,2,48,128]{3,2,1,0:T(8,128)S(1)}, u32[]{:S(2)}, u32[]{:S(2)}) collective-permute-start(f32[4,2,48,128]{3,2,1,0:T(8,128)S(1)} %get-tuple-element.26), channel_id=1, source_target_pairs={{0,63},{1,2},{2,1},{3,4},{4,3},{5,6},{6,5},{7,8},{8,7},{9,10},{10,... | collective-permute-start | bytes 589832 | tf_op jit(solution)/shard_map/ppermute | solution.py:486
  12.5 0.6 copy-done.12
  13.1 0.0 copy-done.13
  13.2 0.7 prepare_kernel.1
  13.9 3.6 %collective-permute-done.1.outer = f32[4,2,48,128]{3,2,1,0:T(8,128)S(1)} collective-permute-done((f32[4,2,48,128]{3,2,1,0:T(8,128)S(1)}, f32[4,2,48,128]{3,2,1,0:T(8,128)S(1)}, u32[]{:S(2)}, u32[]{:S(2)}) %collective-permute-start.1) | collective-permute-done | bytes 196640 | tf_op jit(solution)/shard_map/ppermute | solution.py:486
  17.6 1.2 start_kernel.1
  18.8 0.0 copy-start.1
  18.8 17.0 %all_to_all.35 = f32[64,1,384]{2,1,0:T(1,128)S(1)} all-to-all(f32[64,1,384]{2,1,0:T(1,128)S(1)} %bitcast.26), channel_id=1, replica_groups=mesh['sample'=8,'space'=64] {'space'}, dimensions={0} | all-to-all | bytes 196608 | tf_op jit(solution)/shard_map/all_to_all | solution.py:471
  35.8 0.7 solve_first_kernel.1
  36.5 0.0 copy-start.5
  36.5 14.7 %all_to_all.36 = f32[64,1,512]{2,1,0:T(1,128)S(1)} all-to-all(f32[64,1,512]{2,1,0:T(1,128)S(1)} %bitcast.24), channel_id=1, replica_groups=mesh['sample'=8,'space'=64] {'space'}, dimensions={0} | all-to-all | bytes 262144 | tf_op jit(solution)/shard_map/all_to_all | solution.py:471
  51.2 1.4 middle_kernel.1
  52.6 15.7 %all_to_all.37 = f32[64,1,768]{2,1,0:T(1,128)S(1)} all-to-all(f32[64,1,768]{2,1,0:T(1,128)S(1)} %bitcast.23), channel_id=1, replica_groups=mesh['sample'=8,'space'=64] {'space'}, dimensions={0} | all-to-all | bytes 393216 | tf_op jit(solution)/shard_map/all_to_all | solution.py:471
  68.3 0.7 solve_both_kernel.1
  69.1 17.5 %all_to_all.38 = f32[64,1,1024]{2,1,0:T(1,128)S(1)} all-to-all(f32[64,1,1024]{2,1,0:T(1,128)S(1)} %bitcast.15), channel_id=1, replica_groups=mesh['sample'=8,'space'=64] {'space'}, dimensions={0} | all-to-all | bytes 524288 | tf_op jit(solution)/shard_map/all_to_all | solution.py:471
  86.6 2.0 %adjoint_kernel.1 = (f32[192,128]{1,0:T(8,128)S(1)}, f32[9,48,128]{2,1,0:T(8,128)S(1)}, f32[48,128]{1,0:T(8,128)S(1)}, f32[1,3,3,48,128]{4,3,2,1,0:T(8,128)}, f32[3,48,128]{2,1,0:T(8,128)S(1)}) custom-call(f32[512,128]{1,0:T(8,128)S(1)} %bitcast.16, f32[9,48,128]{2,1,0:T(8,128)S(1)} %get-tuple-element.39.second_trial, ...), custom_call_target="tpu_custom_call" | custom-call | tf_op jit(solution)/shard_map/adjoint_kernel/pallas_call | solution.py:457
  88.6 16.0 %all_to_all.39 = f32[64,1,384]{2,1,0:T(1,128)S(1)} all-to-all(f32[64,1,384]{2,1,0:T(1,128)S(1)} %bitcast.25), channel_id=1, replica_groups=mesh['sample'=8,'space'=64] {'space'}, dimensions={0} | all-to-all | bytes 196608 | tf_op jit(solution)/shard_map/all_to_all | solution.py:471
  104.6 0.7 solve_kernel.1
  105.3 14.5 %all_to_all.40 = f32[64,1,512]{2,1,0:T(1,128)S(1)} all-to-all(f32[64,1,512]{2,1,0:T(1,128)S(1)} %bitcast.19), channel_id=1, replica_groups=mesh['sample'=8,'space'=64] {'space'}, dimensions={0} | all-to-all | bytes 262144 | tf_op jit(solution)/shard_map/all_to_all | solution.py:471
  119.8 0.7 gradient_kernel.1
  120.5 27.3 %all_to_all.41 = f32[8,144,128]{2,1,0:T(8,128)S(1)} all-to-all(f32[8,144,128]{2,1,0:T(8,128)S(1)} %gradient_kernel.1), channel_id=1, replica_groups=mesh['sample'=8,'space'=64] {'sample'}, dimensions={0} | all-to-all | bytes 1179648 | tf_op jit(solution)/shard_map/all_to_all | solution.py:535
  147.8 0.7 reduce_sum.9
  (25 shorter events, 0.1 us)
Async XLA Ops:
  0.6 11.9 %copy-start.6 = (f32[3,48,128]{2,1,0:T(8,128)S(1)}, f32[3,48,128]{2,1,0:T(8,128)}, u32[]{:S(2)}) copy-start(f32[3,48,128]{2,1,0:T(8,128)} %correction.3) | copy-start | bytes 221188
  0.6 11.9 %copy-start.2 = (f32[3,3,48,128]{3,2,1,0:T(8,128)S(1)}, f32[3,3,48,128]{3,2,1,0:T(8,128)}, u32[]{:S(2)}) copy-start(f32[3,3,48,128]{3,2,1,0:T(8,128)} %own.3) | copy-start | bytes 663556
  1.8 12.1 %collective-permute-start = (f32[4,2,48,128]{3,2,1,0:T(8,128)S(1)}, f32[4,2,48,128]{3,2,1,0:T(8,128)S(1)}, u32[]{:S(2)}, u32[]{:S(2)}) collective-permute-start(f32[4,2,48,128]{3,2,1,0:T(8,128)S(1)} %get-tuple-element.25), channel_id=1, source_target_pairs={{0,1},{1,0},{2,3},{3,2},{4,5},{5,4},{6,7},{7,6},{8,9},{9,8},{10,11... | collective-permute-start | bytes 589832 | tf_op jit(solution)/shard_map/ppermute | solution.py:485
  10.5 2.0 %copy-start.11 = (s32[64,3]{0,1:T(4,128)S(1)}, s32[64,3]{0,1:T(4,128)}, u32[]{:S(2)}) copy-start(s32[64,3]{0,1:T(4,128)} %param.15) | copy-start | bytes 2308
  10.6 7.0 %collective-permute-start.1 = (f32[4,2,48,128]{3,2,1,0:T(8,128)S(1)}, f32[4,2,48,128]{3,2,1,0:T(8,128)S(1)}, u32[]{:S(2)}, u32[]{:S(2)}) collective-permute-start(f32[4,2,48,128]{3,2,1,0:T(8,128)S(1)} %get-tuple-element.26), channel_id=1, source_target_pairs={{0,63},{1,2},{2,1},{3,4},{4,3},{5,6},{6,5},{7,8},{8,7},{9,10},{10,... | collective-permute-start | bytes 589832 | tf_op jit(solution)/shard_map/ppermute | solution.py:486
  12.5 0.7 copy-start.12
  12.5 0.7 copy-start.13
  13.2 4.4 %copy-start.4 = (bf16[2,128,128]{2,1,0:T(8,128)(2,1)S(1)}, bf16[2,128,128]{2,1,0:T(8,128)(2,1)}, u32[]{:S(2)}) copy-start(bf16[2,128,128]{2,1,0:T(8,128)(2,1)} %constant.20.clone.to_y) | copy-start | bytes 196612
  13.2 4.4 %copy-start.8 = (bf16[2,48,48]{2,1,0:T(8,128)(2,1)S(1)}, bf16[2,48,48]{2,1,0:T(8,128)(2,1)}, u32[]{:S(2)}) copy-start(bf16[2,48,48]{2,1,0:T(8,128)(2,1)} %constant.22.clone.to_z) | copy-start | bytes 27652
  17.6 18.2 %copy-start = (bf16[3,256,192]{2,1,0:T(8,128)(2,1)S(1)}, bf16[3,256,192]{2,1,0:T(8,128)(2,1)}, u32[]{:S(2)}) copy-start(bf16[3,256,192]{2,1,0:T(8,128)(2,1)} %constant.19.clone.from_x) | copy-start | bytes 884740
  17.6 18.3 %copy-start.9 = (f32[200,128]{1,0:T(8,128)S(1)}, f32[200,128]{1,0:T(8,128)}, u32[]{:S(2)}) copy-start(f32[200,128]{1,0:T(8,128)} %constant.24.clone.squares) | copy-start | bytes 307204
  18.8 17.0 %copy-start.1 = (bf16[2,192,192]{2,1,0:T(8,128)(2,1)S(1)}, bf16[2,192,192]{2,1,0:T(8,128)(2,1)}, u32[]{:S(2)}) copy-start(bf16[2,192,192]{2,1,0:T(8,128)(2,1)} %constant.18.clone.to_x) | copy-start | bytes 442372
  36.5 14.7 %copy-start.3 = (bf16[3,128,128]{2,1,0:T(8,128)(2,1)S(1)}, bf16[3,128,128]{2,1,0:T(8,128)(2,1)}, u32[]{:S(2)}) copy-start(bf16[3,128,128]{2,1,0:T(8,128)(2,1)} %constant.21.clone.from_y) | copy-start | bytes 294916
  36.5 14.7 %copy-start.5 = (bf16[3,48,48]{2,1,0:T(8,128)(2,1)S(1)}, bf16[3,48,48]{2,1,0:T(8,128)(2,1)}, u32[]{:S(2)}) copy-start(bf16[3,48,48]{2,1,0:T(8,128)(2,1)} %constant.23.clone.from_z) | copy-start | bytes 41476
  36.5 14.7 %copy-start.7 = (f32[3,48,128]{2,1,0:T(8,128)S(1)}, f32[3,48,128]{2,1,0:T(8,128)}, u32[]{:S(2)}) copy-start(f32[3,48,128]{2,1,0:T(8,128)} %observed.3) | copy-start | bytes 221188
  52.6 15.8 %copy-start.10 = (f32[192,128]{1,0:T(8,128)S(1)}, f32[192,128]{1,0:T(8,128)}, u32[]{:S(2)}) copy-start(f32[192,128]{1,0:T(8,128)} %constant.25.clone.sine_in) | copy-start | bytes 294916

commit v5 on v4

--- a/solution.py
+++ b/solution.py
@@ -62,12 +62,38 @@
     return ((SLAB * device + slot) % NX).reshape(-1)
 
 
-TO_Y = in_parts(BASIS_Y, 2)
-TO_Z = in_parts(BASIS_Z.T, 2)
-TO_X = in_parts(BASIS_X[stream_rows(0, 3)].T, 2)
-FROM_Y = in_parts(BASIS_Y.T, 3)
-FROM_Z = in_parts(BASIS_Z, 3)
-FROM_X = in_parts(BASIS_X[stream_rows(0, 4)], 3)
+def pairs_of(count):
+    return [(i, order - i) for order in reversed(range(count)) for i in range(order + 1)]
+
+
+def left_table(matrix, count):
+    parts = in_parts(matrix, count)
+    return np.concatenate([parts[i] for i, _ in pairs_of(count)], axis=1)
+
+
+def left_narrow_table(matrix, count):
+    parts = list(in_parts(matrix, count))
+    return np.concatenate(parts if count == 2 else parts + parts[:1], axis=1)
+
+
+def right_table(matrix, count):
+    parts = list(in_parts(matrix, count))
+    none = np.zeros_like(parts[0])
+    if count == 2:
+        rows = [(parts[0], parts[1]), (parts[0], none)]
+    else:
+        rows = [(parts[0], parts[1]), (parts[0], parts[1]), (parts[0], none), (parts[2], none)]
+    return np.concatenate([np.concatenate(row, axis=1) for row in rows], axis=0)
+
+
+TO_Y = right_table(BASIS_Y, 2)
+TO_Z = left_table(BASIS_Z.T, 2)
+TO_X = left_narrow_table(BASIS_X[stream_rows(0, 3)].T, 2)
+TO_X_WIDE = left_table(BASIS_X[stream_rows(0, 3)].T, 2)
+FROM_Y = right_table(BASIS_Y.T, 3)
+FROM_Z = left_table(BASIS_Z, 3)
+FROM_X = left_narrow_table(BASIS_X[stream_rows(0, 4)], 3)
+FROM_X_WIDE = left_table(BASIS_X[stream_rows(0, 4)], 3)
 SINE_X = np.broadcast_to(sine_of(NX)[:, None], (NX, NY)).astype(np.float32)
 SQUARES = np.zeros((NX + 8, NY), np.float32)
 SQUARES[:NX] = sine_of(NX)[:, None] ** 2 + sine_of(NY)[None, :] ** 2
@@ -86,18 +112,28 @@
     return jnp.dot(a, b, preferred_element_type=F32)
 
 
-def left_product(matrix, value):
-    count = matrix.shape[0]
+def left_product(table, value, count):
     parts = split(value, count)
-    pairs = [(i, order - i) for order in reversed(range(count)) for i in range(order + 1)]
-    return sum(dot(matrix[i], parts[k]) for i, k in pairs)
-
-
-def right_product(value, matrix):
-    count = matrix.shape[0]
+    return dot(table[...], jnp.concatenate([parts[k] for _, k in pairs_of(count)], axis=0))
+
+
+def left_narrow_product(table, value, count):
     parts = split(value, count)
-    pairs = [(i, order - i) for order in reversed(range(count)) for i in range(order + 1)]
-    return sum(dot(parts[k], matrix[i]) for i, k in pairs)
+    none = jnp.zeros_like(parts[0])
+    if count == 2:
+        rows = [(parts[0], parts[1]), (parts[0], none)]
+    else:
+        rows = [(parts[0], parts[1]), (parts[0], parts[1]), (parts[0], none), (none, parts[2])]
+    wide = jnp.concatenate([jnp.concatenate(row, axis=1) for row in rows], axis=0)
+    found = dot(table[...], wide)
+    return found[:, :NY] + found[:, NY:]
+
+
+def right_product(value, table, count):
+    parts = split(value, count)
+    wide = jnp.concatenate(parts if count == 2 else parts + parts[:1], axis=1)
+    found = dot(wide, table[...])
+    return found[:, :NY] + found[:, NY:]
 
 
 def up_z(f):
@@ -145,9 +181,9 @@
 
 def to_modes(planes, to_z, to_y, out_ref):
     count = len(planes)
-    side = left_product(to_z, jnp.concatenate(planes, axis=1))
+    side = left_product(to_z, jnp.concatenate(planes, axis=1), 2)
     rows = jnp.concatenate([side[:, NY * i : NY * (i + 1)] for i in range(count)], axis=0)
-    rows = right_product(rows, to_y)
+    rows = right_product(rows, to_y, 2)
     for i in range(count):
         out_ref[pl.ds(i, NZ, stride=count), :] = rows[NZ * i : NZ * (i + 1)]
     out_ref[NZ * count :, :] = jnp.zeros(((SPACE - NZ) * count, NY), F32)
@@ -155,9 +191,9 @@
 
 def from_modes(in_ref, count, from_z, from_y):
     rows = jnp.concatenate([in_ref[pl.ds(i, NZ, stride=count), :] for i in range(count)], axis=0)
-    rows = right_product(rows, from_y)
+    rows = right_product(rows, from_y, 3)
     side = jnp.concatenate([rows[NZ * i : NZ * (i + 1)] for i in range(count)], axis=1)
-    side = left_product(from_z, side)
+    side = left_product(from_z, side, 3)
     return [side[:, NY * i : NY * (i + 1)] for i in range(count)]
 
 
@@ -233,13 +269,19 @@
         fill(inner, outer)
 
 
-def rolled(plane, seeds):
-    return pltpu.roll(pltpu.roll(plane, seeds[0, 0], 1), seeds[0, 1], 0)
+def rolled(plane, shifts):
+    return pltpu.roll(pltpu.roll(plane, shifts[0], 1), shifts[1], 0)
+
+
+def shifts_of(seeds):
+    row = seeds[...]
+    return row[0, 0], row[0, 1]
 
 
 def prepare_kernel(
     seeds, own, correction, cells, heights, state_out, viscosity_out, rotor_out, column_out
 ):
+    shifts = shifts_of(seeds)
     profile = spread_profile(heights[...])
     column_out[...] = profile
     rotor = count_rotors(cells)
@@ -248,7 +290,7 @@
     for j in range(3):
         viscosity_out[j] = BASE_VISCOSITY * jnp.exp(correction[j])
         for c in range(3):
-            plane = rolled(own[c, j], seeds)
+            plane = rolled(own[c, j], shifts)
             state_out[3 * c + j] = plane + profile if c == 0 else plane
 
 
@@ -257,6 +299,7 @@
     buffer, first_trial, source_out, beside_out, laplace_out, viscosity_out,
 ):
     even = lax.rem(lax.axis_index("space"), 2) == 0
+    shifts = shifts_of(seeds)
     profile = column[...]
 
     def halo(j, c):
@@ -279,7 +322,7 @@
             if 0 <= j < 3:
                 state[j] = own_state[3 * c + j]
             else:
-                state[j] = rolled(halo(j, c), seeds)
+                state[j] = rolled(halo(j, c), shifts)
                 if c == 0:
                     state[j] = state[j] + profile
         moved = {}
@@ -315,8 +358,8 @@
 
 
 def solve_rows(modes_in, green, to_x, from_x, out):
-    spectrum = left_product(to_x, gather_slots(modes_in, 0, 3, 3)) * green
-    scatter_slots(out, left_product(from_x, spectrum), 0, 4, 4)
+    spectrum = left_narrow_product(to_x, gather_slots(modes_in, 0, 3, 3), 2) * green
+    scatter_slots(out, left_narrow_product(from_x, spectrum, 3), 0, 4, 4)
 
 
 def solve_first_kernel(modes_in, squares, to_x, from_x, out, green_out):
@@ -325,8 +368,11 @@
     solve_rows(modes_in, green, to_x, from_x, out)
 
 
-def solve_kernel(modes_in, green, to_x, from_x, out):
+def solve_last_kernel(modes_in, green, to_x, from_x, velocity, out, velocity_out, sent):
+    copy = pltpu.make_async_copy(velocity, velocity_out, sent)
+    copy.start()
     solve_rows(modes_in, green[...], to_x, from_x, out)
+    copy.wait()
 
 
 def middle_kernel(
@@ -375,11 +421,11 @@
     both = jnp.concatenate(
         [gather_slots(modes_in, 0, 3, 6), gather_slots(modes_in, 3, 3, 6)], axis=1
     )
-    both = left_product(to_x, both)
+    both = left_product(to_x, both, 2)
     lead = both[:, :NY]
     second = inverse * both[:, NY:]
     third = inverse * swap_waves(lead - swap_waves(second, sine), sine)
-    wide = left_product(from_x, jnp.concatenate([second, third], axis=1))
+    wide = left_product(from_x, jnp.concatenate([second, third], axis=1), 3)
     scatter_slots(out, wide[:, :NY], 0, 4, 8)
     scatter_slots(out, wide[:, NY:], 4, 4, 8)
 
@@ -449,10 +495,11 @@
             out[copy, NZ * j : NZ * (j + 1), :] = total
 
 
-def local_call(kernel, outs, *args, spaces={}, scratch=()):
+def local_call(kernel, outs, *args, spaces={}, out_spaces={}, scratch=()):
     specs = [pl.BlockSpec(memory_space=spaces.get(i, pltpu.VMEM)) for i in range(len(args))]
-    shapes = [jax.ShapeDtypeStruct(shape, F32) for shape in outs]
-    out_specs = [pl.BlockSpec(memory_space=pltpu.VMEM) for _ in outs]
+    out_spaces = [out_spaces.get(i, pltpu.VMEM) for i in range(len(outs))]
+    shapes = [space(shape, F32) for space, shape in zip(out_spaces, outs)]
+    out_specs = [pl.BlockSpec(memory_space=space) for space in out_spaces]
     single = len(outs) == 1
     return pl.pallas_call(
         kernel,
@@ -491,13 +538,11 @@
     state, viscosity, rotor, column = local_call(
         prepare_kernel, [(9, *plane), (3, *plane), (5, *plane), plane],
         inflow_seeds, fluctuation, correction, rotor_cells.T, profile[None, :],
-        spaces={0: pltpu.SMEM},
     )
     buffer, first_trial, source, beside, laplace_start, viscosity = local_call(
         start_kernel,
         [(SPACE * 3, NY), (15, *plane), plane, (2, *plane), (9, *plane), (7, *plane)],
         inflow_seeds, inner, outer, state, viscosity, rotor, column, to_z, to_y,
-        spaces={0: pltpu.SMEM},
     )
     buffer = exchange(buffer)
     buffer, green = local_call(
@@ -514,7 +559,7 @@
     buffer = exchange(buffer)
     buffer = local_call(
         solve_both_kernel, [(SPACE * 8, NY)],
-        buffer, green, jnp.asarray(SINE_X), to_x, from_x,
+        buffer, green, jnp.asarray(SINE_X), jnp.asarray(TO_X_WIDE), jnp.asarray(FROM_X_WIDE),
     )
     buffer = exchange(buffer)
     buffer, fourth_trial, source, velocity, share = local_call(
@@ -524,8 +569,10 @@
         from_z, from_y, to_z, to_y,
     )
     buffer = exchange(buffer)
-    buffer = local_call(
-        solve_kernel, [(SPACE * 4, NY)], buffer, green, to_x, from_x
+    buffer, velocity = local_call(
+        solve_last_kernel, [(SPACE * 4, NY), velocity.shape],
+        buffer, green, to_x, from_x, velocity,
+        out_spaces={1: pltpu.HBM}, scratch=[pltpu.SemaphoreType.DMA],
     )
     buffer = exchange(buffer)
     terms = local_call(

time: 149 us -> 147 us (0.987)
  Pallas kernels: 9.25 us -> 7.03 us
    pallas_call x9, Pallas kernels: 9.25 us -> 7.03 us  [local_call(): pl.pallas_call(kernel, out_shape=shapes[0] if single else shapes, in_spec...]
where the time goes in v5:
time: 147 us
  blocking collectives  123 us (84%)
  starting transfers between devices  10.7 us (7%)
  Pallas kernels  7.03 us (5%)
  waiting for transfers between devices  4.17 us (3%)
    all_to_all x6, blocking collectives, exchange(): return lax.all_to_all(wide, axis, 0, 0, tiled=True).reshape(rows.shape)  95.4 us
    all_to_all x1, blocking collectives, shards(): terms = lax.all_to_all(terms, 'sample', 0, 0, tiled=True)  27.3 us
    ppermute x1, starting transfers between devices, shards(): inner = lax.ppermute(inner, 'space', within)  8.77 us
    pallas_call x9, Pallas kernels, local_call(): pl.pallas_call(kernel, out_shape=shapes[0] if single else shapes, in_spec...  7.03 us
    ppermute x1, waiting for transfers between devices, shards(): outer = lax.ppermute(outer, 'space', between)  4.16 us
  transfers between devices with their start and end apart: 2, of which 1 were waited for; matrix products, arithmetic and copies ran while one was open for 0% of the time, Pallas kernels for 0%

profile of v5, /device:TPU:1, one launch (start us, length us, event | category | flops | bytes accessed | tf_op | source)
XLA Modules:
  0.0 146.8 jit_solution(1311823106801237092)
XLA Ops:
  0.6 1.1 pack_kernel.1
  1.8 8.8 %collective-permute-start = (f32[4,2,48,128]{3,2,1,0:T(8,128)S(1)}, f32[4,2,48,128]{3,2,1,0:T(8,128)S(1)}, u32[]{:S(2)}, u32[]{:S(2)}) collective-permute-start(f32[4,2,48,128]{3,2,1,0:T(8,128)S(1)} %get-tuple-element.27), channel_id=1, source_target_pairs={{0,1},{1,0},{2,3},{3,2},{4,5},{5,4},{6,7},{7,6},{8,9},{9,8},{10,11... | collective-permute-start | bytes 589832 | tf_op jit(solution)/shard_map/ppermute | solution.py:532
  10.6 1.9 %collective-permute-start.1 = (f32[4,2,48,128]{3,2,1,0:T(8,128)S(1)}, f32[4,2,48,128]{3,2,1,0:T(8,128)S(1)}, u32[]{:S(2)}, u32[]{:S(2)}) collective-permute-start(f32[4,2,48,128]{3,2,1,0:T(8,128)S(1)} %get-tuple-element.28), channel_id=1, source_target_pairs={{0,63},{1,2},{2,1},{3,4},{4,3},{5,6},{6,5},{7,8},{8,7},{9,10},{10,... | collective-permute-start | bytes 589832 | tf_op jit(solution)/shard_map/ppermute | solution.py:533
  12.5 0.6 copy-done.13
  13.1 0.0 copy-done.15
  13.2 0.2 prepare_kernel.1
  13.4 4.2 %collective-permute-done.1.outer = f32[4,2,48,128]{3,2,1,0:T(8,128)S(1)} collective-permute-done((f32[4,2,48,128]{3,2,1,0:T(8,128)S(1)}, f32[4,2,48,128]{3,2,1,0:T(8,128)S(1)}, u32[]{:S(2)}, u32[]{:S(2)}) %collective-permute-start.1) | collective-permute-done | bytes 196640 | tf_op jit(solution)/shard_map/ppermute | solution.py:533
  17.6 0.7 start_kernel.1
  18.2 0.0 copy-start.5
  18.2 17.0 %all_to_all.35 = f32[64,1,384]{2,1,0:T(1,128)S(1)} all-to-all(f32[64,1,384]{2,1,0:T(1,128)S(1)} %bitcast.26), channel_id=1, replica_groups=mesh['sample'=8,'space'=64] {'space'}, dimensions={0} | all-to-all | bytes 196608 | tf_op jit(solution)/shard_map/all_to_all | solution.py:518
  35.2 0.0 copy-start.6
  35.3 0.5 solve_first_kernel.1
  35.8 14.7 %all_to_all.36 = f32[64,1,512]{2,1,0:T(1,128)S(1)} all-to-all(f32[64,1,512]{2,1,0:T(1,128)S(1)} %bitcast.24), channel_id=1, replica_groups=mesh['sample'=8,'space'=64] {'space'}, dimensions={0} | all-to-all | bytes 262144 | tf_op jit(solution)/shard_map/all_to_all | solution.py:518
  50.4 1.1 middle_kernel.1
  51.6 15.7 %all_to_all.37 = f32[64,1,768]{2,1,0:T(1,128)S(1)} all-to-all(f32[64,1,768]{2,1,0:T(1,128)S(1)} %bitcast.22), channel_id=1, replica_groups=mesh['sample'=8,'space'=64] {'space'}, dimensions={0} | all-to-all | bytes 393216 | tf_op jit(solution)/shard_map/all_to_all | solution.py:518
  67.3 0.7 solve_both_kernel.1
  68.1 17.5 %all_to_all.38 = f32[64,1,1024]{2,1,0:T(1,128)S(1)} all-to-all(f32[64,1,1024]{2,1,0:T(1,128)S(1)} %bitcast.16), channel_id=1, replica_groups=mesh['sample'=8,'space'=64] {'space'}, dimensions={0} | all-to-all | bytes 524288 | tf_op jit(solution)/shard_map/all_to_all | solution.py:518
  85.6 1.3 adjoint_kernel.1
  86.9 16.0 %all_to_all.39 = f32[64,1,384]{2,1,0:T(1,128)S(1)} all-to-all(f32[64,1,384]{2,1,0:T(1,128)S(1)} %bitcast.25), channel_id=1, replica_groups=mesh['sample'=8,'space'=64] {'space'}, dimensions={0} | all-to-all | bytes 196608 | tf_op jit(solution)/shard_map/all_to_all | solution.py:518
  102.9 0.9 solve_last_kernel.1
  103.8 14.5 %all_to_all.40 = f32[64,1,512]{2,1,0:T(1,128)S(1)} all-to-all(f32[64,1,512]{2,1,0:T(1,128)S(1)} %bitcast.23), channel_id=1, replica_groups=mesh['sample'=8,'space'=64] {'space'}, dimensions={0} | all-to-all | bytes 262144 | tf_op jit(solution)/shard_map/all_to_all | solution.py:518
  118.3 0.6 gradient_kernel.1
  118.9 27.3 %all_to_all.41 = f32[8,144,128]{2,1,0:T(8,128)S(1)} all-to-all(f32[8,144,128]{2,1,0:T(8,128)S(1)} %gradient_kernel.1), channel_id=1, replica_groups=mesh['sample'=8,'space'=64] {'sample'}, dimensions={0} | all-to-all | bytes 1179648 | tf_op jit(solution)/shard_map/all_to_all | solution.py:582
  146.2 0.7 reduce_sum.9
  (29 shorter events, 0.1 us)
Async XLA Ops:
  0.6 11.9 %copy-start.8 = (f32[3,48,128]{2,1,0:T(8,128)S(1)}, f32[3,48,128]{2,1,0:T(8,128)}, u32[]{:S(2)}) copy-start(f32[3,48,128]{2,1,0:T(8,128)} %correction.3) | copy-start | bytes 221188
  0.6 11.9 %copy-start.3 = (f32[3,3,48,128]{3,2,1,0:T(8,128)S(1)}, f32[3,3,48,128]{3,2,1,0:T(8,128)}, u32[]{:S(2)}) copy-start(f32[3,3,48,128]{3,2,1,0:T(8,128)} %own.3) | copy-start | bytes 663556
  1.8 11.6 %collective-permute-start = (f32[4,2,48,128]{3,2,1,0:T(8,128)S(1)}, f32[4,2,48,128]{3,2,1,0:T(8,128)S(1)}, u32[]{:S(2)}, u32[]{:S(2)}) collective-permute-start(f32[4,2,48,128]{3,2,1,0:T(8,128)S(1)} %get-tuple-element.27), channel_id=1, source_target_pairs={{0,1},{1,0},{2,3},{3,2},{4,5},{5,4},{6,7},{7,6},{8,9},{9,8},{10,11... | collective-permute-start | bytes 589832 | tf_op jit(solution)/shard_map/ppermute | solution.py:532
  10.5 2.0 %copy-start.14 = (s32[64,3]{0,1:T(4,128)S(1)}, s32[64,3]{0,1:T(4,128)}, u32[]{:S(2)}) copy-start(s32[64,3]{0,1:T(4,128)} %param.17) | copy-start | bytes 2308
  10.6 7.0 %collective-permute-start.1 = (f32[4,2,48,128]{3,2,1,0:T(8,128)S(1)}, f32[4,2,48,128]{3,2,1,0:T(8,128)S(1)}, u32[]{:S(2)}, u32[]{:S(2)}) collective-permute-start(f32[4,2,48,128]{3,2,1,0:T(8,128)S(1)} %get-tuple-element.28), channel_id=1, source_target_pairs={{0,63},{1,2},{2,1},{3,4},{4,3},{5,6},{6,5},{7,8},{8,7},{9,10},{10,... | collective-permute-start | bytes 589832 | tf_op jit(solution)/shard_map/ppermute | solution.py:533
  12.5 0.7 copy-start.13
  12.5 0.7 copy-start.15
  13.2 4.4 %copy-start.2 = (bf16[256,256]{1,0:T(8,128)(2,1)S(1)}, bf16[256,256]{1,0:T(8,128)(2,1)}, u32[]{:S(2)}) copy-start(bf16[256,256]{1,0:T(8,128)(2,1)} %constant.24.clone.to_y) | copy-start | bytes 393220
  13.2 4.4 %copy-start.10 = (bf16[48,144]{1,0:T(8,128)(2,1)S(1)}, bf16[48,144]{1,0:T(8,128)(2,1)}, u32[]{:S(2)}) copy-start(bf16[48,144]{1,0:T(8,128)(2,1)} %constant.26.clone.to_z) | copy-start | bytes 41476
  17.6 17.7 %copy-start.1 = (bf16[256,768]{1,0:T(8,128)(2,1)S(1)}, bf16[256,768]{1,0:T(8,128)(2,1)}, u32[]{:S(2)}) copy-start(bf16[256,768]{1,0:T(8,128)(2,1)} %constant.23.clone.from_x) | copy-start | bytes 1179652
  17.6 17.7 %copy-start.11 = (f32[200,128]{1,0:T(8,128)S(1)}, f32[200,128]{1,0:T(8,128)}, u32[]{:S(2)}) copy-start(f32[200,128]{1,0:T(8,128)} %constant.28.clone.squares) | copy-start | bytes 307204
  18.2 17.0 %copy-start.5 = (bf16[192,384]{1,0:T(8,128)(2,1)S(1)}, bf16[192,384]{1,0:T(8,128)(2,1)}, u32[]{:S(2)}) copy-start(bf16[192,384]{1,0:T(8,128)(2,1)} %constant.22.clone.to_x) | copy-start | bytes 442372
  35.2 15.2 %copy-start.6 = (bf16[48,288]{1,0:T(8,128)(2,1)S(1)}, bf16[48,288]{1,0:T(8,128)(2,1)}, u32[]{:S(2)}) copy-start(bf16[48,288]{1,0:T(8,128)(2,1)} %constant.27.clone.from_z) | copy-start | bytes 82948
  35.2 15.2 %copy-start.7 = (f32[3,48,128]{2,1,0:T(8,128)S(1)}, f32[3,48,128]{2,1,0:T(8,128)}, u32[]{:S(2)}) copy-start(f32[3,48,128]{2,1,0:T(8,128)} %observed.3) | copy-start | bytes 221188
  35.7 14.7 %copy-start = (bf16[512,256]{1,0:T(8,128)(2,1)S(1)}, bf16[512,256]{1,0:T(8,128)(2,1)}, u32[]{:S(2)}) copy-start(bf16[512,256]{1,0:T(8,128)(2,1)} %constant.25.clone.from_y) | copy-start | bytes 786436
  50.4 16.9 %copy-start.4 = (bf16[256,1152]{1,0:T(8,128)(2,1)S(1)}, bf16[256,1152]{1,0:T(8,128)(2,1)}, u32[]{:S(2)}) copy-start(bf16[256,1152]{1,0:T(8,128)(2,1)} %constant.31.clone.from_x) | copy-start | bytes 1769476
  51.6 15.8 %copy-start.9 = (bf16[192,576]{1,0:T(8,128)(2,1)S(1)}, bf16[192,576]{1,0:T(8,128)(2,1)}, u32[]{:S(2)}) copy-start(bf16[192,576]{1,0:T(8,128)(2,1)} %constant.30.clone.to_x) | copy-start | bytes 663556
  51.6 15.8 %copy-start.12 = (f32[192,128]{1,0:T(8,128)S(1)}, f32[192,128]{1,0:T(8,128)}, u32[]{:S(2)}) copy-start(f32[192,128]{1,0:T(8,128)} %constant.29.clone.sine_in) | copy-start | bytes 294916

commit v6 on v5

--- a/solution.py
+++ b/solution.py
@@ -94,10 +94,20 @@
 FROM_Z = left_table(BASIS_Z, 3)
 FROM_X = left_narrow_table(BASIS_X[stream_rows(0, 4)], 3)
 FROM_X_WIDE = left_table(BASIS_X[stream_rows(0, 4)], 3)
-SINE_X = np.broadcast_to(sine_of(NX)[:, None], (NX, NY)).astype(np.float32)
-SQUARES = np.zeros((NX + 8, NY), np.float32)
-SQUARES[:NX] = sine_of(NX)[:, None] ** 2 + sine_of(NY)[None, :] ** 2
-SQUARES[NX, :NZ] = sine_of(NZ) ** 2
+BLOCK = 32
+BLOCKS = NY // BLOCK
+UNITS = NZ * BLOCKS // SPACE
+
+
+def symbol_table():
+    table = np.ones((NX + SPACE, NY))
+    table[:NX] = sine_of(NX)[:, None]
+    squares = (sine_of(NZ) ** 2)[:, None] + (sine_of(NY) ** 2)[None, :]
+    table[NX:, : UNITS * BLOCK] = squares.reshape(SPACE, UNITS * BLOCK)
+    return table.astype(np.float32)
+
+
+SYMBOLS = symbol_table()
 
 
 def split(value, count):
@@ -179,32 +189,89 @@
     return {-1: below, 0: planes[0], 1: planes[1], 2: planes[2], 3: planes[3]}
 
 
-def to_modes(planes, to_z, to_y, out_ref):
+def block_of(array):
+    return lax.broadcasted_iota(jnp.int32, array.shape, 1) // BLOCK
+
+
+def move(array, blocks):
+    return pltpu.roll(array, BLOCK * blocks, 1)
+
+
+THIRD = NZ // UNITS
+
+
+def by_device(sheet_ref, first):
+    a, b, c = [sheet_ref[pl.ds(first + i, THIRD, stride=UNITS), :] for i in range(UNITS)]
+    block = block_of(a)
+    return [a, move(jnp.where(block == 3, a, b), 1), move(jnp.where(block >= 2, b, c), 2), move(c, 3)]
+
+
+def by_height(parts):
+    block = block_of(parts[0])
+    b, c, d = move(parts[1], 3), move(parts[2], 2), move(parts[3], 1)
+    return [
+        jnp.where(block == 3, b, parts[0]),
+        jnp.where(block < 2, b, c),
+        jnp.where(block == 0, c, d),
+    ]
+
+
+def to_modes(planes, to_z, to_y, out_ref, sheet_ref):
     count = len(planes)
     side = left_product(to_z, jnp.concatenate(planes, axis=1), 2)
     rows = jnp.concatenate([side[:, NY * i : NY * (i + 1)] for i in range(count)], axis=0)
-    rows = right_product(rows, to_y, 2)
-    for i in range(count):
-        out_ref[pl.ds(i, NZ, stride=count), :] = rows[NZ * i : NZ * (i + 1)]
-    out_ref[NZ * count :, :] = jnp.zeros(((SPACE - NZ) * count, NY), F32)
-
-
-def from_modes(in_ref, count, from_z, from_y):
-    rows = jnp.concatenate([in_ref[pl.ds(i, NZ, stride=count), :] for i in range(count)], axis=0)
-    rows = right_product(rows, from_y, 3)
+    sheet_ref[: NZ * count, :] = right_product(rows, to_y, 2)
+    sheets = [by_device(sheet_ref, NZ * i) for i in range(count)]
+    fourth = sheets.pop(3) if count > 3 else None
+    width = len(sheets)
+    for row, parts in enumerate(sheets):
+        for i in range(BLOCKS):
+            part = parts[i]
+            if row < UNITS and fourth is not None:
+                part = jnp.where(block_of(part) == 3, move(fourth[i], 3 - row), part)
+            out_ref[pl.ds(i * width + row, THIRD, stride=BLOCKS * width), :] = part
+
+
+def from_modes(in_ref, groups, from_z, from_y, sheet_ref):
+    count = 4 * groups
+    for g in range(groups):
+        for p in range(UNITS):
+            first = p * groups + g
+            parts = [
+                in_ref[pl.ds(i * UNITS * groups + first, THIRD, stride=BLOCKS * UNITS * groups), :]
+                for i in range(BLOCKS)
+            ]
+            for i, part in enumerate(by_height(parts)):
+                sheet_ref[pl.ds(NZ * (4 * g + p) + i, THIRD, stride=UNITS), :] = part
+        units = [in_ref[pl.ds(j * groups + g, NZ, stride=BLOCKS * groups), :] for j in range(BLOCKS)]
+        block = block_of(units[3])
+        fourth = units[3]
+        for j in range(UNITS):
+            fourth = jnp.where(block == j, move(units[j], j + 1), fourth)
+        sheet_ref[NZ * (4 * g + 3) : NZ * (4 * g + 4), :] = fourth
+    rows = right_product(sheet_ref[: NZ * count, :], from_y, 3)
     side = jnp.concatenate([rows[NZ * i : NZ * (i + 1)] for i in range(count)], axis=1)
     side = left_product(from_z, side, 3)
     return [side[:, NY * i : NY * (i + 1)] for i in range(count)]
 
 
-def gather_slots(in_ref, first, count, total):
-    parts = [in_ref[pl.ds(i, SPACE, stride=total), :] for i in range(first, first + count)]
-    return jnp.concatenate(parts, axis=0)
-
-
-def scatter_slots(out_ref, rows, first, count, total):
-    for i in range(count):
-        out_ref[pl.ds(first + i, SPACE, stride=total), :] = rows[SPACE * i : SPACE * (i + 1)]
+def gather_planes(in_ref, width):
+    rows = [in_ref[pl.ds(i, SPACE, stride=width), :] for i in range(width)]
+    if width == UNITS:
+        return rows
+    block = block_of(rows[0])
+    fourth = jnp.where(block == 0, move(rows[0], 1), move(rows[2], 3))
+    fourth = jnp.where(block == 1, move(rows[1], 2), fourth)
+    return rows[:UNITS] + [fourth] + rows[UNITS:]
+
+
+def scatter_planes(out_ref, wide, groups):
+    for g in range(groups):
+        sheet = wide[:, NY * g : NY * (g + 1)]
+        planes = [sheet[SPACE * p : SPACE * (p + 1)] for p in range(4)]
+        for u in range(UNITS):
+            row = jnp.where(block_of(planes[u]) == 3, move(planes[3], 3 - u), planes[u])
+            out_ref[pl.ds(u * groups + g, SPACE, stride=UNITS * groups), :] = row
 
 
 def swap_waves(modes, sine):
@@ -296,7 +363,7 @@
 
 def start_kernel(
     seeds, inner, outer, own_state, own_viscosity, rotor, column, to_z, to_y,
-    buffer, first_trial, source_out, beside_out, laplace_out, viscosity_out,
+    buffer, first_trial, source_out, beside_out, laplace_out, viscosity_out, sheet,
 ):
     even = lax.rem(lax.axis_index("space"), 2) == 0
     shifts = shifts_of(seeds)
@@ -346,24 +413,24 @@
         for j in range(3)
     ]
     source_out[...] = sources[1]
-    to_modes(sources, to_z, to_y, buffer)
-
-
-def green_table(squares):
-    place = lax.broadcasted_iota(jnp.int32, (1, NY), 1)
-    mine = jnp.where(place == lax.axis_index("space"), squares[NX : NX + 1, :], 0.0)
-    summed = squares[:NX, :] + jnp.sum(mine, axis=1, keepdims=True)
+    to_modes(sources, to_z, to_y, buffer, sheet)
+
+
+def green_table(symbols):
+    sine = symbols[:NX, :]
+    summed = sine * sine + symbols[pl.ds(NX + lax.axis_index("space"), 1), :]
     null_mode = summed == 0.0
     return jnp.where(null_mode, 0.0, -1.0 / jnp.where(null_mode, 1.0, summed))
 
 
 def solve_rows(modes_in, green, to_x, from_x, out):
-    spectrum = left_narrow_product(to_x, gather_slots(modes_in, 0, 3, 3), 2) * green
-    scatter_slots(out, left_narrow_product(from_x, spectrum, 3), 0, 4, 4)
-
-
-def solve_first_kernel(modes_in, squares, to_x, from_x, out, green_out):
-    green = green_table(squares)
+    planes = jnp.concatenate(gather_planes(modes_in, 3), axis=0)
+    spectrum = left_narrow_product(to_x, planes, 2) * green
+    scatter_planes(out, left_narrow_product(from_x, spectrum, 3), 1)
+
+
+def solve_first_kernel(modes_in, symbols, to_x, from_x, out, green_out):
+    green = green_table(symbols)
     green_out[...] = green
     solve_rows(modes_in, green, to_x, from_x, out)
 
@@ -378,10 +445,10 @@
 def middle_kernel(
     modes_in, first_trial, source, state, beside, viscosity, rotor, observed, column,
     from_z, from_y, to_z, to_y,
-    buffer, second_trial, source_out, laplace_out,
+    buffer, second_trial, source_out, laplace_out, sheet,
 ):
     profile = column[...]
-    pressure = with_plane_below(from_modes(modes_in, 4, from_z, from_y), source[...])
+    pressure = with_plane_below(from_modes(modes_in, 1, from_z, from_y, sheet), source[...])
     span = {j: first_trial[6 + j] - along_span(pressure[j]) for j in range(-1, 4)}
     height = {j: first_trial[11 + j] - along_height(pressure[j]) for j in range(-1, 4)}
     stream = {j: first_trial[1 + j] - along_stream(pressure, j) for j in range(3)}
@@ -412,31 +479,31 @@
     ]
     source_out[...] = sources[1]
     sheets = [trial[0][j] - observed[j] for j in range(3)] + sources
-    to_modes(sheets, to_z, to_y, buffer)
-
-
-def solve_both_kernel(modes_in, green, sine_in, to_x, from_x, out):
-    sine = sine_in[...]
+    to_modes(sheets, to_z, to_y, buffer, sheet)
+
+
+def solve_both_kernel(modes_in, green, symbols, to_x, from_x, out):
+    sine = symbols[:NX, :]
     inverse = green[...]
+    planes = gather_planes(modes_in, 5)
     both = jnp.concatenate(
-        [gather_slots(modes_in, 0, 3, 6), gather_slots(modes_in, 3, 3, 6)], axis=1
+        [jnp.concatenate(planes[:3], axis=0), jnp.concatenate(planes[3:], axis=0)], axis=1
     )
     both = left_product(to_x, both, 2)
     lead = both[:, :NY]
     second = inverse * both[:, NY:]
     third = inverse * swap_waves(lead - swap_waves(second, sine), sine)
     wide = left_product(from_x, jnp.concatenate([second, third], axis=1), 3)
-    scatter_slots(out, wide[:, :NY], 0, 4, 8)
-    scatter_slots(out, wide[:, NY:], 4, 4, 8)
+    scatter_planes(out, wide, 2)
 
 
 def adjoint_kernel(
     modes_in, second_trial, source, laplace_mid, viscosity, rotor, observed, column,
     from_z, from_y, to_z, to_y,
-    buffer, fourth_trial, source_out, velocity, share_out,
+    buffer, fourth_trial, source_out, velocity, share_out, sheet,
 ):
     profile = column[...]
-    found = from_modes(modes_in, 8, from_z, from_y)
+    found = from_modes(modes_in, 2, from_z, from_y, sheet)
     second = with_plane_below(found[:4], source[...])
     misfit = []
     for j in range(3):
@@ -478,13 +545,13 @@
         for j in range(3)
     ]
     source_out[...] = sources[1]
-    to_modes(sources, to_z, to_y, buffer)
+    to_modes(sources, to_z, to_y, buffer, sheet)
 
 
 def gradient_kernel(
-    modes_in, fourth_trial, source, laplace_start, viscosity, share, from_z, from_y, out
+    modes_in, fourth_trial, source, laplace_start, viscosity, share, from_z, from_y, out, sheet
 ):
-    pressure = with_plane_below(from_modes(modes_in, 4, from_z, from_y), source[...])
+    pressure = with_plane_below(from_modes(modes_in, 1, from_z, from_y, sheet), source[...])
     for j in range(3):
         push = [along_stream(pressure, j), along_span(pressure[j]), along_height(pressure[j])]
         total = share[j]
@@ -512,6 +579,10 @@
     )(*args)
 
 
+def sheets(count):
+    return [pltpu.VMEM((NZ * count, NY), F32)]
+
+
 def exchange(rows, axis="space"):
     count = lax.axis_size(axis)
     wide = rows.reshape(count, 1, rows.size // count)
@@ -539,38 +610,41 @@
         prepare_kernel, [(9, *plane), (3, *plane), (5, *plane), plane],
         inflow_seeds, fluctuation, correction, rotor_cells.T, profile[None, :],
     )
+    rows = NZ * BLOCKS
+    symbols = jnp.asarray(SYMBOLS)
     buffer, first_trial, source, beside, laplace_start, viscosity = local_call(
         start_kernel,
-        [(SPACE * 3, NY), (15, *plane), plane, (2, *plane), (9, *plane), (7, *plane)],
+        [(rows, NY), (15, *plane), plane, (2, *plane), (9, *plane), (7, *plane)],
         inflow_seeds, inner, outer, state, viscosity, rotor, column, to_z, to_y,
+        scratch=sheets(3),
     )
     buffer = exchange(buffer)
     buffer, green = local_call(
-        solve_first_kernel, [(SPACE * 4, NY), (NX, NY)],
-        buffer, jnp.asarray(SQUARES), to_x, from_x,
+        solve_first_kernel, [(rows, NY), (NX, NY)],
+        buffer, symbols, to_x, from_x,
     )
     buffer = exchange(buffer)
     buffer, second_trial, source, laplace_mid = local_call(
         middle_kernel,
-        [(SPACE * 6, NY), (9, *plane), plane, (9, *plane)],
+        [(5 * SPACE, NY), (9, *plane), plane, (9, *plane)],
         buffer, first_trial, source, state, beside, viscosity, rotor, observed, column,
-        from_z, from_y, to_z, to_y,
+        from_z, from_y, to_z, to_y, scratch=sheets(6),
     )
     buffer = exchange(buffer)
     buffer = local_call(
-        solve_both_kernel, [(SPACE * 8, NY)],
-        buffer, green, jnp.asarray(SINE_X), jnp.asarray(TO_X_WIDE), jnp.asarray(FROM_X_WIDE),
+        solve_both_kernel, [(2 * rows, NY)],
+        buffer, green, symbols, jnp.asarray(TO_X_WIDE), jnp.asarray(FROM_X_WIDE),
     )
     buffer = exchange(buffer)
     buffer, fourth_trial, source, velocity, share = local_call(
         adjoint_kernel,
-        [(SPACE * 3, NY), (9, *plane), plane, (1, 3, 3, *plane), (3, *plane)],
+        [(rows, NY), (9, *plane), plane, (1, 3, 3, *plane), (3, *plane)],
         buffer, second_trial, source, laplace_mid, viscosity, rotor, observed, column,
-        from_z, from_y, to_z, to_y,
+        from_z, from_y, to_z, to_y, scratch=sheets(8),
     )
     buffer = exchange(buffer)
     buffer, velocity = local_call(
-        solve_last_kernel, [(SPACE * 4, NY), velocity.shape],
+        solve_last_kernel, [(rows, NY), velocity.shape],
         buffer, green, to_x, from_x, velocity,
         out_spaces={1: pltpu.HBM}, scratch=[pltpu.SemaphoreType.DMA],
     )
@@ -578,6 +652,7 @@
     terms = local_call(
         gradient_kernel, [(samples, SLAB * NZ, NY)],
         buffer, fourth_trial, source, laplace_start, viscosity, share, from_z, from_y,
+        scratch=sheets(4),
     )
     terms = lax.all_to_all(terms, "sample", 0, 0, tiled=True)
     gradient = jnp.sum(terms, axis=0).reshape(SLAB, *plane)

time: 147 us -> 145 us (0.986)
  blocking collectives: 123 us -> 120 us
    all_to_all x6, blocking collectives: 95.4 us -> 92.5 us  [exchange(): return lax.all_to_all(wide, axis, 0, 0, tiled=True).reshape(rows.shape)]
where the time goes in v6:
time: 145 us; the launch traced here: 144 us
  blocking collectives  120 us (83%)
  starting transfers between devices  10.7 us (7%)
  Pallas kernels  7.53 us (5%)
  waiting for transfers between devices  4.17 us (3%)
    all_to_all x6, blocking collectives, exchange(): return lax.all_to_all(wide, axis, 0, 0, tiled=True).reshape(rows.shape)  92.5 us
    all_to_all x1, blocking collectives, shards(): terms = lax.all_to_all(terms, 'sample', 0, 0, tiled=True)  27.3 us
    ppermute x1, starting transfers between devices, shards(): inner = lax.ppermute(inner, 'space', within)  8.77 us
    pallas_call x9, Pallas kernels, local_call(): pl.pallas_call(kernel, out_shape=shapes[0] if single else shapes, in_spec...  7.53 us
    ppermute x1, waiting for transfers between devices, shards(): outer = lax.ppermute(outer, 'space', between)  4.16 us
  transfers between devices with their start and end apart: 2, of which 1 were waited for; matrix products, arithmetic and copies ran while one was open for 0% of the time, Pallas kernels for 0%

profile of v6, /device:TPU:1, one launch (start us, length us, event | category | flops | bytes accessed | tf_op | source)
XLA Modules:
  0.0 144.3 jit_solution(1128093118500473577)
XLA Ops:
  0.6 1.1 pack_kernel.1
  1.8 8.8 %collective-permute-start = (f32[4,2,48,128]{3,2,1,0:T(8,128)S(1)}, f32[4,2,48,128]{3,2,1,0:T(8,128)S(1)}, u32[]{:S(2)}, u32[]{:S(2)}) collective-permute-start(f32[4,2,48,128]{3,2,1,0:T(8,128)S(1)} %get-tuple-element.27), channel_id=1, source_target_pairs={{0,1},{1,0},{2,3},{3,2},{4,5},{5,4},{6,7},{7,6},{8,9},{9,8},{10,11... | collective-permute-start | bytes 589832 | tf_op jit(solution)/shard_map/ppermute | solution.py:603
  10.6 1.9 %collective-permute-start.1 = (f32[4,2,48,128]{3,2,1,0:T(8,128)S(1)}, f32[4,2,48,128]{3,2,1,0:T(8,128)S(1)}, u32[]{:S(2)}, u32[]{:S(2)}) collective-permute-start(f32[4,2,48,128]{3,2,1,0:T(8,128)S(1)} %get-tuple-element.28), channel_id=1, source_target_pairs={{0,63},{1,2},{2,1},{3,4},{4,3},{5,6},{6,5},{7,8},{8,7},{9,10},{10,... | collective-permute-start | bytes 589832 | tf_op jit(solution)/shard_map/ppermute | solution.py:604
  12.5 0.6 copy-done.12
  13.1 0.0 copy-done.14
  13.2 0.2 prepare_kernel.1
  13.4 4.2 %collective-permute-done.1.outer = f32[4,2,48,128]{3,2,1,0:T(8,128)S(1)} collective-permute-done((f32[4,2,48,128]{3,2,1,0:T(8,128)S(1)}, f32[4,2,48,128]{3,2,1,0:T(8,128)S(1)}, u32[]{:S(2)}, u32[]{:S(2)}) %collective-permute-start.1) | collective-permute-done | bytes 196640 | tf_op jit(solution)/shard_map/ppermute | solution.py:604
  17.6 0.7 start_kernel.1
  18.3 17.0 %all_to_all.35 = f32[64,1,384]{2,1,0:T(1,128)S(1)} all-to-all(f32[64,1,384]{2,1,0:T(1,128)S(1)} %bitcast.24), channel_id=1, replica_groups=mesh['sample'=8,'space'=64] {'space'}, dimensions={0} | all-to-all | bytes 196608 | tf_op jit(solution)/shard_map/all_to_all | solution.py:589
  35.3 0.0 copy-start
  35.3 0.6 solve_first_kernel.1
  35.9 0.0 copy-start.7
  35.9 14.5 %all_to_all.36 = f32[64,1,384]{2,1,0:T(1,128)S(1)} all-to-all(f32[64,1,384]{2,1,0:T(1,128)S(1)} %bitcast.26), channel_id=1, replica_groups=mesh['sample'=8,'space'=64] {'space'}, dimensions={0} | all-to-all | bytes 196608 | tf_op jit(solution)/shard_map/all_to_all | solution.py:589
  50.4 1.3 middle_kernel.1
  51.7 14.9 %all_to_all.37 = f32[64,1,640]{2,1,0:T(1,128)S(1)} all-to-all(f32[64,1,640]{2,1,0:T(1,128)S(1)} %bitcast.22), channel_id=1, replica_groups=mesh['sample'=8,'space'=64] {'space'}, dimensions={0} | all-to-all | bytes 327680 | tf_op jit(solution)/shard_map/all_to_all | solution.py:589
  66.6 0.9 solve_both_kernel.1
  67.5 16.1 %all_to_all.38 = f32[64,1,768]{2,1,0:T(1,128)S(1)} all-to-all(f32[64,1,768]{2,1,0:T(1,128)S(1)} %bitcast.16), channel_id=1, replica_groups=mesh['sample'=8,'space'=64] {'space'}, dimensions={0} | all-to-all | bytes 393216 | tf_op jit(solution)/shard_map/all_to_all | solution.py:589
  83.6 1.4 adjoint_kernel.1
  85.0 15.7 %all_to_all.39 = f32[64,1,384]{2,1,0:T(1,128)S(1)} all-to-all(f32[64,1,384]{2,1,0:T(1,128)S(1)} %bitcast.23), channel_id=1, replica_groups=mesh['sample'=8,'space'=64] {'space'}, dimensions={0} | all-to-all | bytes 196608 | tf_op jit(solution)/shard_map/all_to_all | solution.py:589
  100.7 0.7 solve_last_kernel.1
  101.4 14.3 %all_to_all.40 = f32[64,1,384]{2,1,0:T(1,128)S(1)} all-to-all(f32[64,1,384]{2,1,0:T(1,128)S(1)} %bitcast.25), channel_id=1, replica_groups=mesh['sample'=8,'space'=64] {'space'}, dimensions={0} | all-to-all | bytes 196608 | tf_op jit(solution)/shard_map/all_to_all | solution.py:589
  115.7 0.6 gradient_kernel.1
  116.4 27.3 %all_to_all.41 = f32[8,144,128]{2,1,0:T(8,128)S(1)} all-to-all(f32[8,144,128]{2,1,0:T(8,128)S(1)} %gradient_kernel.1), channel_id=1, replica_groups=mesh['sample'=8,'space'=64] {'sample'}, dimensions={0} | all-to-all | bytes 1179648 | tf_op jit(solution)/shard_map/all_to_all | solution.py:657
  143.7 0.7 reduce_sum.9
  (27 shorter events, 0.1 us)
Async XLA Ops:
  0.6 11.9 %copy-start.9 = (f32[3,48,128]{2,1,0:T(8,128)S(1)}, f32[3,48,128]{2,1,0:T(8,128)}, u32[]{:S(2)}) copy-start(f32[3,48,128]{2,1,0:T(8,128)} %correction.3) | copy-start | bytes 221188
  0.6 11.9 %copy-start.3 = (f32[3,3,48,128]{3,2,1,0:T(8,128)S(1)}, f32[3,3,48,128]{3,2,1,0:T(8,128)}, u32[]{:S(2)}) copy-start(f32[3,3,48,128]{3,2,1,0:T(8,128)} %own.3) | copy-start | bytes 663556
  1.8 11.6 %collective-permute-start = (f32[4,2,48,128]{3,2,1,0:T(8,128)S(1)}, f32[4,2,48,128]{3,2,1,0:T(8,128)S(1)}, u32[]{:S(2)}, u32[]{:S(2)}) collective-permute-start(f32[4,2,48,128]{3,2,1,0:T(8,128)S(1)} %get-tuple-element.27), channel_id=1, source_target_pairs={{0,1},{1,0},{2,3},{3,2},{4,5},{5,4},{6,7},{7,6},{8,9},{9,8},{10,11... | collective-permute-start | bytes 589832 | tf_op jit(solution)/shard_map/ppermute | solution.py:603
  10.5 2.0 %copy-start.13 = (s32[64,3]{0,1:T(4,128)S(1)}, s32[64,3]{0,1:T(4,128)}, u32[]{:S(2)}) copy-start(s32[64,3]{0,1:T(4,128)} %param.16) | copy-start | bytes 2308
  10.6 7.0 %collective-permute-start.1 = (f32[4,2,48,128]{3,2,1,0:T(8,128)S(1)}, f32[4,2,48,128]{3,2,1,0:T(8,128)S(1)}, u32[]{:S(2)}, u32[]{:S(2)}) collective-permute-start(f32[4,2,48,128]{3,2,1,0:T(8,128)S(1)} %get-tuple-element.28), channel_id=1, source_target_pairs={{0,63},{1,2},{2,1},{3,4},{4,3},{5,6},{6,5},{7,8},{8,7},{9,10},{10,... | collective-permute-start | bytes 589832 | tf_op jit(solution)/shard_map/ppermute | solution.py:604
  12.5 0.7 copy-start.12
  12.5 0.7 copy-start.14
  13.2 4.4 %copy-start.2 = (bf16[256,256]{1,0:T(8,128)(2,1)S(1)}, bf16[256,256]{1,0:T(8,128)(2,1)}, u32[]{:S(2)}) copy-start(bf16[256,256]{1,0:T(8,128)(2,1)} %constant.22.clone.to_y) | copy-start | bytes 393220
  13.2 4.4 %copy-start.11 = (bf16[48,144]{1,0:T(8,128)(2,1)S(1)}, bf16[48,144]{1,0:T(8,128)(2,1)}, u32[]{:S(2)}) copy-start(bf16[48,144]{1,0:T(8,128)(2,1)} %constant.24.clone.to_z) | copy-start | bytes 41476
  17.6 17.7 %copy-start.1 = (bf16[256,768]{1,0:T(8,128)(2,1)S(1)}, bf16[256,768]{1,0:T(8,128)(2,1)}, u32[]{:S(2)}) copy-start(bf16[256,768]{1,0:T(8,128)(2,1)} %constant.21.clone.from_x) | copy-start | bytes 1179652
  17.6 17.7 %copy-start.6 = (f32[256,128]{1,0:T(8,128)S(1)}, f32[256,128]{1,0:T(8,128)}, u32[]{:S(2)}) copy-start(f32[256,128]{1,0:T(8,128)} %constant.26.clone.symbols) | copy-start | bytes 393220
  18.3 17.0 %copy-start.5 = (bf16[192,384]{1,0:T(8,128)(2,1)S(1)}, bf16[192,384]{1,0:T(8,128)(2,1)}, u32[]{:S(2)}) copy-start(bf16[192,384]{1,0:T(8,128)(2,1)} %constant.20.clone.to_x) | copy-start | bytes 442372
  35.3 15.1 %copy-start = (bf16[512,256]{1,0:T(8,128)(2,1)S(1)}, bf16[512,256]{1,0:T(8,128)(2,1)}, u32[]{:S(2)}) copy-start(bf16[512,256]{1,0:T(8,128)(2,1)} %constant.23.clone.from_y) | copy-start | bytes 786436
  35.9 14.5 %copy-start.7 = (bf16[48,288]{1,0:T(8,128)(2,1)S(1)}, bf16[48,288]{1,0:T(8,128)(2,1)}, u32[]{:S(2)}) copy-start(bf16[48,288]{1,0:T(8,128)(2,1)} %constant.25.clone.from_z) | copy-start | bytes 82948
  35.9 14.5 %copy-start.8 = (f32[3,48,128]{2,1,0:T(8,128)S(1)}, f32[3,48,128]{2,1,0:T(8,128)}, u32[]{:S(2)}) copy-start(f32[3,48,128]{2,1,0:T(8,128)} %observed.3) | copy-start | bytes 221188
  50.4 16.2 %copy-start.4 = (bf16[256,1152]{1,0:T(8,128)(2,1)S(1)}, bf16[256,1152]{1,0:T(8,128)(2,1)}, u32[]{:S(2)}) copy-start(bf16[256,1152]{1,0:T(8,128)(2,1)} %constant.28.clone.from_x) | copy-start | bytes 1769476
  51.7 14.9 %copy-start.10 = (bf16[192,576]{1,0:T(8,128)(2,1)S(1)}, bf16[192,576]{1,0:T(8,128)(2,1)}, u32[]{:S(2)}) copy-start(bf16[192,576]{1,0:T(8,128)(2,1)} %constant.27.clone.to_x) | copy-start | bytes 663556

commit v7 on v6

--- a/solution.py
+++ b/solution.py
@@ -92,8 +92,8 @@
 TO_X_WIDE = left_table(BASIS_X[stream_rows(0, 3)].T, 2)
 FROM_Y = right_table(BASIS_Y.T, 3)
 FROM_Z = left_table(BASIS_Z, 3)
-FROM_X = left_narrow_table(BASIS_X[stream_rows(0, 4)], 3)
-FROM_X_WIDE = left_table(BASIS_X[stream_rows(0, 4)], 3)
+FROM_X = left_narrow_table(BASIS_X[stream_rows(0, 3)], 3)
+FROM_X_WIDE = left_table(BASIS_X[stream_rows(0, 3)], 3)
 BLOCK = 32
 BLOCKS = NY // BLOCK
 UNITS = NZ * BLOCKS // SPACE
@@ -268,7 +268,8 @@
 def scatter_planes(out_ref, wide, groups):
     for g in range(groups):
         sheet = wide[:, NY * g : NY * (g + 1)]
-        planes = [sheet[SPACE * p : SPACE * (p + 1)] for p in range(4)]
+        planes = [sheet[SPACE * p : SPACE * (p + 1)] for p in range(SLAB)]
+        planes.append(pltpu.roll(planes[0], SPACE - 1, 0))
         for u in range(UNITS):
             row = jnp.where(block_of(planes[u]) == 3, move(planes[3], 3 - u), planes[u])
             out_ref[pl.ds(u * groups + g, SPACE, stride=UNITS * groups), :] = row
@@ -362,7 +363,7 @@
 
 
 def start_kernel(
-    seeds, inner, outer, own_state, own_viscosity, rotor, column, to_z, to_y,
+    seeds, outer, inner, own_state, own_viscosity, rotor, column, to_z, to_y,
     buffer, first_trial, source_out, beside_out, laplace_out, viscosity_out, sheet,
 ):
     even = lax.rem(lax.axis_index("space"), 2) == 0
@@ -615,7 +616,7 @@
     buffer, first_trial, source, beside, laplace_start, viscosity = local_call(
         start_kernel,
         [(rows, NY), (15, *plane), plane, (2, *plane), (9, *plane), (7, *plane)],
-        inflow_seeds, inner, outer, state, viscosity, rotor, column, to_z, to_y,
+        inflow_seeds, outer, inner, state, viscosity, rotor, column, to_z, to_y,
         scratch=sheets(3),
     )
     buffer = exchange(buffer)

time: 145 us -> 143 us (0.986)
  waiting for transfers between devices: 4.17 us -> 0.15 us
    ppermute x1, waiting for transfers between devices: 4.16 us -> 0.01 us  [shards(): outer = lax.ppermute(outer, 'space', between)]
    ppermute x1, starting transfers between devices: 8.77 us -> 6.11 us  [shards(): inner = lax.ppermute(inner, 'space', within)]
    ppermute x1, starting transfers between devices: 1.92 us -> 4.58 us  [shards(): outer = lax.ppermute(outer, 'space', between)]
    all_to_all x6, blocking collectives: 92.5 us -> 94 us  [exchange(): return lax.all_to_all(wide, axis, 0, 0, tiled=True).reshape(rows.shape)]
where the time goes in v7:
time: 143 us; the launch traced here: 142 us
  blocking collectives  121 us (85%)
  starting transfers between devices  10.7 us (7%)
  Pallas kernels  7.4 us (5%)
    all_to_all x6, blocking collectives, exchange(): return lax.all_to_all(wide, axis, 0, 0, tiled=True).reshape(rows.shape)  94 us
    all_to_all x1, blocking collectives, shards(): terms = lax.all_to_all(terms, 'sample', 0, 0, tiled=True)  27.3 us
    pallas_call x9, Pallas kernels, local_call(): pl.pallas_call(kernel, out_shape=shapes[0] if single else shapes, in_spec...  7.4 us
    ppermute x1, starting transfers between devices, shards(): inner = lax.ppermute(inner, 'space', within)  6.11 us
    ppermute x1, starting transfers between devices, shards(): outer = lax.ppermute(outer, 'space', between)  4.58 us
  transfers between devices with their start and end apart: 2, of which 1 were waited for; matrix products, arithmetic and copies ran while one was open for 0% of the time, Pallas kernels for 0%

profile of v7, /device:TPU:1, one launch (start us, length us, event | category | flops | bytes accessed | tf_op | source)
XLA Modules:
  0.0 142.3 jit_solution(12312679057203470510)
XLA Ops:
  0.6 1.1 pack_kernel.1
  1.8 4.6 %collective-permute-start = (f32[4,2,48,128]{3,2,1,0:T(8,128)S(1)}, f32[4,2,48,128]{3,2,1,0:T(8,128)S(1)}, u32[]{:S(2)}, u32[]{:S(2)}) collective-permute-start(f32[4,2,48,128]{3,2,1,0:T(8,128)S(1)} %get-tuple-element.27), channel_id=1, source_target_pairs={{0,63},{1,2},{2,1},{3,4},{4,3},{5,6},{6,5},{7,8},{8,7},{9,10},{10,... | collective-permute-start | bytes 589832 | tf_op jit(solution)/shard_map/ppermute | solution.py:605
  6.4 6.1 %collective-permute-start.1 = (f32[4,2,48,128]{3,2,1,0:T(8,128)S(1)}, f32[4,2,48,128]{3,2,1,0:T(8,128)S(1)}, u32[]{:S(2)}, u32[]{:S(2)}) collective-permute-start(f32[4,2,48,128]{3,2,1,0:T(8,128)S(1)} %get-tuple-element.28), channel_id=1, source_target_pairs={{0,1},{1,0},{2,3},{3,2},{4,5},{5,4},{6,7},{7,6},{8,9},{9,8},{10,11... | collective-permute-start | bytes 589832 | tf_op jit(solution)/shard_map/ppermute | solution.py:604
  12.5 0.6 copy-done.12
  13.1 0.0 copy-done.14
  13.2 0.2 prepare_kernel.1
  13.4 0.2 collective-permute-done.1.inner
  13.5 0.5 copy-done.1
  14.1 0.7 start_kernel.1
  14.8 18.6 %all_to_all.35 = f32[64,1,384]{2,1,0:T(1,128)S(1)} all-to-all(f32[64,1,384]{2,1,0:T(1,128)S(1)} %bitcast.24), channel_id=1, replica_groups=mesh['sample'=8,'space'=64] {'space'}, dimensions={0} | all-to-all | bytes 196608 | tf_op jit(solution)/shard_map/all_to_all | solution.py:590
  33.4 0.0 copy-start
  33.4 0.5 solve_first_kernel.1
  33.9 14.5 %all_to_all.36 = f32[64,1,384]{2,1,0:T(1,128)S(1)} all-to-all(f32[64,1,384]{2,1,0:T(1,128)S(1)} %bitcast.26), channel_id=1, replica_groups=mesh['sample'=8,'space'=64] {'space'}, dimensions={0} | all-to-all | bytes 196608 | tf_op jit(solution)/shard_map/all_to_all | solution.py:590
  48.4 1.3 middle_kernel.1
  49.7 14.9 %all_to_all.37 = f32[64,1,640]{2,1,0:T(1,128)S(1)} all-to-all(f32[64,1,640]{2,1,0:T(1,128)S(1)} %bitcast.22), channel_id=1, replica_groups=mesh['sample'=8,'space'=64] {'space'}, dimensions={0} | all-to-all | bytes 327680 | tf_op jit(solution)/shard_map/all_to_all | solution.py:590
  64.6 0.8 solve_both_kernel.1
  65.5 16.1 %all_to_all.38 = f32[64,1,768]{2,1,0:T(1,128)S(1)} all-to-all(f32[64,1,768]{2,1,0:T(1,128)S(1)} %bitcast.15), channel_id=1, replica_groups=mesh['sample'=8,'space'=64] {'space'}, dimensions={0} | all-to-all | bytes 393216 | tf_op jit(solution)/shard_map/all_to_all | solution.py:590
  81.6 1.4 adjoint_kernel.1
  83.0 15.7 %all_to_all.39 = f32[64,1,384]{2,1,0:T(1,128)S(1)} all-to-all(f32[64,1,384]{2,1,0:T(1,128)S(1)} %bitcast.23), channel_id=1, replica_groups=mesh['sample'=8,'space'=64] {'space'}, dimensions={0} | all-to-all | bytes 196608 | tf_op jit(solution)/shard_map/all_to_all | solution.py:590
  98.6 0.7 solve_last_kernel.1
  99.4 14.3 %all_to_all.40 = f32[64,1,384]{2,1,0:T(1,128)S(1)} all-to-all(f32[64,1,384]{2,1,0:T(1,128)S(1)} %bitcast.25), channel_id=1, replica_groups=mesh['sample'=8,'space'=64] {'space'}, dimensions={0} | all-to-all | bytes 196608 | tf_op jit(solution)/shard_map/all_to_all | solution.py:590
  113.7 0.6 gradient_kernel.1
  114.3 27.3 %all_to_all.41 = f32[8,144,128]{2,1,0:T(8,128)S(1)} all-to-all(f32[8,144,128]{2,1,0:T(8,128)S(1)} %gradient_kernel.1), channel_id=1, replica_groups=mesh['sample'=8,'space'=64] {'sample'}, dimensions={0} | all-to-all | bytes 1179648 | tf_op jit(solution)/shard_map/all_to_all | solution.py:658
  141.6 0.7 reduce_sum.9
  (27 shorter events, 0.1 us)
Async XLA Ops:
  0.6 11.9 %copy-start.9 = (f32[3,48,128]{2,1,0:T(8,128)S(1)}, f32[3,48,128]{2,1,0:T(8,128)}, u32[]{:S(2)}) copy-start(f32[3,48,128]{2,1,0:T(8,128)} %correction.3) | copy-start | bytes 221188
  0.6 11.9 %copy-start.3 = (f32[3,3,48,128]{3,2,1,0:T(8,128)S(1)}, f32[3,3,48,128]{3,2,1,0:T(8,128)}, u32[]{:S(2)}) copy-start(f32[3,3,48,128]{3,2,1,0:T(8,128)} %own.3) | copy-start | bytes 663556
  1.8 11.6 %collective-permute-start = (f32[4,2,48,128]{3,2,1,0:T(8,128)S(1)}, f32[4,2,48,128]{3,2,1,0:T(8,128)S(1)}, u32[]{:S(2)}, u32[]{:S(2)}) collective-permute-start(f32[4,2,48,128]{3,2,1,0:T(8,128)S(1)} %get-tuple-element.27), channel_id=1, source_target_pairs={{0,63},{1,2},{2,1},{3,4},{4,3},{5,6},{6,5},{7,8},{8,7},{9,10},{10,... | collective-permute-start | bytes 589832 | tf_op jit(solution)/shard_map/ppermute | solution.py:605
  6.4 6.2 %copy-start.13 = (s32[64,3]{0,1:T(4,128)S(1)}, s32[64,3]{0,1:T(4,128)}, u32[]{:S(2)}) copy-start(s32[64,3]{0,1:T(4,128)} %param.16) | copy-start | bytes 2308
  6.4 7.2 %collective-permute-start.1 = (f32[4,2,48,128]{3,2,1,0:T(8,128)S(1)}, f32[4,2,48,128]{3,2,1,0:T(8,128)S(1)}, u32[]{:S(2)}, u32[]{:S(2)}) collective-permute-start(f32[4,2,48,128]{3,2,1,0:T(8,128)S(1)} %get-tuple-element.28), channel_id=1, source_target_pairs={{0,1},{1,0},{2,3},{3,2},{4,5},{5,4},{6,7},{7,6},{8,9},{9,8},{10,11... | collective-permute-start | bytes 589832 | tf_op jit(solution)/shard_map/ppermute | solution.py:604
  12.5 0.7 copy-start.12
  12.5 0.7 copy-start.14
  13.2 0.9 copy-start.1
  13.2 0.9 copy-start.11
  14.1 19.3 %copy-start.2 = (bf16[192,768]{1,0:T(8,128)(2,1)S(1)}, bf16[192,768]{1,0:T(8,128)(2,1)}, u32[]{:S(2)}) copy-start(bf16[192,768]{1,0:T(8,128)(2,1)} %constant.21.clone.from_x) | copy-start | bytes 884740
  14.1 19.3 %copy-start.5 = (f32[256,128]{1,0:T(8,128)S(1)}, f32[256,128]{1,0:T(8,128)}, u32[]{:S(2)}) copy-start(f32[256,128]{1,0:T(8,128)} %constant.26.clone.symbols) | copy-start | bytes 393220
  14.8 18.6 %copy-start.4 = (bf16[192,384]{1,0:T(8,128)(2,1)S(1)}, bf16[192,384]{1,0:T(8,128)(2,1)}, u32[]{:S(2)}) copy-start(bf16[192,384]{1,0:T(8,128)(2,1)} %constant.20.clone.to_x) | copy-start | bytes 442372
  33.4 15.0 %copy-start = (bf16[512,256]{1,0:T(8,128)(2,1)S(1)}, bf16[512,256]{1,0:T(8,128)(2,1)}, u32[]{:S(2)}) copy-start(bf16[512,256]{1,0:T(8,128)(2,1)} %constant.23.clone.from_y) | copy-start | bytes 786436
  33.9 14.5 %copy-start.7 = (bf16[48,288]{1,0:T(8,128)(2,1)S(1)}, bf16[48,288]{1,0:T(8,128)(2,1)}, u32[]{:S(2)}) copy-start(bf16[48,288]{1,0:T(8,128)(2,1)} %constant.25.clone.from_z) | copy-start | bytes 82948
  33.9 14.5 %copy-start.8 = (f32[3,48,128]{2,1,0:T(8,128)S(1)}, f32[3,48,128]{2,1,0:T(8,128)}, u32[]{:S(2)}) copy-start(f32[3,48,128]{2,1,0:T(8,128)} %observed.3) | copy-start | bytes 221188
  48.4 16.2 %copy-start.6 = (bf16[192,1152]{1,0:T(8,128)(2,1)S(1)}, bf16[192,1152]{1,0:T(8,128)(2,1)}, u32[]{:S(2)}) copy-start(bf16[192,1152]{1,0:T(8,128)(2,1)} %constant.28.clone.from_x) | copy-start | bytes 1327108
  49.7 14.9 %copy-start.10 = (bf16[192,576]{1,0:T(8,128)(2,1)S(1)}, bf16[192,576]{1,0:T(8,128)(2,1)}, u32[]{:S(2)}) copy-start(bf16[192,576]{1,0:T(8,128)(2,1)} %constant.27.clone.to_x) | copy-start | bytes 663556

commit v8 on v7

--- a/solution.py
+++ b/solution.py
@@ -174,10 +174,12 @@
     return 0.5 * (planes[j + 1] - planes[j - 1])
 
 
+def flat_laplace(f):
+    return up_z(f) + down_z(f) + up_y(f) + down_y(f) - 6.0 * f
+
+
 def laplace(planes, j):
-    f = planes[j]
-    summed = planes[j + 1] + planes[j - 1] + up_z(f) + down_z(f) + up_y(f) + down_y(f)
-    return summed - 6.0 * f
+    return planes[j + 1] + planes[j - 1] + flat_laplace(planes[j])
 
 
 def cross_laplace(f):
@@ -249,10 +251,11 @@
         for j in range(UNITS):
             fourth = jnp.where(block == j, move(units[j], j + 1), fourth)
         sheet_ref[NZ * (4 * g + 3) : NZ * (4 * g + 4), :] = fourth
-    rows = right_product(sheet_ref[: NZ * count, :], from_y, 3)
-    side = jnp.concatenate([rows[NZ * i : NZ * (i + 1)] for i in range(count)], axis=1)
+    side = jnp.concatenate([sheet_ref[NZ * i : NZ * (i + 1), :] for i in range(count)], axis=1)
     side = left_product(from_z, side, 3)
-    return [side[:, NY * i : NY * (i + 1)] for i in range(count)]
+    rows = jnp.concatenate([side[:, NY * i : NY * (i + 1)] for i in range(count)], axis=0)
+    rows = right_product(rows, from_y, 3)
+    return [rows[NZ * i : NZ * (i + 1)] for i in range(count)]
 
 
 def gather_planes(in_ref, width):
@@ -346,24 +349,42 @@
     return row[0, 0], row[0, 1]
 
 
+def trial_terms(state, flat, viscosity, rotor):
+    return state + TIME_STEP * (viscosity * flat - rotor * state)
+
+
+def stream_terms(viscosity, profile):
+    return TIME_STEP * (viscosity - 0.5 * profile), TIME_STEP * (viscosity + 0.5 * profile)
+
+
 def prepare_kernel(
-    seeds, own, correction, cells, heights, state_out, viscosity_out, rotor_out, column_out
+    seeds, own, correction, cells, heights,
+    state_out, flat_out, part_out, stream_out, viscosity_out, rotor_out, column_out,
 ):
     shifts = shifts_of(seeds)
     profile = spread_profile(heights[...])
     column_out[...] = profile
     rotor = count_rotors(cells)
     for j in range(5):
+        rotor[j] = THRUST * rotor[j]
         rotor_out[j] = rotor[j]
     for j in range(3):
-        viscosity_out[j] = BASE_VISCOSITY * jnp.exp(correction[j])
+        viscosity = BASE_VISCOSITY * jnp.exp(correction[j])
+        viscosity_out[j] = viscosity
+        stream_out[0, j], stream_out[1, j] = stream_terms(viscosity, profile)
         for c in range(3):
-            plane = rolled(own[c, j], shifts)
-            state_out[3 * c + j] = plane + profile if c == 0 else plane
+            state = rolled(own[c, j], shifts)
+            if c == 0:
+                state = state + profile
+            flat = flat_laplace(state)
+            state_out[3 * c + j] = state
+            flat_out[3 * c + j] = flat
+            part_out[3 * c + j] = trial_terms(state, flat, viscosity, rotor[j + 1])
 
 
 def start_kernel(
-    seeds, outer, inner, own_state, own_viscosity, rotor, column, to_z, to_y,
+    seeds, outer, inner, own_state, own_flat, own_part, own_stream, own_viscosity, rotor, column,
+    to_z, to_y,
     buffer, first_trial, source_out, beside_out, laplace_out, viscosity_out, sheet,
 ):
     even = lax.rem(lax.axis_index("space"), 2) == 0
@@ -376,35 +397,33 @@
         high = inner if j < 0 else outer
         return jnp.where(even, low[c, i], high[c, i])
 
-    viscosity = {}
-    for j in range(-2, 5):
-        if 0 <= j < 3:
-            viscosity[j] = own_viscosity[j]
-        else:
-            viscosity[j] = BASE_VISCOSITY * jnp.exp(halo(j, 3))
-        viscosity_out[j + 2] = viscosity[j]
+    stream = {j: (own_stream[0, j], own_stream[1, j]) for j in range(3)}
+    beside = {}
+    for j in (-2, -1, 3, 4):
+        viscosity = BASE_VISCOSITY * jnp.exp(halo(j, 3))
+        viscosity_out[j + 2] = viscosity
+        if j in (-1, 3):
+            beside[j] = viscosity
+            stream[j] = stream_terms(viscosity, profile)
+    for j in range(3):
+        viscosity_out[j + 2] = own_viscosity[j]
     trial = []
     for c in range(3):
-        state = {}
-        for j in range(-2, 5):
-            if 0 <= j < 3:
-                state[j] = own_state[3 * c + j]
-            else:
-                state[j] = rolled(halo(j, c), shifts)
-                if c == 0:
-                    state[j] = state[j] + profile
+        state = {j: own_state[3 * c + j] for j in range(3)}
+        for j in (-2, -1, 3, 4):
+            state[j] = rolled(halo(j, c), shifts)
+            if c == 0:
+                state[j] = state[j] + profile
         moved = {}
         for j in range(-1, 4):
-            curvature = laplace(state, j)
-            forcing = (
-                viscosity[j] * curvature
-                - profile * along_stream(state, j)
-                - THRUST * rotor[j + 1] * state[j]
-            )
-            moved[j] = state[j] + TIME_STEP * forcing
-            first_trial[5 * c + j + 1] = moved[j]
             if 0 <= j < 3:
-                laplace_out[3 * c + j] = curvature
+                part = own_part[3 * c + j]
+                laplace_out[3 * c + j] = own_flat[3 * c + j] + (state[j + 1] + state[j - 1])
+            else:
+                part = trial_terms(state[j], flat_laplace(state[j]), beside[j], rotor[j + 1])
+            moved[j] = part + stream[j][0] * state[j + 1] + stream[j][1] * state[j - 1]
+            if c > 0 or 0 <= j < 3:
+                first_trial[5 * c + j + 1] = moved[j]
         trial.append(moved)
         if c == 0:
             beside_out[0] = state[-1]
@@ -467,7 +486,7 @@
             forcing = (
                 viscosity[j + 2] * curvature
                 - profile * along_stream(middle, j)
-                - THRUST * rotor[j + 1] * middle[j]
+                - rotor[j + 1] * middle[j]
             )
             moved[j] = 0.5 * start + 0.5 * (middle[j] + TIME_STEP * forcing)
             if 0 <= j < 3:
@@ -531,7 +550,7 @@
             pulled = (
                 profile * along_stream(adjoint, j)
                 + laplace(spread, j)
-                - THRUST * rotor[j + 1] * adjoint[j]
+                - rotor[j + 1] * adjoint[j]
             )
             moved[j] = 0.5 * adjoint[j] + 0.5 * TIME_STEP * pulled
         for j in range(3):
@@ -607,8 +626,12 @@
     to_y, from_y = jnp.asarray(TO_Y), jnp.asarray(FROM_Y)
     to_z, from_z = jnp.asarray(TO_Z), jnp.asarray(FROM_Z)
 
-    state, viscosity, rotor, column = local_call(
-        prepare_kernel, [(9, *plane), (3, *plane), (5, *plane), plane],
+    state, flat, part, stream, viscosity, rotor, column = local_call(
+        prepare_kernel,
+        [
+            (9, *plane), (9, *plane), (9, *plane), (2, 3, *plane), (3, *plane), (5, *plane),
+            plane,
+        ],
         inflow_seeds, fluctuation, correction, rotor_cells.T, profile[None, :],
     )
     rows = NZ * BLOCKS
@@ -616,7 +639,8 @@
     buffer, first_trial, source, beside, laplace_start, viscosity = local_call(
         start_kernel,
         [(rows, NY), (15, *plane), plane, (2, *plane), (9, *plane), (7, *plane)],
-        inflow_seeds, outer, inner, state, viscosity, rotor, column, to_z, to_y,
+        inflow_seeds, outer, inner, state, flat, part, stream, viscosity, rotor, column,
+        to_z, to_y,
         scratch=sheets(3),
     )
     buffer = exchange(buffer)

time: 143 us -> 143 us (level)
  transfers between devices with their start and end apart: 2 -> 2, of which waited for: 1 -> 0; matrix products, arithmetic and copies ran while one was open for 0% -> 0% of each run, Pallas kernels for 0% -> 0%
where the time goes in v8:
time: 143 us; the launch traced here: 142 us
  blocking collectives  121 us (85%)
  starting transfers between devices  10.7 us (7%)
  Pallas kernels  7.38 us (5%)
    all_to_all x6, blocking collectives, exchange(): return lax.all_to_all(wide, axis, 0, 0, tiled=True).reshape(rows.shape)  94 us
    all_to_all x1, blocking collectives, shards(): terms = lax.all_to_all(terms, 'sample', 0, 0, tiled=True)  27.3 us
    pallas_call x9, Pallas kernels, local_call(): pl.pallas_call(kernel, out_shape=shapes[0] if single else shapes, in_spec...  7.38 us
    ppermute x1, starting transfers between devices, shards(): inner = lax.ppermute(inner, 'space', within)  6.11 us
    ppermute x1, starting transfers between devices, shards(): outer = lax.ppermute(outer, 'space', between)  4.58 us
  transfers between devices with their start and end apart: 2, of which 0 were waited for; matrix products, arithmetic and copies ran while one was open for 0% of the time, Pallas kernels for 0%

profile of v8, /device:TPU:1, one launch (start us, length us, event | category | flops | bytes accessed | tf_op | source)
XLA Modules:
  0.0 142.1 jit_solution(18271695335481349565)
XLA Ops:
  0.6 1.1 pack_kernel.1
  1.8 4.6 %collective-permute-start = (f32[4,2,48,128]{3,2,1,0:T(8,128)S(1)}, f32[4,2,48,128]{3,2,1,0:T(8,128)S(1)}, u32[]{:S(2)}, u32[]{:S(2)}) collective-permute-start(f32[4,2,48,128]{3,2,1,0:T(8,128)S(1)} %get-tuple-element.30), channel_id=1, source_target_pairs={{0,63},{1,2},{2,1},{3,4},{4,3},{5,6},{6,5},{7,8},{8,7},{9,10},{10,... | collective-permute-start | bytes 589832 | tf_op jit(solution)/shard_map/ppermute | solution.py:624
  6.4 6.1 %collective-permute-start.1 = (f32[4,2,48,128]{3,2,1,0:T(8,128)S(1)}, f32[4,2,48,128]{3,2,1,0:T(8,128)S(1)}, u32[]{:S(2)}, u32[]{:S(2)}) collective-permute-start(f32[4,2,48,128]{3,2,1,0:T(8,128)S(1)} %get-tuple-element.31), channel_id=1, source_target_pairs={{0,1},{1,0},{2,3},{3,2},{4,5},{5,4},{6,7},{7,6},{8,9},{9,8},{10,11... | collective-permute-start | bytes 589832 | tf_op jit(solution)/shard_map/ppermute | solution.py:623
  12.5 0.6 copy-done.13
  13.1 0.0 copy-done.14
  13.2 0.4 prepare_kernel.1
  13.6 0.5 copy-done.1
  14.1 0.6 start_kernel.1
  14.7 18.6 %all_to_all.35 = f32[64,1,384]{2,1,0:T(1,128)S(1)} all-to-all(f32[64,1,384]{2,1,0:T(1,128)S(1)} %bitcast.24), channel_id=1, replica_groups=mesh['sample'=8,'space'=64] {'space'}, dimensions={0} | all-to-all | bytes 196608 | tf_op jit(solution)/shard_map/all_to_all | solution.py:609
  33.3 0.0 copy-start
  33.3 0.5 solve_first_kernel.1
  33.8 0.0 copy-start.7
  33.9 14.5 %all_to_all.36 = f32[64,1,384]{2,1,0:T(1,128)S(1)} all-to-all(f32[64,1,384]{2,1,0:T(1,128)S(1)} %bitcast.26), channel_id=1, replica_groups=mesh['sample'=8,'space'=64] {'space'}, dimensions={0} | all-to-all | bytes 196608 | tf_op jit(solution)/shard_map/all_to_all | solution.py:609
  48.4 1.3 middle_kernel.1
  49.7 14.9 %all_to_all.37 = f32[64,1,640]{2,1,0:T(1,128)S(1)} all-to-all(f32[64,1,640]{2,1,0:T(1,128)S(1)} %bitcast.22), channel_id=1, replica_groups=mesh['sample'=8,'space'=64] {'space'}, dimensions={0} | all-to-all | bytes 327680 | tf_op jit(solution)/shard_map/all_to_all | solution.py:609
  64.6 0.8 solve_both_kernel.1
  65.4 16.1 %all_to_all.38 = f32[64,1,768]{2,1,0:T(1,128)S(1)} all-to-all(f32[64,1,768]{2,1,0:T(1,128)S(1)} %bitcast.15), channel_id=1, replica_groups=mesh['sample'=8,'space'=64] {'space'}, dimensions={0} | all-to-all | bytes 393216 | tf_op jit(solution)/shard_map/all_to_all | solution.py:609
  81.5 1.3 adjoint_kernel.1
  82.8 15.7 %all_to_all.39 = f32[64,1,384]{2,1,0:T(1,128)S(1)} all-to-all(f32[64,1,384]{2,1,0:T(1,128)S(1)} %bitcast.23), channel_id=1, replica_groups=mesh['sample'=8,'space'=64] {'space'}, dimensions={0} | all-to-all | bytes 196608 | tf_op jit(solution)/shard_map/all_to_all | solution.py:609
  98.5 0.7 solve_last_kernel.1
  99.2 14.3 %all_to_all.40 = f32[64,1,384]{2,1,0:T(1,128)S(1)} all-to-all(f32[64,1,384]{2,1,0:T(1,128)S(1)} %bitcast.25), channel_id=1, replica_groups=mesh['sample'=8,'space'=64] {'space'}, dimensions={0} | all-to-all | bytes 196608 | tf_op jit(solution)/shard_map/all_to_all | solution.py:609
  113.5 0.6 gradient_kernel.1
  114.1 27.3 %all_to_all.41 = f32[8,144,128]{2,1,0:T(8,128)S(1)} all-to-all(f32[8,144,128]{2,1,0:T(8,128)S(1)} %gradient_kernel.1), channel_id=1, replica_groups=mesh['sample'=8,'space'=64] {'sample'}, dimensions={0} | all-to-all | bytes 1179648 | tf_op jit(solution)/shard_map/all_to_all | solution.py:682
  141.4 0.7 reduce_sum.9
  (27 shorter events, 0.1 us)
Async XLA Ops:
  0.6 11.9 %copy-start.9 = (f32[3,48,128]{2,1,0:T(8,128)S(1)}, f32[3,48,128]{2,1,0:T(8,128)}, u32[]{:S(2)}) copy-start(f32[3,48,128]{2,1,0:T(8,128)} %correction.3) | copy-start | bytes 221188
  0.6 11.9 %copy-start.3 = (f32[3,3,48,128]{3,2,1,0:T(8,128)S(1)}, f32[3,3,48,128]{3,2,1,0:T(8,128)}, u32[]{:S(2)}) copy-start(f32[3,3,48,128]{3,2,1,0:T(8,128)} %own.3) | copy-start | bytes 663556
  1.8 11.8 %collective-permute-start = (f32[4,2,48,128]{3,2,1,0:T(8,128)S(1)}, f32[4,2,48,128]{3,2,1,0:T(8,128)S(1)}, u32[]{:S(2)}, u32[]{:S(2)}) collective-permute-start(f32[4,2,48,128]{3,2,1,0:T(8,128)S(1)} %get-tuple-element.30), channel_id=1, source_target_pairs={{0,63},{1,2},{2,1},{3,4},{4,3},{5,6},{6,5},{7,8},{8,7},{9,10},{10,... | collective-permute-start | bytes 589832 | tf_op jit(solution)/shard_map/ppermute | solution.py:624
  6.4 6.2 %copy-start.12 = (s32[64,3]{0,1:T(4,128)S(1)}, s32[64,3]{0,1:T(4,128)}, u32[]{:S(2)}) copy-start(s32[64,3]{0,1:T(4,128)} %param.16) | copy-start | bytes 2308
  6.4 7.2 %collective-permute-start.1 = (f32[4,2,48,128]{3,2,1,0:T(8,128)S(1)}, f32[4,2,48,128]{3,2,1,0:T(8,128)S(1)}, u32[]{:S(2)}, u32[]{:S(2)}) collective-permute-start(f32[4,2,48,128]{3,2,1,0:T(8,128)S(1)} %get-tuple-element.31), channel_id=1, source_target_pairs={{0,1},{1,0},{2,3},{3,2},{4,5},{5,4},{6,7},{7,6},{8,9},{9,8},{10,11... | collective-permute-start | bytes 589832 | tf_op jit(solution)/shard_map/ppermute | solution.py:623
  12.5 0.7 copy-start.13
  12.5 0.7 copy-start.14
  13.2 0.9 copy-start.1
  13.2 0.9 copy-start.11
  14.1 19.2 %copy-start.2 = (bf16[192,768]{1,0:T(8,128)(2,1)S(1)}, bf16[192,768]{1,0:T(8,128)(2,1)}, u32[]{:S(2)}) copy-start(bf16[192,768]{1,0:T(8,128)(2,1)} %constant.21.clone.from_x) | copy-start | bytes 884740
  14.1 19.2 %copy-start.5 = (f32[256,128]{1,0:T(8,128)S(1)}, f32[256,128]{1,0:T(8,128)}, u32[]{:S(2)}) copy-start(f32[256,128]{1,0:T(8,128)} %constant.26.clone.symbols) | copy-start | bytes 393220
  14.7 18.6 %copy-start.4 = (bf16[192,384]{1,0:T(8,128)(2,1)S(1)}, bf16[192,384]{1,0:T(8,128)(2,1)}, u32[]{:S(2)}) copy-start(bf16[192,384]{1,0:T(8,128)(2,1)} %constant.20.clone.to_x) | copy-start | bytes 442372
  33.3 15.0 %copy-start = (bf16[512,256]{1,0:T(8,128)(2,1)S(1)}, bf16[512,256]{1,0:T(8,128)(2,1)}, u32[]{:S(2)}) copy-start(bf16[512,256]{1,0:T(8,128)(2,1)} %constant.23.clone.from_y) | copy-start | bytes 786436
  33.8 14.5 %copy-start.7 = (bf16[48,288]{1,0:T(8,128)(2,1)S(1)}, bf16[48,288]{1,0:T(8,128)(2,1)}, u32[]{:S(2)}) copy-start(bf16[48,288]{1,0:T(8,128)(2,1)} %constant.25.clone.from_z) | copy-start | bytes 82948
  33.8 14.5 %copy-start.8 = (f32[3,48,128]{2,1,0:T(8,128)S(1)}, f32[3,48,128]{2,1,0:T(8,128)}, u32[]{:S(2)}) copy-start(f32[3,48,128]{2,1,0:T(8,128)} %observed.3) | copy-start | bytes 221188
  48.3 16.2 %copy-start.6 = (bf16[192,1152]{1,0:T(8,128)(2,1)S(1)}, bf16[192,1152]{1,0:T(8,128)(2,1)}, u32[]{:S(2)}) copy-start(bf16[192,1152]{1,0:T(8,128)(2,1)} %constant.28.clone.from_x) | copy-start | bytes 1327108
  49.7 14.9 %copy-start.10 = (bf16[192,576]{1,0:T(8,128)(2,1)S(1)}, bf16[192,576]{1,0:T(8,128)(2,1)}, u32[]{:S(2)}) copy-start(bf16[192,576]{1,0:T(8,128)(2,1)} %constant.27.clone.to_x) | copy-start | bytes 663556

commit v9 on v8

--- a/solution.py
+++ b/solution.py
@@ -88,7 +88,8 @@
 
 TO_Y = right_table(BASIS_Y, 2)
 TO_Z = left_table(BASIS_Z.T, 2)
-TO_X = left_narrow_table(BASIS_X[stream_rows(0, 3)].T, 2)
+EDGE_ROWS = np.where(np.arange(SPACE) % 2 == 0, stream_rows(-1, 1), stream_rows(3, 1))
+TO_X = left_narrow_table(BASIS_X[np.concatenate([stream_rows(0, 3), EDGE_ROWS])].T, 2)
 TO_X_WIDE = left_table(BASIS_X[stream_rows(0, 3)].T, 2)
 FROM_Y = right_table(BASIS_Y.T, 3)
 FROM_Z = left_table(BASIS_Z, 3)
@@ -124,7 +125,9 @@
 
 def left_product(table, value, count):
     parts = split(value, count)
-    return dot(table[...], jnp.concatenate([parts[k] for _, k in pairs_of(count)], axis=0))
+    wide = jnp.concatenate([parts[k] for _, k in pairs_of(count)], axis=0)
+    columns = range(0, wide.shape[1], NY)
+    return jnp.concatenate([dot(table[...], wide[:, i : i + NY]) for i in columns], axis=1)
 
 
 def left_narrow_product(table, value, count):
@@ -172,6 +175,15 @@
 
 def along_stream(planes, j):
     return 0.5 * (planes[j + 1] - planes[j - 1])
+
+
+def without_edge(planes, even):
+    planes[-1] = jnp.where(even, 0.0, planes[-1])
+    planes[3] = jnp.where(even, planes[3], 0.0)
+
+
+def edge_term(planes, even):
+    return jnp.where(even, 0.5 * planes[0], -0.5 * planes[2])
 
 
 def flat_laplace(f):
@@ -260,8 +272,6 @@
 
 def gather_planes(in_ref, width):
     rows = [in_ref[pl.ds(i, SPACE, stride=width), :] for i in range(width)]
-    if width == UNITS:
-        return rows
     block = block_of(rows[0])
     fourth = jnp.where(block == 0, move(rows[0], 1), move(rows[2], 3))
     fourth = jnp.where(block == 1, move(rows[1], 2), fourth)
@@ -311,21 +321,29 @@
     return jnp.broadcast_to(column, (NZ, NY))
 
 
-def pack_kernel(own, correction, inner, outer, arrived):
+def pack_kernel(
+    own, correction, seeds, cells, heights, inner, outer, seeds_out, cells_out, heights_out, arrived
+):
     even = lax.rem(lax.axis_index("space"), 2) == 0
 
     def fill(first, last):
         copies = []
-        for i, (target, start) in enumerate(((last, 1), (first, 0))):
+
+        def add(source, target):
+            copies.append(pltpu.make_async_copy(source, target, arrived.at[len(copies)]))
+
+        add(seeds, seeds_out)
+        add(cells, cells_out)
+        add(heights, heights_out)
+        for target, start, near in ((last, 1, 2), (first, 0, 0)):
             planes = pl.ds(start, 2)
-            copies.append(
-                pltpu.make_async_copy(own.at[:, planes], target.at[0:3], arrived.at[2 * i])
-            )
-            copies.append(
-                pltpu.make_async_copy(
-                    correction.at[planes], target.at[3], arrived.at[2 * i + 1]
-                )
-            )
+            if target is inner:
+                add(own.at[:, planes], inner.at[0:3])
+                add(correction.at[planes], inner.at[3])
+            else:
+                add(own.at[1:3, planes], outer.at[1:3])
+                add(own.at[0, near], outer.at[0, 0])
+                add(correction.at[near], outer.at[0, 1])
         for copy in copies:
             copy.start()
         for copy in copies:
@@ -382,6 +400,15 @@
             part_out[3 * c + j] = trial_terms(state, flat, viscosity, rotor[j + 1])
 
 
+def outer_kernel(seeds, outer, column, to_z, to_y, outer_out):
+    shifts = shifts_of(seeds)
+    outer_out[0, 0] = rolled(outer[0, 0], shifts) + column[...]
+    outer_out[0, 1] = BASE_VISCOSITY * jnp.exp(outer[0, 1])
+    for c in (1, 2):
+        for i in range(2):
+            outer_out[c, i] = rolled(outer[c, i], shifts)
+
+
 def start_kernel(
     seeds, outer, inner, own_state, own_flat, own_part, own_stream, own_viscosity, rotor, column,
     to_z, to_y,
@@ -393,14 +420,24 @@
 
     def halo(j, c):
         i = j + 2 if j < 0 else j - 3
-        low = outer if j < 0 else inner
-        high = inner if j < 0 else outer
-        return jnp.where(even, low[c, i], high[c, i])
+        if c == 3:
+            within = BASE_VISCOSITY * jnp.exp(inner[c, i])
+        else:
+            within = rolled(inner[c, i], shifts)
+            if c == 0:
+                within = within + profile
+        if c in (1, 2):
+            between = outer[c, i]
+        elif j in (-1, 3):
+            between = outer[0, 0 if c == 0 else 1]
+        else:
+            return within
+        return jnp.where(even, between, within) if j < 0 else jnp.where(even, within, between)
 
     stream = {j: (own_stream[0, j], own_stream[1, j]) for j in range(3)}
     beside = {}
     for j in (-2, -1, 3, 4):
-        viscosity = BASE_VISCOSITY * jnp.exp(halo(j, 3))
+        viscosity = halo(j, 3)
         viscosity_out[j + 2] = viscosity
         if j in (-1, 3):
             beside[j] = viscosity
@@ -411,9 +448,7 @@
     for c in range(3):
         state = {j: own_state[3 * c + j] for j in range(3)}
         for j in (-2, -1, 3, 4):
-            state[j] = rolled(halo(j, c), shifts)
-            if c == 0:
-                state[j] = state[j] + profile
+            state[j] = halo(j, c)
         moved = {}
         for j in range(-1, 4):
             if 0 <= j < 3:
@@ -424,6 +459,8 @@
             moved[j] = part + stream[j][0] * state[j + 1] + stream[j][1] * state[j - 1]
             if c > 0 or 0 <= j < 3:
                 first_trial[5 * c + j + 1] = moved[j]
+        if c == 0:
+            without_edge(moved, even)
         trial.append(moved)
         if c == 0:
             beside_out[0] = state[-1]
@@ -433,7 +470,7 @@
         for j in range(3)
     ]
     source_out[...] = sources[1]
-    to_modes(sources, to_z, to_y, buffer, sheet)
+    to_modes(sources + [edge_term(trial[0], even)], to_z, to_y, buffer, sheet)
 
 
 def green_table(symbols):
@@ -522,6 +559,7 @@
     from_z, from_y, to_z, to_y,
     buffer, fourth_trial, source_out, velocity, share_out, sheet,
 ):
+    even = lax.rem(lax.axis_index("space"), 2) == 0
     profile = column[...]
     found = from_modes(modes_in, 2, from_z, from_y, sheet)
     second = with_plane_below(found[:4], source[...])
@@ -553,6 +591,8 @@
                 - rotor[j + 1] * adjoint[j]
             )
             moved[j] = 0.5 * adjoint[j] + 0.5 * TIME_STEP * pulled
+        if c == 0:
+            without_edge(moved, even)
         for j in range(3):
             fourth_trial[3 * c + j] = moved[j]
             term = adjoint[j] * laplace_mid[3 * c + j]
@@ -565,7 +605,7 @@
         for j in range(3)
     ]
     source_out[...] = sources[1]
-    to_modes(sources, to_z, to_y, buffer, sheet)
+    to_modes(sources + [edge_term(trial[0], even)], to_z, to_y, buffer, sheet)
 
 
 def gradient_kernel(
@@ -582,10 +622,13 @@
             out[copy, NZ * j : NZ * (j + 1), :] = total
 
 
-def local_call(kernel, outs, *args, spaces={}, out_spaces={}, scratch=()):
+def local_call(kernel, outs, *args, spaces={}, out_spaces={}, scratch=(), cost=None):
     specs = [pl.BlockSpec(memory_space=spaces.get(i, pltpu.VMEM)) for i in range(len(args))]
     out_spaces = [out_spaces.get(i, pltpu.VMEM) for i in range(len(outs))]
-    shapes = [space(shape, F32) for space, shape in zip(out_spaces, outs)]
+    shapes = [
+        space(*(out if isinstance(out[0], tuple) else (out, F32)))
+        for space, out in zip(out_spaces, outs)
+    ]
     out_specs = [pl.BlockSpec(memory_space=space) for space in out_spaces]
     single = len(outs) == 1
     return pl.pallas_call(
@@ -595,6 +638,7 @@
         out_specs=out_specs[0] if single else out_specs,
         scratch_shapes=scratch,
         name=kernel.__name__,
+        cost_estimate=cost,
         compiler_params=pltpu.CompilerParams(vmem_limit_bytes=24 * 1024 * 1024),
     )(*args)
 
@@ -614,11 +658,16 @@
     within = [(i, i + 1 - 2 * (i % 2)) for i in range(SPACE)]
     between = [(i, (i - 1 + 2 * (i % 2)) % SPACE) for i in range(SPACE)]
     plane = (NZ, NY)
-    inner, outer = local_call(
-        pack_kernel, [(4, 2, *plane), (4, 2, *plane)],
-        pltpu.with_memory_space_constraint(fluctuation, pltpu.HBM),
-        pltpu.with_memory_space_constraint(correction, pltpu.HBM),
-        spaces={0: pltpu.HBM, 1: pltpu.HBM}, scratch=[pltpu.SemaphoreType.DMA((4,))],
+    inputs = [fluctuation, correction, inflow_seeds, rotor_cells.T, profile[None, :]]
+    inner, outer, seeds, cells, heights = local_call(
+        pack_kernel,
+        [
+            (4, 2, *plane), (3, 2, *plane), (inflow_seeds.shape, jnp.int32),
+            (inputs[3].shape, jnp.int32), (1, NZ),
+        ],
+        *[pltpu.with_memory_space_constraint(f, pltpu.HBM) for f in inputs],
+        spaces={i: pltpu.HBM for i in range(len(inputs))},
+        scratch=[pltpu.SemaphoreType.DMA((8,))],
     )
     inner = lax.ppermute(inner, "space", within)
     outer = lax.ppermute(outer, "space", between)
@@ -632,16 +681,20 @@
             (9, *plane), (9, *plane), (9, *plane), (2, 3, *plane), (3, *plane), (5, *plane),
             plane,
         ],
-        inflow_seeds, fluctuation, correction, rotor_cells.T, profile[None, :],
+        seeds, fluctuation, correction, cells, heights,
+    )
+    outer = local_call(
+        outer_kernel, [(3, 2, *plane)], seeds, outer, column, to_z, to_y,
+        cost=pl.CostEstimate(flops=10**10, bytes_accessed=10**6, transcendentals=0),
     )
     rows = NZ * BLOCKS
     symbols = jnp.asarray(SYMBOLS)
     buffer, first_trial, source, beside, laplace_start, viscosity = local_call(
         start_kernel,
         [(rows, NY), (15, *plane), plane, (2, *plane), (9, *plane), (7, *plane)],
-        inflow_seeds, outer, inner, state, flat, part, stream, viscosity, rotor, column,
+        seeds, outer, inner, state, flat, part, stream, viscosity, rotor, column,
         to_z, to_y,
-        scratch=sheets(3),
+        scratch=sheets(4),
     )
     buffer = exchange(buffer)
     buffer, green = local_call(

time: 143 us -> 142 us (level)
    pallas_call x9 -> x10, Pallas kernels: 7.38 us -> 7.77 us  [local_call(): pl.pallas_call(kernel, out_shape=shapes[0] if single else shapes, in_spec...]
where the time goes in v9:
time: 142 us
  blocking collectives  121 us (85%)
  starting transfers between devices  10.7 us (8%)
  Pallas kernels  7.77 us (5%)
    all_to_all x6, blocking collectives, exchange(): return lax.all_to_all(wide, axis, 0, 0, tiled=True).reshape(rows.shape)  94.1 us
    all_to_all x1, blocking collectives, shards(): terms = lax.all_to_all(terms, 'sample', 0, 0, tiled=True)  27.3 us
    pallas_call x10, Pallas kernels, local_call(): pl.pallas_call(kernel, out_shape=shapes[0] if single else shapes, in_spec...  7.77 us
    ppermute x1, starting transfers between devices, shards(): inner = lax.ppermute(inner, 'space', within)  6.11 us
    ppermute x1, starting transfers between devices, shards(): outer = lax.ppermute(outer, 'space', between)  4.56 us
  transfers between devices with their start and end apart: 2, of which 0 were waited for; matrix products, arithmetic and copies ran while one was open for 0% of the time, Pallas kernels for 0%

profile of v9, /device:TPU:1, one launch (start us, length us, event | category | flops | bytes accessed | tf_op | source)
XLA Modules:
  0.0 141.9 jit_solution(9114821196210033869)
XLA Ops:
  0.7 1.2 pack_kernel.1
  1.9 4.6 %collective-permute-start = (f32[3,2,48,128]{3,2,1,0:T(8,128)S(1)}, f32[3,2,48,128]{3,2,1,0:T(8,128)S(1)}, u32[]{:S(2)}, u32[]{:S(2)}) collective-permute-start(f32[3,2,48,128]{3,2,1,0:T(8,128)S(1)} %get-tuple-element.34), channel_id=1, source_target_pairs={{0,63},{1,2},{2,1},{3,4},{4,3},{5,6},{6,5},{7,8},{8,7},{9,10},{10,... | collective-permute-start | bytes 442376 | tf_op jit(solution)/shard_map/ppermute | solution.py:673
  6.4 6.1 %collective-permute-start.1 = (f32[4,2,48,128]{3,2,1,0:T(8,128)S(1)}, f32[4,2,48,128]{3,2,1,0:T(8,128)S(1)}, u32[]{:S(2)}, u32[]{:S(2)}) collective-permute-start(f32[4,2,48,128]{3,2,1,0:T(8,128)S(1)} %get-tuple-element.38), channel_id=1, source_target_pairs={{0,1},{1,0},{2,3},{3,2},{4,5},{5,4},{6,7},{7,6},{8,9},{9,8},{10,11... | collective-permute-start | bytes 589832 | tf_op jit(solution)/shard_map/ppermute | solution.py:672
  12.6 0.0 copy-start.2
  12.6 0.0 copy-start.11
  12.6 0.4 prepare_kernel.1
  13.0 0.5 copy-done.2
  13.5 0.1 outer_kernel.1.outer
  13.6 0.0 copy-start.1
  13.7 0.8 start_kernel.1
  14.4 18.7 %all_to_all.35 = f32[64,1,384]{2,1,0:T(1,128)S(1)} all-to-all(f32[64,1,384]{2,1,0:T(1,128)S(1)} %bitcast.23), channel_id=1, replica_groups=mesh['sample'=8,'space'=64] {'space'}, dimensions={0} | all-to-all | bytes 196608 | tf_op jit(solution)/shard_map/all_to_all | solution.py:653
  33.1 0.6 solve_first_kernel.1
  33.7 14.5 %all_to_all.36 = f32[64,1,384]{2,1,0:T(1,128)S(1)} all-to-all(f32[64,1,384]{2,1,0:T(1,128)S(1)} %bitcast.26), channel_id=1, replica_groups=mesh['sample'=8,'space'=64] {'space'}, dimensions={0} | all-to-all | bytes 196608 | tf_op jit(solution)/shard_map/all_to_all | solution.py:653
  48.2 1.3 middle_kernel.1
  49.5 14.9 %all_to_all.37 = f32[64,1,640]{2,1,0:T(1,128)S(1)} all-to-all(f32[64,1,640]{2,1,0:T(1,128)S(1)} %bitcast.22), channel_id=1, replica_groups=mesh['sample'=8,'space'=64] {'space'}, dimensions={0} | all-to-all | bytes 327680 | tf_op jit(solution)/shard_map/all_to_all | solution.py:653
  64.4 0.8 solve_both_kernel.1
  65.2 16.1 %all_to_all.38 = f32[64,1,768]{2,1,0:T(1,128)S(1)} all-to-all(f32[64,1,768]{2,1,0:T(1,128)S(1)} %bitcast.15), channel_id=1, replica_groups=mesh['sample'=8,'space'=64] {'space'}, dimensions={0} | all-to-all | bytes 393216 | tf_op jit(solution)/shard_map/all_to_all | solution.py:653
  81.3 1.4 %adjoint_kernel.1 = (f32[192,128]{1,0:T(8,128)S(1)}, f32[9,48,128]{2,1,0:T(8,128)S(1)}, f32[48,128]{1,0:T(8,128)S(1)}, f32[1,3,3,48,128]{4,3,2,1,0:T(8,128)S(1)}, f32[3,48,128]{2,1,0:T(8,128)S(1)}) custom-call(f32[384,128]{1,0:T(8,128)S(1)} %bitcast.16, f32[9,48,128]{2,1,0:T(8,128)S(1)} %get-tuple-element.53.second_trial, ...), custom_call_target="tpu_custom_call" | custom-call | tf_op jit(solution)/shard_map/adjoint_kernel/pallas_call | solution.py:634
  82.7 15.7 %all_to_all.39 = f32[64,1,384]{2,1,0:T(1,128)S(1)} all-to-all(f32[64,1,384]{2,1,0:T(1,128)S(1)} %bitcast.24), channel_id=1, replica_groups=mesh['sample'=8,'space'=64] {'space'}, dimensions={0} | all-to-all | bytes 196608 | tf_op jit(solution)/shard_map/all_to_all | solution.py:653
  98.4 0.7 solve_last_kernel.1
  99.1 14.3 %all_to_all.40 = f32[64,1,384]{2,1,0:T(1,128)S(1)} all-to-all(f32[64,1,384]{2,1,0:T(1,128)S(1)} %bitcast.25), channel_id=1, replica_groups=mesh['sample'=8,'space'=64] {'space'}, dimensions={0} | all-to-all | bytes 196608 | tf_op jit(solution)/shard_map/all_to_all | solution.py:653
  113.4 0.6 gradient_kernel.1
  114.0 27.3 %all_to_all.41 = f32[8,144,128]{2,1,0:T(8,128)S(1)} all-to-all(f32[8,144,128]{2,1,0:T(8,128)S(1)} %gradient_kernel.1), channel_id=1, replica_groups=mesh['sample'=8,'space'=64] {'sample'}, dimensions={0} | all-to-all | bytes 1179648 | tf_op jit(solution)/shard_map/all_to_all | solution.py:735
  141.3 0.7 reduce_sum.9
  (22 shorter events, 0.1 us)
Async XLA Ops:
  0.6 11.9 %copy-start.3 = (f32[3,3,48,128]{3,2,1,0:T(8,128)S(1)}, f32[3,3,48,128]{3,2,1,0:T(8,128)}, u32[]{:S(2)}) copy-start(f32[3,3,48,128]{3,2,1,0:T(8,128)} %own.3) | copy-start | bytes 663556
  0.6 11.9 %copy-start.9 = (f32[3,48,128]{2,1,0:T(8,128)S(1)}, f32[3,48,128]{2,1,0:T(8,128)}, u32[]{:S(2)}) copy-start(f32[3,48,128]{2,1,0:T(8,128)} %correction.3) | copy-start | bytes 221188
  1.9 11.2 %collective-permute-start = (f32[3,2,48,128]{3,2,1,0:T(8,128)S(1)}, f32[3,2,48,128]{3,2,1,0:T(8,128)S(1)}, u32[]{:S(2)}, u32[]{:S(2)}) collective-permute-start(f32[3,2,48,128]{3,2,1,0:T(8,128)S(1)} %get-tuple-element.34), channel_id=1, source_target_pairs={{0,63},{1,2},{2,1},{3,4},{4,3},{5,6},{6,5},{7,8},{8,7},{9,10},{10,... | collective-permute-start | bytes 442376 | tf_op jit(solution)/shard_map/ppermute | solution.py:673
  6.4 7.2 %collective-permute-start.1 = (f32[4,2,48,128]{3,2,1,0:T(8,128)S(1)}, f32[4,2,48,128]{3,2,1,0:T(8,128)S(1)}, u32[]{:S(2)}, u32[]{:S(2)}) collective-permute-start(f32[4,2,48,128]{3,2,1,0:T(8,128)S(1)} %get-tuple-element.38), channel_id=1, source_target_pairs={{0,1},{1,0},{2,3},{3,2},{4,5},{5,4},{6,7},{7,6},{8,9},{9,8},{10,11... | collective-permute-start | bytes 589832 | tf_op jit(solution)/shard_map/ppermute | solution.py:672
  12.6 0.9 copy-start.2
  12.6 0.9 copy-start.11
  13.6 19.5 %copy-start.1 = (bf16[192,768]{1,0:T(8,128)(2,1)S(1)}, bf16[192,768]{1,0:T(8,128)(2,1)}, u32[]{:S(2)}) copy-start(bf16[192,768]{1,0:T(8,128)(2,1)} %constant.21.clone.from_x) | copy-start | bytes 884740
  13.6 19.5 %copy-start.5 = (f32[256,128]{1,0:T(8,128)S(1)}, f32[256,128]{1,0:T(8,128)}, u32[]{:S(2)}) copy-start(f32[256,128]{1,0:T(8,128)} %constant.26.clone.symbols) | copy-start | bytes 393220
  14.4 18.7 %copy-start.4 = (bf16[192,512]{1,0:T(8,128)(2,1)S(1)}, bf16[192,512]{1,0:T(8,128)(2,1)}, u32[]{:S(2)}) copy-start(bf16[192,512]{1,0:T(8,128)(2,1)} %constant.20.clone.to_x) | copy-start | bytes 589828
  33.1 15.1 %copy-start = (bf16[512,256]{1,0:T(8,128)(2,1)S(1)}, bf16[512,256]{1,0:T(8,128)(2,1)}, u32[]{:S(2)}) copy-start(bf16[512,256]{1,0:T(8,128)(2,1)} %constant.23.clone.from_y) | copy-start | bytes 786436
  33.7 14.5 %copy-start.7 = (bf16[48,288]{1,0:T(8,128)(2,1)S(1)}, bf16[48,288]{1,0:T(8,128)(2,1)}, u32[]{:S(2)}) copy-start(bf16[48,288]{1,0:T(8,128)(2,1)} %constant.25.clone.from_z) | copy-start | bytes 82948
  33.7 14.5 %copy-start.8 = (f32[3,48,128]{2,1,0:T(8,128)S(1)}, f32[3,48,128]{2,1,0:T(8,128)}, u32[]{:S(2)}) copy-start(f32[3,48,128]{2,1,0:T(8,128)} %observed.3) | copy-start | bytes 221188
  48.2 16.2 %copy-start.6 = (bf16[192,1152]{1,0:T(8,128)(2,1)S(1)}, bf16[192,1152]{1,0:T(8,128)(2,1)}, u32[]{:S(2)}) copy-start(bf16[192,1152]{1,0:T(8,128)(2,1)} %constant.28.clone.from_x) | copy-start | bytes 1327108
  49.5 14.9 %copy-start.10 = (bf16[192,576]{1,0:T(8,128)(2,1)S(1)}, bf16[192,576]{1,0:T(8,128)(2,1)}, u32[]{:S(2)}) copy-start(bf16[192,576]{1,0:T(8,128)(2,1)} %constant.27.clone.to_x) | copy-start | bytes 663556

commit v10 on v9

--- a/solution.py
+++ b/solution.py
@@ -195,7 +195,9 @@
 
 
 def cross_laplace(f):
-    return along_span(along_span(f)) + along_height(along_height(f))
+    span = pltpu.roll(f, 2, 1) + pltpu.roll(f, NY - 2, 1)
+    height = pltpu.roll(f, 2, 0) + pltpu.roll(f, NZ - 2, 0)
+    return 0.25 * (span + height) - f
 
 
 def with_plane_below(planes, source):

time: 142 us -> 142 us (level)
  no operation moved by 1% of the time
where the time goes in v10:
time: 142 us
  blocking collectives  121 us (85%)
  starting transfers between devices  10.7 us (8%)
  Pallas kernels  7.64 us (5%)
    all_to_all x6, blocking collectives, exchange(): return lax.all_to_all(wide, axis, 0, 0, tiled=True).reshape(rows.shape)  94.1 us
    all_to_all x1, blocking collectives, shards(): terms = lax.all_to_all(terms, 'sample', 0, 0, tiled=True)  27.3 us
    pallas_call x10, Pallas kernels, local_call(): pl.pallas_call(kernel, out_shape=shapes[0] if single else shapes, in_spec...  7.64 us
    ppermute x1, starting transfers between devices, shards(): inner = lax.ppermute(inner, 'space', within)  6.11 us
    ppermute x1, starting transfers between devices, shards(): outer = lax.ppermute(outer, 'space', between)  4.56 us
  transfers between devices with their start and end apart: 2, of which 0 were waited for; matrix products, arithmetic and copies ran while one was open for 0% of the time, Pallas kernels for 0%

profile of v10, /device:TPU:1, one launch (start us, length us, event | category | flops | bytes accessed | tf_op | source)
XLA Modules:
  0.0 141.8 jit_solution(1615222506543339188)
XLA Ops:
  0.7 1.2 pack_kernel.1
  1.9 4.6 %collective-permute-start = (f32[3,2,48,128]{3,2,1,0:T(8,128)S(1)}, f32[3,2,48,128]{3,2,1,0:T(8,128)S(1)}, u32[]{:S(2)}, u32[]{:S(2)}) collective-permute-start(f32[3,2,48,128]{3,2,1,0:T(8,128)S(1)} %get-tuple-element.34), channel_id=1, source_target_pairs={{0,63},{1,2},{2,1},{3,4},{4,3},{5,6},{6,5},{7,8},{8,7},{9,10},{10,... | collective-permute-start | bytes 442376 | tf_op jit(solution)/shard_map/ppermute | solution.py:675
  6.4 6.1 %collective-permute-start.1 = (f32[4,2,48,128]{3,2,1,0:T(8,128)S(1)}, f32[4,2,48,128]{3,2,1,0:T(8,128)S(1)}, u32[]{:S(2)}, u32[]{:S(2)}) collective-permute-start(f32[4,2,48,128]{3,2,1,0:T(8,128)S(1)} %get-tuple-element.38), channel_id=1, source_target_pairs={{0,1},{1,0},{2,3},{3,2},{4,5},{5,4},{6,7},{7,6},{8,9},{9,8},{10,11... | collective-permute-start | bytes 589832 | tf_op jit(solution)/shard_map/ppermute | solution.py:674
  12.6 0.0 copy-start.2
  12.6 0.0 copy-start.11
  12.6 0.4 prepare_kernel.1
  13.0 0.5 copy-done.2
  13.5 0.1 outer_kernel.1.outer
  13.6 0.0 copy-start.1
  13.7 0.8 start_kernel.1
  14.4 18.7 %all_to_all.35 = f32[64,1,384]{2,1,0:T(1,128)S(1)} all-to-all(f32[64,1,384]{2,1,0:T(1,128)S(1)} %bitcast.23), channel_id=1, replica_groups=mesh['sample'=8,'space'=64] {'space'}, dimensions={0} | all-to-all | bytes 196608 | tf_op jit(solution)/shard_map/all_to_all | solution.py:655
  33.1 0.6 solve_first_kernel.1
  33.7 14.5 %all_to_all.36 = f32[64,1,384]{2,1,0:T(1,128)S(1)} all-to-all(f32[64,1,384]{2,1,0:T(1,128)S(1)} %bitcast.26), channel_id=1, replica_groups=mesh['sample'=8,'space'=64] {'space'}, dimensions={0} | all-to-all | bytes 196608 | tf_op jit(solution)/shard_map/all_to_all | solution.py:655
  48.2 1.2 middle_kernel.1
  49.5 14.9 %all_to_all.37 = f32[64,1,640]{2,1,0:T(1,128)S(1)} all-to-all(f32[64,1,640]{2,1,0:T(1,128)S(1)} %bitcast.22), channel_id=1, replica_groups=mesh['sample'=8,'space'=64] {'space'}, dimensions={0} | all-to-all | bytes 327680 | tf_op jit(solution)/shard_map/all_to_all | solution.py:655
  64.4 0.8 solve_both_kernel.1
  65.2 16.1 %all_to_all.38 = f32[64,1,768]{2,1,0:T(1,128)S(1)} all-to-all(f32[64,1,768]{2,1,0:T(1,128)S(1)} %bitcast.15), channel_id=1, replica_groups=mesh['sample'=8,'space'=64] {'space'}, dimensions={0} | all-to-all | bytes 393216 | tf_op jit(solution)/shard_map/all_to_all | solution.py:655
  81.2 1.4 adjoint_kernel.1
  82.6 15.7 %all_to_all.39 = f32[64,1,384]{2,1,0:T(1,128)S(1)} all-to-all(f32[64,1,384]{2,1,0:T(1,128)S(1)} %bitcast.24), channel_id=1, replica_groups=mesh['sample'=8,'space'=64] {'space'}, dimensions={0} | all-to-all | bytes 196608 | tf_op jit(solution)/shard_map/all_to_all | solution.py:655
  98.3 0.7 solve_last_kernel.1
  99.0 14.3 %all_to_all.40 = f32[64,1,384]{2,1,0:T(1,128)S(1)} all-to-all(f32[64,1,384]{2,1,0:T(1,128)S(1)} %bitcast.25), channel_id=1, replica_groups=mesh['sample'=8,'space'=64] {'space'}, dimensions={0} | all-to-all | bytes 196608 | tf_op jit(solution)/shard_map/all_to_all | solution.py:655
  113.4 0.5 gradient_kernel.1
  113.9 27.3 %all_to_all.41 = f32[8,144,128]{2,1,0:T(8,128)S(1)} all-to-all(f32[8,144,128]{2,1,0:T(8,128)S(1)} %gradient_kernel.1), channel_id=1, replica_groups=mesh['sample'=8,'space'=64] {'sample'}, dimensions={0} | all-to-all | bytes 1179648 | tf_op jit(solution)/shard_map/all_to_all | solution.py:737
  141.2 0.7 reduce_sum.9
  (22 shorter events, 0.1 us)
Async XLA Ops:
  0.6 11.9 %copy-start.3 = (f32[3,3,48,128]{3,2,1,0:T(8,128)S(1)}, f32[3,3,48,128]{3,2,1,0:T(8,128)}, u32[]{:S(2)}) copy-start(f32[3,3,48,128]{3,2,1,0:T(8,128)} %own.3) | copy-start | bytes 663556
  0.6 11.9 %copy-start.9 = (f32[3,48,128]{2,1,0:T(8,128)S(1)}, f32[3,48,128]{2,1,0:T(8,128)}, u32[]{:S(2)}) copy-start(f32[3,48,128]{2,1,0:T(8,128)} %correction.3) | copy-start | bytes 221188
  1.9 11.2 %collective-permute-start = (f32[3,2,48,128]{3,2,1,0:T(8,128)S(1)}, f32[3,2,48,128]{3,2,1,0:T(8,128)S(1)}, u32[]{:S(2)}, u32[]{:S(2)}) collective-permute-start(f32[3,2,48,128]{3,2,1,0:T(8,128)S(1)} %get-tuple-element.34), channel_id=1, source_target_pairs={{0,63},{1,2},{2,1},{3,4},{4,3},{5,6},{6,5},{7,8},{8,7},{9,10},{10,... | collective-permute-start | bytes 442376 | tf_op jit(solution)/shard_map/ppermute | solution.py:675
  6.4 7.2 %collective-permute-start.1 = (f32[4,2,48,128]{3,2,1,0:T(8,128)S(1)}, f32[4,2,48,128]{3,2,1,0:T(8,128)S(1)}, u32[]{:S(2)}, u32[]{:S(2)}) collective-permute-start(f32[4,2,48,128]{3,2,1,0:T(8,128)S(1)} %get-tuple-element.38), channel_id=1, source_target_pairs={{0,1},{1,0},{2,3},{3,2},{4,5},{5,4},{6,7},{7,6},{8,9},{9,8},{10,11... | collective-permute-start | bytes 589832 | tf_op jit(solution)/shard_map/ppermute | solution.py:674
  12.6 0.9 copy-start.2
  12.6 0.9 copy-start.11
  13.6 19.5 %copy-start.1 = (bf16[192,768]{1,0:T(8,128)(2,1)S(1)}, bf16[192,768]{1,0:T(8,128)(2,1)}, u32[]{:S(2)}) copy-start(bf16[192,768]{1,0:T(8,128)(2,1)} %constant.21.clone.from_x) | copy-start | bytes 884740
  13.6 19.5 %copy-start.5 = (f32[256,128]{1,0:T(8,128)S(1)}, f32[256,128]{1,0:T(8,128)}, u32[]{:S(2)}) copy-start(f32[256,128]{1,0:T(8,128)} %constant.26.clone.symbols) | copy-start | bytes 393220
  14.4 18.7 %copy-start.4 = (bf16[192,512]{1,0:T(8,128)(2,1)S(1)}, bf16[192,512]{1,0:T(8,128)(2,1)}, u32[]{:S(2)}) copy-start(bf16[192,512]{1,0:T(8,128)(2,1)} %constant.20.clone.to_x) | copy-start | bytes 589828
  33.1 15.1 %copy-start = (bf16[512,256]{1,0:T(8,128)(2,1)S(1)}, bf16[512,256]{1,0:T(8,128)(2,1)}, u32[]{:S(2)}) copy-start(bf16[512,256]{1,0:T(8,128)(2,1)} %constant.23.clone.from_y) | copy-start | bytes 786436
  33.7 14.5 %copy-start.7 = (bf16[48,288]{1,0:T(8,128)(2,1)S(1)}, bf16[48,288]{1,0:T(8,128)(2,1)}, u32[]{:S(2)}) copy-start(bf16[48,288]{1,0:T(8,128)(2,1)} %constant.25.clone.from_z) | copy-start | bytes 82948
  33.7 14.5 %copy-start.8 = (f32[3,48,128]{2,1,0:T(8,128)S(1)}, f32[3,48,128]{2,1,0:T(8,128)}, u32[]{:S(2)}) copy-start(f32[3,48,128]{2,1,0:T(8,128)} %observed.3) | copy-start | bytes 221188
  48.2 16.1 %copy-start.6 = (bf16[192,1152]{1,0:T(8,128)(2,1)S(1)}, bf16[192,1152]{1,0:T(8,128)(2,1)}, u32[]{:S(2)}) copy-start(bf16[192,1152]{1,0:T(8,128)(2,1)} %constant.28.clone.from_x) | copy-start | bytes 1327108
  49.5 14.9 %copy-start.10 = (bf16[192,576]{1,0:T(8,128)(2,1)S(1)}, bf16[192,576]{1,0:T(8,128)(2,1)}, u32[]{:S(2)}) copy-start(bf16[192,576]{1,0:T(8,128)(2,1)} %constant.27.clone.to_x) | copy-start | bytes 663556
